TPU v7x, 32 devices: a whole 2x2x4 slice. The times are simulated.
32 devices in a mesh: dp: 8 (over y, x, core), ctx: 4 (over z).
Axes of the slice: x: 2, y: 2, z: 4, core: 2. Of those that a mesh axis runs over, the one named last changes fastest.
Arguments:
- tokens: bfloat16 [8, 1024, 1536], P('dp', 'ctx'), may hold values from -6 to 6
- lengths: int32 [8], P('dp'), may hold values from 256 to 1024, as said below
- routes: int32 [8, 1024, 8], P('dp', 'ctx'), may hold values from 0 to 15, all different within a row; in each aligned block of 256 rows (0 to 255, 256 to 511, ..., all dimensions but the last counted through in order) at most 144 rows name the same one
- cotangent: bfloat16 [8, 1024, 1536], P('dp', 'ctx'), may hold values from -6 to 6
- gain_attn: bfloat16 [1536], P('dp'), may hold values from 0.5 to 1.5
- gain_moe: bfloat16 [1536], P('dp'), may hold values from 0.5 to 1.5
- w_query: bfloat16 [1536, 1536], P('dp'), may hold values from -0.15625 to 0.15625
- w_keyval: bfloat16 [1536, 1024], P('dp'), may hold values from -0.15625 to 0.15625
- w_output: bfloat16 [1536, 1536], P('dp'), may hold values from -4 to 4
- w_router: bfloat16 [1536, 16], P('dp'), may hold values from -0.079589844 to 0.079589844
- w_gate_up: bfloat16 [16, 1536, 1024], P('dp'), may hold values from -0.15625 to 0.15625
- w_down: bfloat16 [16, 512, 1536], P('dp'), may hold values from -1 to 1
Outputs:
- outcome: bfloat16 [8, 1024, 1536], P('dp', 'ctx')
- grad_tokens: bfloat16 [8, 1024, 1536], P('dp', 'ctx')
- grad_gain_attn: float32 [1536], P('dp')
- grad_gain_moe: float32 [1536], P('dp')
- grad_w_query: float32 [1536, 1536], P('dp')
- grad_w_keyval: float32 [1536, 1024], P('dp')
- grad_w_output: float32 [1536, 1536], P('dp')
- grad_w_router: float32 [1536, 16], P('dp')
- grad_w_gate_up: float32 [16, 1536, 1024], P('dp')
- grad_w_down: float32 [16, 512, 1536], P('dp')
Inputs may be any that keep to these rules, and one draw needn't show every extreme that they name: `lengths`: some slot holds 1024 live tokens in every draw. `routes`: each token names 8 different experts; within the 256 rows of one device no expert is named by more than 144 rows, and some expert reaches 144.
All inputs are finite; a program needn't handle non-finite values.
Results may differ from a plain program's by a relative error of at most 0.022.
Values may be sent and summed in bfloat16 or wider, within the bound.
No kernel may reach another device: no remote copies, remote signals or barrier semaphores. Data moves between devices by JAX's collectives and lax.ppermute only.
A program may use at most 256 MiB of HBM per device.

v0:
```python
import math

import jax
import jax.numpy as jnp
from jax import lax
from jax.sharding import PartitionSpec as P

HD = 64


NORM_EPS = 1e-06
ROPE_BASE = 10000.0
MASK_FLOOR = -1e30


def rotary(values, places, sine_sign):
    half_dim = values.shape[-1] // 2
    frequency = ROPE_BASE ** (-jnp.arange(half_dim, dtype=jnp.float32) * 2.0 / values.shape[-1])
    angles = places.astype(jnp.float32)[:, None] * frequency[None, :]
    cosine = jnp.cos(angles)[:, None, :]
    sine_part = sine_sign * jnp.sin(angles)[:, None, :]
    first_half = values[..., :half_dim]
    second_half = values[..., half_dim:]
    return jnp.concatenate(
        [
            first_half * cosine - second_half * sine_part,
            second_half * cosine + first_half * sine_part,
        ],
        -1,
    )


def attend_piece(carry, piece, start, queries, places, length, score_scale):
    run_max, run_total, run_acc = carry
    kv_heads = queries.shape[1]
    head_size = queries.shape[3]
    piece_rows = piece.shape[0]
    key_part = piece[:, : kv_heads * head_size].reshape(piece_rows, kv_heads, head_size)
    value_part = piece[:, kv_heads * head_size :].reshape(piece_rows, kv_heads, head_size)
    key_places = start + jnp.arange(piece_rows, dtype=jnp.int32)
    allowed = (key_places[None, :] <= places[:, None]) & (key_places < length)[None, :]
    scores = (
        jnp.einsum("rkgd,nkd->kgrn", queries, key_part, preferred_element_type=jnp.float32)
        * score_scale
    )
    masked = jnp.where(allowed, scores, MASK_FLOOR)
    new_max = jnp.maximum(run_max, jnp.max(masked, -1))
    weights = jnp.where(allowed, jnp.exp(masked - new_max[..., None]), 0.0)
    factor = jnp.exp(run_max - new_max)
    run_total = run_total * factor + jnp.sum(weights, -1)
    run_acc = run_acc * factor[..., None] + jnp.einsum(
        "kgrn,nkd->kgrd",
        weights.astype(jnp.bfloat16),
        value_part,
        preferred_element_type=jnp.float32,
    )
    return (new_max, run_total, run_acc)


def fold_blocks(carry, piece, step_fn):
    piece_rows = piece.shape[0]
    block_rows = math.gcd(piece_rows, 512)
    blocks = piece.reshape(piece_rows // block_rows, block_rows, piece.shape[1])

    def inner(held, item):
        block_index, block = item
        return (step_fn(held, block, block_index * block_rows), None)

    carry, _ = lax.scan(
        inner, carry, (jnp.arange(piece_rows // block_rows, dtype=jnp.int32), blocks)
    )
    return carry


def expert_forward(rows_in, gate_w, down_w, expert_hidden):
    gate_up = jnp.einsum("ecd,edf->ecf", rows_in, gate_w, preferred_element_type=jnp.float32)
    act_low = (jax.nn.silu(gate_up[..., :expert_hidden]) * gate_up[..., expert_hidden:]).astype(
        jnp.bfloat16
    )
    produced = jnp.einsum(
        "ecf,efd->ecd", act_low, down_w, preferred_element_type=jnp.float32
    ).astype(jnp.bfloat16)
    return (produced, gate_up, act_low)


def expert_backward(grad_rows, gate_up, gate_w, down_w, expert_hidden):
    grad_act = jnp.einsum("ecd,efd->ecf", grad_rows, down_w, preferred_element_type=jnp.float32)
    pre_gate = gate_up[..., :expert_hidden]
    pre_up = gate_up[..., expert_hidden:]
    sigma = jax.nn.sigmoid(pre_gate)
    grad_gate = grad_act * pre_up * sigma * (1.0 + pre_gate * (1.0 - sigma))
    grad_up = grad_act * pre_gate * sigma
    grad_gate_up = jnp.concatenate([grad_gate, grad_up], -1).astype(jnp.bfloat16)
    grad_rows_in = jnp.einsum(
        "ecf,edf->ecd", grad_gate_up, gate_w, preferred_element_type=jnp.float32
    ).astype(jnp.bfloat16)
    return (grad_gate_up, grad_rows_in)


def per_device(
    tokens,
    lengths,
    routes,
    cotangent,
    gain_attn,
    gain_moe,
    w_query,
    w_keyval,
    w_output,
    w_router,
    w_gate_up,
    w_down,
):
    row_count = tokens.shape[1]
    model_width = tokens.shape[2]
    experts = w_router.shape[1]
    top_count = routes.shape[2]
    expert_hidden = w_down.shape[1]
    kv_width = w_keyval.shape[1] // 2
    head_total = w_query.shape[1]
    head_size = HD
    kv_heads = kv_width // head_size
    groups = head_total // kv_width
    score_scale = head_size ** (-0.5)
    capacity = row_count * 9 // 16
    seq_len = row_count * lax.axis_size("ctx")
    places = lax.axis_index("ctx") * row_count + jnp.arange(row_count, dtype=jnp.int32)
    length = lengths[0]
    valid_rows = places < length
    inputs = tokens[0].astype(jnp.float32)
    gain_one, gain_two, query_w, keyval_w, output_w, router_w = (
        lax.all_gather(gain_attn, "dp", axis=0, tiled=True),
        lax.all_gather(gain_moe, "dp", axis=0, tiled=True),
        lax.all_gather(w_query, "dp", axis=0, tiled=True),
        lax.all_gather(w_keyval, "dp", axis=0, tiled=True),
        lax.all_gather(w_output, "dp", axis=0, tiled=True),
        lax.all_gather(w_router, "dp", axis=0, tiled=True),
    )
    gain_one = gain_one.astype(jnp.float32)
    gain_two = gain_two.astype(jnp.float32)
    inv_one = lax.rsqrt(jnp.mean(inputs * inputs, -1, keepdims=True) + NORM_EPS)
    normed_one = inputs * inv_one
    hn_one = (normed_one * gain_one).astype(jnp.bfloat16)
    query_raw = jnp.dot(hn_one, query_w, preferred_element_type=jnp.float32)
    keyval_raw = jnp.dot(hn_one, keyval_w, preferred_element_type=jnp.float32)
    queries = (
        rotary(query_raw.reshape(row_count, head_total // head_size, head_size), places, 1.0)
        .astype(jnp.bfloat16)
        .reshape(row_count, kv_heads, groups, head_size)
    )
    keys_rot = rotary(
        keyval_raw[:, :kv_width].reshape(row_count, kv_heads, head_size), places, 1.0
    ).reshape(row_count, kv_width)
    keyval = jnp.concatenate([keys_rot, keyval_raw[:, kv_width:]], 1).astype(jnp.bfloat16)

    def forward_step(carry, piece, start):
        live_block = (start <= places[row_count - 1]) & (start < length)
        return lax.cond(
            live_block,
            lambda held: attend_piece(held, piece, start, queries, places, length, score_scale),
            lambda held: held,
            carry,
        )

    initial = (
        jnp.full((kv_heads, groups, row_count), MASK_FLOOR, jnp.float32),
        jnp.zeros((kv_heads, groups, row_count), jnp.float32),
        jnp.zeros((kv_heads, groups, row_count, head_size), jnp.float32),
    )
    run_max, run_total, run_acc = fold_blocks(
        initial, lax.all_gather(keyval, "ctx", axis=0, tiled=True), forward_step
    )
    attn_out = run_acc / run_total[..., None]
    attn_low = (
        jnp.transpose(attn_out, (2, 0, 1, 3)).reshape(row_count, head_total).astype(jnp.bfloat16)
    )
    resid = inputs + jnp.dot(attn_low, output_w, preferred_element_type=jnp.float32)
    inv_two = lax.rsqrt(jnp.mean(resid * resid, -1, keepdims=True) + NORM_EPS)
    normed_two = resid * inv_two
    hn_two = (normed_two * gain_two).astype(jnp.bfloat16)
    logits = jnp.dot(hn_two, router_w, preferred_element_type=jnp.float32)
    route = routes[0]
    route_hits = route[:, :, None] == jnp.arange(experts, dtype=jnp.int32)[None, None, :]
    chosen = jnp.sum(jnp.where(route_hits, logits[:, None, :], 0.0), -1)
    gates = jax.nn.softmax(chosen, -1)
    counts = jnp.sum(route_hits.astype(jnp.int32), 1)
    slot_places = jnp.cumsum(counts, 0) - 1
    slot_index = jnp.sum(jnp.where(route_hits, slot_places[:, None, :], 0), -1)
    token_ids = jnp.broadcast_to(
        jnp.arange(row_count, dtype=jnp.int32)[:, None], (row_count, top_count)
    )
    source = (
        jnp.full((experts, capacity), row_count, jnp.int32).at[route, slot_index].set(token_ids)
    )
    padded = jnp.concatenate([hn_two, jnp.zeros((1, model_width), jnp.bfloat16)], 0)
    expert_in = padded[source]
    arrived = lax.all_to_all(expert_in, "dp", split_axis=0, concat_axis=1, tiled=True)
    produced, gate_up, act_low = expert_forward(arrived, w_gate_up, w_down, expert_hidden)
    expert_out = lax.all_to_all(produced, "dp", split_axis=1, concat_axis=0, tiled=True)
    received = expert_out[route, slot_index].astype(jnp.float32)
    moe = jnp.sum(gates[..., None] * received, 1)
    outcome = jnp.where(valid_rows[:, None], resid + moe, 0.0).astype(jnp.bfloat16)
    grad_y = jnp.where(valid_rows[:, None], cotangent[0].astype(jnp.float32), 0.0)
    grad_gates = jnp.sum(grad_y[:, None, :] * received, -1)
    grad_chosen = gates * (grad_gates - jnp.sum(gates * grad_gates, -1, keepdims=True))
    grad_logits = jnp.sum(jnp.where(route_hits, grad_chosen[:, :, None], 0.0), 1).astype(
        jnp.bfloat16
    )
    gate_table = jnp.sum(jnp.where(route_hits, gates[:, :, None], 0.0), 1)
    gate_pad = jnp.concatenate([gate_table, jnp.zeros((1, experts), jnp.float32)], 0)
    slot_gates = gate_pad[source, jnp.arange(experts, dtype=jnp.int32)[:, None]]
    grad_pad = jnp.concatenate([grad_y, jnp.zeros((1, model_width), jnp.float32)], 0)
    grad_out = (slot_gates[..., None] * grad_pad[source]).astype(jnp.bfloat16)
    grad_arrived = lax.all_to_all(grad_out, "dp", split_axis=0, concat_axis=1, tiled=True)
    grad_gate_up, grad_in_own = expert_backward(
        grad_arrived, gate_up, w_gate_up, w_down, expert_hidden
    )
    grad_in = lax.all_to_all(grad_in_own, "dp", split_axis=1, concat_axis=0, tiled=True)
    grad_w_gate_up = jnp.einsum(
        "ecd,ecf->edf", arrived, grad_gate_up, preferred_element_type=jnp.float32
    )
    grad_w_down = jnp.einsum(
        "ecf,ecd->efd", act_low, grad_arrived, preferred_element_type=jnp.float32
    )
    grad_hn_two = jnp.sum(grad_in[route, slot_index].astype(jnp.float32), 1) + jnp.einsum(
        "te,de->td", grad_logits, router_w, preferred_element_type=jnp.float32
    )
    grad_normed_two = grad_hn_two * gain_two
    grad_resid = grad_y + inv_two * (
        grad_normed_two - normed_two * jnp.mean(grad_normed_two * normed_two, -1, keepdims=True)
    )
    grad_attn = grad_resid.astype(jnp.bfloat16)
    grad_heads = jnp.einsum("td,hd->th", grad_attn, output_w, preferred_element_type=jnp.float32)
    grad_heads = jnp.transpose(
        grad_heads.reshape(row_count, kv_heads, groups, head_size), (1, 2, 0, 3)
    )
    grad_unscaled = (grad_heads / run_total[..., None]).astype(jnp.bfloat16)
    delta = jnp.sum(attn_out * grad_heads, -1) / run_total
    keys_all = lax.all_gather(keyval, "ctx", axis=0, tiled=True)
    block_rows = math.gcd(seq_len, 512)
    block_count = seq_len // block_rows
    kv_blocks = keys_all.reshape(block_count, block_rows, 2 * kv_width)

    def backward_step(grad_query, item):
        block_index, block = item
        start = block_index * block_rows
        key_part = block[:, :kv_width].reshape(block_rows, kv_heads, head_size)
        value_part = block[:, kv_width:].reshape(block_rows, kv_heads, head_size)
        key_places = start + jnp.arange(block_rows, dtype=jnp.int32)
        allowed = (key_places[None, :] <= places[:, None]) & (key_places < length)[None, :]

        def compute(held):
            scores = (
                jnp.einsum("rkgd,nkd->kgrn", queries, key_part, preferred_element_type=jnp.float32)
                * score_scale
            )
            weights = jnp.where(allowed, jnp.exp(scores - run_max[..., None]), 0.0)
            grad_probs = jnp.einsum(
                "kgrd,nkd->kgrn", grad_unscaled, value_part, preferred_element_type=jnp.float32
            )
            grad_scores = (weights * (grad_probs - delta[..., None])).astype(jnp.bfloat16)
            held = (
                held
                + jnp.einsum(
                    "kgrn,nkd->rkgd", grad_scores, key_part, preferred_element_type=jnp.float32
                )
                * score_scale
            )
            grad_keys = (
                jnp.einsum(
                    "kgrn,rkgd->nkd", grad_scores, queries, preferred_element_type=jnp.float32
                )
                * score_scale
            )
            grad_values = jnp.einsum(
                "kgrn,kgrd->nkd",
                weights.astype(jnp.bfloat16),
                grad_unscaled,
                preferred_element_type=jnp.float32,
            )
            return (
                held,
                jnp.concatenate(
                    [
                        grad_keys.reshape(block_rows, kv_width),
                        grad_values.reshape(block_rows, kv_width),
                    ],
                    1,
                ),
            )

        def skipped(held):
            return (held, jnp.zeros((block_rows, 2 * kv_width), jnp.float32))

        live_block = (start <= places[row_count - 1]) & (start < length)
        return lax.cond(live_block, compute, skipped, grad_query)

    grad_query, grad_kv_blocks = lax.scan(
        backward_step,
        jnp.zeros((row_count, kv_heads, groups, head_size), jnp.float32),
        (jnp.arange(block_count, dtype=jnp.int32), kv_blocks),
    )
    grad_kv_flat = grad_kv_blocks.reshape(seq_len, 2 * kv_width)
    grad_kv_mine = lax.psum_scatter(
        grad_kv_flat.astype(jnp.bfloat16), "ctx", scatter_dimension=0, tiled=True
    ).astype(jnp.float32)
    grad_query_raw = (
        rotary(grad_query.reshape(row_count, head_total // head_size, head_size), places, -1.0)
        .reshape(row_count, head_total)
        .astype(jnp.bfloat16)
    )
    grad_keys_raw = rotary(
        grad_kv_mine[:, :kv_width].reshape(row_count, kv_heads, head_size), places, -1.0
    ).reshape(row_count, kv_width)
    grad_keyval_raw = jnp.concatenate([grad_keys_raw, grad_kv_mine[:, kv_width:]], 1).astype(
        jnp.bfloat16
    )
    grad_hn_one = jnp.einsum(
        "th,dh->td", grad_query_raw, query_w, preferred_element_type=jnp.float32
    ) + jnp.einsum("tk,dk->td", grad_keyval_raw, keyval_w, preferred_element_type=jnp.float32)
    grad_normed_one = grad_hn_one * gain_one
    grad_inputs = grad_resid + inv_one * (
        grad_normed_one - normed_one * jnp.mean(grad_normed_one * normed_one, -1, keepdims=True)
    )
    part_gain_one = jnp.sum(grad_hn_one * normed_one, 0)
    part_gain_two = jnp.sum(grad_hn_two * normed_two, 0)
    part_query = jnp.einsum("td,th->dh", hn_one, grad_query_raw, preferred_element_type=jnp.float32)
    part_keyval = jnp.einsum(
        "td,tk->dk", hn_one, grad_keyval_raw, preferred_element_type=jnp.float32
    )
    part_output = jnp.einsum("th,td->hd", attn_low, grad_attn, preferred_element_type=jnp.float32)
    part_router = jnp.einsum("td,te->de", hn_two, grad_logits, preferred_element_type=jnp.float32)
    share_gain_one, share_gain_two, share_query, share_keyval, share_output, share_router = (
        lax.psum_scatter(
            part_gain_one.astype(jnp.bfloat16), "dp", scatter_dimension=0, tiled=True
        ).astype(jnp.float32),
        lax.psum_scatter(
            part_gain_two.astype(jnp.bfloat16), "dp", scatter_dimension=0, tiled=True
        ).astype(jnp.float32),
        lax.psum_scatter(
            part_query.astype(jnp.bfloat16), "dp", scatter_dimension=0, tiled=True
        ).astype(jnp.float32),
        lax.psum_scatter(
            part_keyval.astype(jnp.bfloat16), "dp", scatter_dimension=0, tiled=True
        ).astype(jnp.float32),
        lax.psum_scatter(
            part_output.astype(jnp.bfloat16), "dp", scatter_dimension=0, tiled=True
        ).astype(jnp.float32),
        lax.psum_scatter(
            part_router.astype(jnp.bfloat16), "dp", scatter_dimension=0, tiled=True
        ).astype(jnp.float32),
    )
    (
        total_gain_one,
        total_gain_two,
        total_query,
        total_keyval,
        total_output,
        total_router,
        total_gate_up,
        total_down,
    ) = (
        lax.psum(share_gain_one.astype(jnp.bfloat16), "ctx").astype(jnp.float32),
        lax.psum(share_gain_two.astype(jnp.bfloat16), "ctx").astype(jnp.float32),
        lax.psum(share_query.astype(jnp.bfloat16), "ctx").astype(jnp.float32),
        lax.psum(share_keyval.astype(jnp.bfloat16), "ctx").astype(jnp.float32),
        lax.psum(share_output.astype(jnp.bfloat16), "ctx").astype(jnp.float32),
        lax.psum(share_router.astype(jnp.bfloat16), "ctx").astype(jnp.float32),
        lax.psum(grad_w_gate_up.astype(jnp.bfloat16), "ctx").astype(jnp.float32),
        lax.psum(grad_w_down.astype(jnp.bfloat16), "ctx").astype(jnp.float32),
    )
    return (
        outcome[None],
        grad_inputs.astype(jnp.bfloat16)[None],
        total_gain_one,
        total_gain_two,
        total_query,
        total_keyval,
        total_output,
        total_router,
        total_gate_up,
        total_down,
    )


def solution(mesh):
    in_specs = (
        P("dp", "ctx", None),
        P("dp"),
        P("dp", "ctx", None),
        P("dp", "ctx", None),
        P("dp"),
        P("dp"),
        P("dp", None),
        P("dp", None),
        P("dp", None),
        P("dp", None),
        P("dp", None, None),
        P("dp", None, None),
    )
    out_specs = (
        P("dp", "ctx", None),
        P("dp", "ctx", None),
        P("dp"),
        P("dp"),
        P("dp", None),
        P("dp", None),
        P("dp", None),
        P("dp", None),
        P("dp", None, None),
        P("dp", None, None),
    )
    return jax.shard_map(
        per_device, mesh=mesh, in_specs=in_specs, out_specs=out_specs, check_vma=False
    )
```

profile of v0, /device:TPU:0, one launch (start us, length us, event | category | flops | bytes accessed | tf_op | source)
XLA Modules:
  0.0 1552.4 jit_solution(14308481383569162392)
XLA Ops:
  12.5 15.7 %all-reduce.8 = (bf16[1536]{0:T(1024)(128)(2,1)S(1)}, bf16[1536]{0:T(1024)(128)(2,1)S(1)}) all-reduce(bf16[1536]{0:T(1024)(128)(2,1)S(1)} %dynamic-update-slice, bf16[1536]{0:T(1024)(128)(2,1)S(1)} %dynamic-update-slice.1), channel_id=1, replica_groups=mesh['dp'=8,'ctx'=4] {'dp'}, use_global_device_ids=true, to_apply=%add.3 | all-reduce | flops 3072 | bytes 12288
  30.5 14.6 all-gather.6.cloned.1.call-done
  58.0 8.3 scatter_custom_fusion
  66.5 19.5 %all-gather.10.cloned.1.call-done = bf16[1536,1536]{1,0:T(8,128)(2,1)} async-done(((bf16[192,1536]{1,0:T(8,128)(2,1)}), bf16[1536,1536]{1,0:T(8,128)(2,1)}) %all-gather.10.cloned.1.call-update) | async-done | bytes 4718608 | tf_op jit(solution)/shard_map/all_gather | solution.py:134
  85.9 6.6 copy.140
  98.0 36.0 %all-gather.8.cloned.1.call-done = bf16[1024,1024]{1,0:T(8,128)(2,1)} async-done(((bf16[256,1024]{1,0:T(8,128)(2,1)}), bf16[1024,1024]{1,0:T(8,128)(2,1)}) %all-gather.8.cloned.1.call-update) | async-done | bytes 2097168 | tf_op jit(solution)/shard_map/all_gather | solution.py:171
  139.4 18.5 %while.29 = (s32[]{:T(128)}, f32[8,3,256]{2,1,0:T(4,128)S(1)}, f32[8,3,256]{2,1,0:T(4,128)S(1)}, f32[8,3,256,64]{2,3,1,0:T(8,128)}, s32[2]{0:T(128)S(1)}, /*inde...) while((s32[]{:T(128)}, f32[8,3,256]{2,1,0:T(4,128)S(1)}, ...), condition=%wide.region_6.7_spmd, body=%wide.region_1.6_spmd.sunk | while | flops 847263232 | bytes 63576456 | solution.py:69
  142.6 12.2 conditional.4
  160.5 13.0 all-gather.12.cloned.1.call-done
  181.0 16.1 %gather_fusion = bf16[2304,1536]{1,0:T(8,128)(2,1)} fusion(bf16[257,1536]{1,0:T(8,128)(2,1)} %concatenate.59, s32[3072]{0:T(1024)S(1)} %pad_clamp_fusion), kind=kCustom, calls=%fused_computation | custom fusion | bytes 14164992 | tf_op jit(solution)/shard_map/gather | solution.py:196
  197.1 84.0 %all_to_all.72 = bf16[16,144,1536]{2,1,0:T(8,128)(2,1)S(1)} all-to-all(bf16[16,144,1536]{2,1,0:T(8,128)(2,1)} %bitcast.260), channel_id=1, replica_groups=mesh['dp'=8,'ctx'=4] {'dp'}, dimensions={0} | all-to-all | bytes 14155776 | tf_op jit(solution)/shard_map/all_to_all | solution.py:197
  284.5 14.7 fusion.70
  299.2 4.5 multiply_convert_fusion.3
  307.8 35.2 %copy.150 = bf16[2,1152,1536]{2,0,1:T(2,128)(2,1)} copy(bf16[2,1152,1536]{2,1,0:T(8,128)(2,1)S(1)} %convolution_convert_fusion.1) | data formatting | bytes 14155776 | tf_op jit(solution)/shard_map/convert_element_type | solution.py:82
  343.1 5.0 all-to-all-start.1
  348.7 82.7 %all-gather = bf16[8,192,16]{1,2,0:T(8,128)(2,1)S(1)} all-gather(bf16[1,192,16]{1,2,0:T(8,128)(2,1)S(1)} %bitcast.293), channel_id=1, replica_groups=mesh['dp'=8,'ctx'=4] {'dp'}, dimensions={0}, use_global_device_ids=true | all-gather | bytes 55296 | tf_op jit(solution)/shard_map/all_gather | solution.py:137
  435.7 16.1 %gather_fusion.3 = f32[2304,1536]{1,0:T(8,128)} fusion(f32[257,1536]{1,0:T(8,128)} %concatenate.63, s32[3072]{0:T(1024)S(1)} %pad_clamp_fusion), kind=kCustom, calls=%fused_computation.3 | custom fusion | bytes 28320768 | tf_op jit(solution)/shard_map/gather | solution.py:213
  453.5 7.3 copy.151
  460.8 45.9 %gather_fusion.1 = bf16[2048,1536]{1,0:T(8,128)(2,1)} fusion(bf16[16,144,1536]{2,1,0:T(8,128)(2,1)} %bitcast.252, s32[2048]{0:T(1024)S(1)} %reshape.444), kind=kCustom, calls=%fused_computation.1 | custom fusion | bytes 12599296 | tf_op jit(solution)/shard_map/gather | solution.py:200
  506.7 9.6 fusion.22
  516.6 14.4 gather_fusion.2
  531.1 8.8 multiply_convert_fusion
  539.9 83.9 %all_to_all.73 = bf16[16,144,1536]{2,1,0:T(8,128)(2,1)S(1)} all-to-all(bf16[16,144,1536]{2,1,0:T(8,128)(2,1)} %multiply_convert_fusion), channel_id=1, replica_groups=mesh['dp'=8,'ctx'=4] {'dp'}, dimensions={0} | all-to-all | bytes 14155776 | tf_op jit(solution)/shard_map/all_to_all | solution.py:214
  627.2 10.8 multiply_convert_fusion.2
  638.0 14.2 convolution_convert_fusion
  652.2 32.7 %copy.156 = bf16[2,1152,1536]{2,0,1:T(2,128)(2,1)} copy(bf16[2,1152,1536]{2,1,0:T(8,128)(2,1)} %convolution_convert_fusion) | data formatting | bytes 14155776 | tf_op jit(solution)/shard_map/convert_element_type | solution.py:96
  684.9 4.8 all-to-all-start.3
  690.0 79.8 %all-to-all-done.3 = bf16[2,1152,1536]{2,0,1:T(2,128)(2,1)} async-done(((bf16[2,1152,1536]{2,0,1:T(2,128)(2,1)}), bf16[2,1152,1536]{2,0,1:T(2,128)(2,1)}, u32[]{:S(2)}, u32[]{:S(2)}) %all-to-all-start.3) | async-done | bytes 7077920 | tf_op jit(solution)/shard_map/all_to_all | solution.py:218
  769.7 7.4 copy.157
  777.1 45.9 %gather_fusion.4 = bf16[2048,1536]{1,0:T(8,128)(2,1)} fusion(bf16[16,144,1536]{2,1,0:T(8,128)(2,1)} %bitcast.251, s32[2048]{0:T(1024)S(1)} %reshape.444), kind=kCustom, calls=%fused_computation.4 | custom fusion | bytes 12599296 | tf_op jit(solution)/shard_map/gather | solution.py:225
  823.0 7.2 convert_reduce_fusion
  836.9 41.1 %while.30 = (s32[]{:T(128)}, f32[256,8,3,64]{0,3,2,1:T(8,128)S(1)}, bf16[2,512,1024]{2,1,0:T(8,128)(2,1)}, s32[2]{0:T(128)S(1)}, s32[256]{0:T(256)S(1)}, /*index...) while((s32[]{:T(128)}, f32[256,8,3,64]{0,3,2,1:T(8,128)S(1)}, ...), condition=%wide.region_27.28_spmd, body=%wide.region_24.27_spmd.sunk | while | flops 2048394240 | bytes 148851632 | solution.py:298
  840.5 24.2 %conditional.5 = (f32[256,8,3,64]{0,3,2,1:T(8,128)S(1)}, bf16[1,512,1024]{1,2,0:T(8,128)(2,1)}) conditional(s32[]{:T(128)} %convert_element_type.345, f32[256,8,3,64]{0,3,2,1:T(8,128)S(1)} %get-tuple-element.669, (s32[]{:T(128)}, s32[1,512]{1,0:T(1,128)S(1)}, s32[256]{0:T(256)S(1)}, s32[]{:T(128)}, bf16[2,512,1024]{1,2,0:T(8,128)(2,1)}, ...), branch_computations={%region_25.25_spmd, %region_26.26_spmd} | conditional | flops 2048394240 | bytes 144654480 | solution.py:296
  844.6 5.8 fusion.11
  850.5 4.8 fusion.18
  855.3 7.2 fusion.15
  878.1 5.2 convolution_convert_fusion.2
  888.4 55.9 %reduce-scatter.8.cloned.1.call-done = bf16[256,1024]{1,0:T(8,128)(2,1)} async-done(((bf16[1024,1024]{1,0:T(8,128)(2,1)}), bf16[256,1024]{1,0:T(8,128)(2,1)}) %reduce-scatter.8.cloned.1.call-update) | async-done | bytes 524304 | tf_op jit(solution)/shard_map/reduce_scatter | solution.py:304
  951.0 15.2 convolution_convert_fusion.4
  966.3 8.6 convolution_convert_fusion.5
  974.9 26.4 %reduce-scatter.14.cloned.1.call-done = bf16[192,1536]{1,0:T(8,128)(2,1)} async-done(((bf16[1536,1536]{1,0:T(8,128)(2,1)}), bf16[192,1536]{1,0:T(8,128)(2,1)}) %reduce-scatter.14.cloned.1.call-update) | async-done | bytes 589840 | tf_op jit(solution)/shard_map/reduce_scatter | solution.py:346
  1001.3 58.0 %reduce-scatter.10.cloned.1.call-done = bf16[192,1536]{1,0:T(8,128)(2,1)} async-done(((bf16[1536,1536]{1,0:T(8,128)(2,1)}), bf16[192,1536]{1,0:T(8,128)(2,1)}) %reduce-scatter.10.cloned.1.call-update) | async-done | bytes 589840 | tf_op jit(solution)/shard_map/reduce_scatter | solution.py:340
  1059.3 50.0 %reduce-scatter.12.cloned.1.call-done = bf16[192,1024]{1,0:T(8,128)(2,1)} async-done(((bf16[1536,1024]{1,0:T(8,128)(2,1)}), bf16[192,1024]{1,0:T(8,128)(2,1)}) %reduce-scatter.12.cloned.1.call-update) | async-done | bytes 393232 | tf_op jit(solution)/shard_map/reduce_scatter | solution.py:343
  1110.0 36.8 %reduce-scatter.16.cloned.1.call-done = bf16[192,16]{1,0:T(8,128)(2,1)} async-done(((bf16[1536,16]{1,0:T(8,128)(2,1)}), bf16[192,16]{1,0:T(8,128)(2,1)}) %reduce-scatter.16.cloned.1.call-update) | async-done | bytes 6160
  1154.0 12.9 all-reduce.7
  1167.1 13.5 all-reduce.9
  1185.0 344.2 %all-reduce.13.cloned.1.call-done = (bf16[192,1536]{1,0:T(8,128)(2,1)}, bf16[192,1024]{1,0:T(8,128)(2,1)}, bf16[192,1536]{1,0:T(8,128)(2,1)}, bf16[2,1536,1024]{2,1,0:T(8,128)(2,1)}, bf16[2,512,1536]{2,1,0:T(8,128)(2,1)}) async-done(((bf16[192,1536]{1,0:T(8,128)(2,1)}, bf16[192,1024]{1,0:T(8,128)(2,1)}, bf16[192,1536]{1,0:T(8,128)(2,1)}, bf16[2,1536,1024]{2,1,0:T(8,128)(2,1)}, ...) | async-done | bytes 11010064 | tf_op jit(solution)/shard_map/psum | solution.py:365
  1529.2 9.3 convert_element_type.242
  (281 shorter events, 129.3 us)
Async XLA Ops:
  7.2 296.5 %copy-start = (bf16[2,512,1536]{2,1,0:T(8,128)(2,1)S(1)}, bf16[2,512,1536]{2,1,0:T(8,128)(2,1)}, u32[]{:S(2)}) copy-start(bf16[2,512,1536]{2,1,0:T(8,128)(2,1)} %param.31) | copy-start | bytes 9437188
  7.2 37.9 %all-gather.6.cloned.1.call-start = ((), (), s32[]{:S(2)}) async-start(), calls=%async_computation.9 | async-start | bytes 3538944 | tf_op jit(solution)/shard_map/all_gather | solution.py:135
  7.9 78.0 %all-gather.10.cloned.1.call-start = ((), (), s32[]{:S(2)}) async-start(), calls=%async_computation.11 | async-start | bytes 5308416 | tf_op jit(solution)/shard_map/all_gather | solution.py:134
  8.7 125.4 %all-gather.8.cloned.1.call-start = ((), (), s32[]{:S(2)}) async-start(), calls=%async_computation.10 | async-start | bytes 2621440 | tf_op jit(solution)/shard_map/all_gather | solution.py:171
  28.2 64.3 %copy-start.32 = (f32[1536]{0:T(1024)}, f32[1536]{0:T(1024)S(1)}, u32[]{:S(2)}) copy-start(f32[1536]{0:T(1024)S(1)} %convert_element_type.200) | copy-start | bytes 18436
  29.7 62.9 %copy-start.42 = (f32[256]{0:T(256)}, f32[256]{0:T(256)S(1)}, u32[]{:S(2)}) copy-start(f32[256]{0:T(256)S(1)} %add_rsqrt_fusion.1) | copy-start | bytes 3076
  30.5 66.3 %copy-start.25 = (f32[256,32]{0,1:T(8,128)}, f32[256,32]{0,1:T(8,128)S(1)}, u32[]{:S(2)}) copy-start(f32[256,32]{0,1:T(8,128)S(1)} %get-tuple-element.473) | copy-start | bytes 98308
  48.3 8.2 copy-start.34
  49.1 8.3 copy-start.49
  49.1 8.4 copy-start.48
  55.8 117.6 %all-gather.12.cloned.1.call-start = ((), (), s32[]{:S(2)}) async-start(), calls=%async_computation.12 | async-start | bytes 5308416 | tf_op jit(solution)/shard_map/all_gather | solution.py:136
  56.4 121.4 %copy-start.36 = (f32[1536]{0:T(1024)}, f32[1536]{0:T(1024)S(1)}, u32[]{:S(2)}) copy-start(f32[1536]{0:T(1024)S(1)} %convert_element_type.209) | copy-start | bytes 18436
  142.6 2.4 copy-start.3
  146.9 3.1 copy-start.9
  158.0 19.8 %copy-start.17 = (f32[8,3,256]{2,1,0:T(4,128)}, f32[8,3,256]{2,1,0:T(4,128)S(1)}, u32[]{:S(2)}) copy-start(f32[8,3,256]{2,1,0:T(4,128)S(1)} %get-tuple-element.663) | copy-start | bytes 73732
  158.0 19.8 %copy-start.21 = (f32[8,3,256]{2,1,0:T(4,128)}, f32[8,3,256]{2,1,0:T(4,128)S(1)}, u32[]{:S(2)}) copy-start(f32[8,3,256]{2,1,0:T(4,128)S(1)} %get-tuple-element.278) | copy-start | bytes 73732
  158.0 19.8 %copy-start.38 = (s32[256]{0:T(256)}, s32[256]{0:T(256)S(1)}, u32[]{:S(2)}) copy-start(s32[256]{0:T(256)S(1)} %get-tuple-element.760) | copy-start | bytes 3076
  177.8 19.3 %copy-start.45 = (f32[256]{0:T(256)}, f32[256]{0:T(256)S(1)}, u32[]{:S(2)}) copy-start(f32[256]{0:T(256)S(1)} %add_rsqrt_fusion) | copy-start | bytes 3076
  303.6 4.2 copy-start.23
  343.1 5.6 copy-start.47
  343.1 110.5 %all-to-all-start.1 = ((bf16[2,1152,1536]{2,0,1:T(2,128)(2,1)}), bf16[2,1152,1536]{2,0,1:T(2,128)(2,1)}, u32[]{:S(2)}, u32[]{:S(2)}) async-start(bf16[2,1152,1536]{2,0,1:T(2,128)(2,1)} %copy.150), calls=%async_computation.1 | async-start | bytes 14155776 | tf_op jit(solution)/shard_map/all_to_all | solution.py:199
  435.7 17.6 %copy-start.35 = (s32[1,256,8]{1,2,0:T(8,128)S(1)}, s32[1,256,8]{1,2,0:T(8,128)}, u32[]{:S(2)}) copy-start(s32[1,256,8]{1,2,0:T(8,128)} %param.22) | copy-start | bytes 24580
  516.5 313.7 %copy-start.40 = (bf16[256,16]{0,1:T(8,128)(2,1)}, bf16[256,16]{0,1:T(8,128)(2,1)S(1)}, u32[]{:S(2)}) copy-start(bf16[256,16]{0,1:T(8,128)(2,1)S(1)} %get-tuple-element.388) | copy-start | bytes 24580
  684.9 84.8 %all-to-all-start.3 = ((bf16[2,1152,1536]{2,0,1:T(2,128)(2,1)}), bf16[2,1152,1536]{2,0,1:T(2,128)(2,1)}, u32[]{:S(2)}, u32[]{:S(2)}) async-start(bf16[2,1152,1536]{2,0,1:T(2,128)(2,1)} %copy.156), calls=%async_computation.3 | async-start | bytes 14155776 | tf_op jit(solution)/shard_map/all_to_all | solution.py:218
  689.7 254.7 %reduce-scatter.8.cloned.1.call-start = ((), (), s32[]{:S(2)}) async-start(), calls=%async_computation.13 | async-start | bytes 2621440 | tf_op jit(solution)/shard_map/reduce_scatter | solution.py:304
  823.0 7.2 copy-start.6
  823.0 7.2 copy-start.37
  823.0 7.2 copy-start.46
  823.0 10.3 slice-start.2
  830.3 3.1 slice-start.3
  841.9 2.8 copy-start.27
  843.7 6.8 copy-start.2
  855.2 8.2 slice-start
  855.3 8.2 slice-start.1
  878.0 123.3 %reduce-scatter.14.cloned.1.call-start = ((), (), s32[]{:S(2)}) async-start(), calls=%async_computation.16 | async-start | bytes 5308416 | tf_op jit(solution)/shard_map/reduce_scatter | solution.py:346
  883.4 175.9 %reduce-scatter.10.cloned.1.call-start = ((), (), s32[]{:S(2)}) async-start(), calls=%async_computation.14 | async-start | bytes 5308416 | tf_op jit(solution)/shard_map/reduce_scatter | solution.py:340
  888.2 221.1 %reduce-scatter.12.cloned.1.call-start = ((), (), s32[]{:S(2)}) async-start(), calls=%async_computation.15 | async-start | bytes 3538944 | tf_op jit(solution)/shard_map/reduce_scatter | solution.py:343
  948.7 198.1 %reduce-scatter.16.cloned.1.call-start = ((), (), s32[]{:S(2)}) async-start(), calls=%async_computation.17 | async-start | bytes 442368
  951.0 578.2 %all-reduce.13.cloned.1.call-start = ((), (), s32[]{:S(2)}) async-start(), calls=%async_computation.18 | async-start | bytes 22020096 | tf_op jit(solution)/shard_map/psum | solution.py:365
  951.0 15.3 copy-start.24
  1147.6 4.0 copy-start.50
  1151.6 2.4 copy-start.44
  1151.6 30.7 %copy-start.13 = (f32[256,1536]{1,0:T(8,128)S(1)}, f32[256,1536]{1,0:T(8,128)}, u32[]{:S(2)}) copy-start(f32[256,1536]{1,0:T(8,128)} %copy-done.12) | copy-start | bytes 4718596
  1529.2 9.3 copy-start.19
  1538.5 3.6 copy-start.29
  1538.5 4.7 copy-start.28
  1538.5 6.9 copy-start.1
  1542.0 2.3 copy-start.30
  (19 other events, 26.1 us)
Sparse Core Ops, SparseCore 0:
  9.9 35.1 all-gather.5
  47.0 38.9 all-gather.9
  88.1 45.9 all-gather.7
  135.8 37.6 all-gather.11
  878.1 66.1 reduce-scatter.7
  948.1 53.2 reduce-scatter.13
  1005.3 53.8 reduce-scatter.9
  1063.0 46.2 reduce-scatter.11
  1112.9 33.7 reduce-scatter.15
  1150.3 378.8 all-reduce.12
where the time goes:
time: 1560 us; the launch traced here: 1550 us
  waiting for transfers between devices  736 us (47%)
  blocking collectives  293 us (19%)
  local copies, waits for them, and re-layouts  286 us (18%)
  matrix products  128 us (8%)
  other arithmetic  72.5 us (5%)
  between operations  17.3 us (1%)
    psum x1, waiting for transfers between devices, per_device(): lax.psum(share_query.astype(jnp.bfloat16), 'ctx').astype(jnp.float32)  344 us
    all_to_all x1, blocking collectives, per_device(): lax.all_to_all(expert_in, 'dp', split_axis=0, concat_axis=1, tiled=True)  84 us
    all_to_all x1, blocking collectives, per_device(): lax.all_to_all(grad_out, 'dp', split_axis=0, concat_axis=1, tiled=True)  83.9 us
    all_gather x1, blocking collectives, per_device(): lax.all_gather(w_router, 'dp', axis=0, tiled=True)  82.7 us
    all_to_all x1, waiting for transfers between devices, per_device(): lax.all_to_all(grad_in_own, 'dp', split_axis=1, concat_axis=0, tiled=True)  79.8 us
    reduce_scatter x1, waiting for transfers between devices, per_device(): lax.psum_scatter(part_query.astype(jnp.bfloat16), 'dp', scatter_dimension...  58 us
    reduce_scatter x1, waiting for transfers between devices, per_device(): lax.psum_scatter(grad_kv_flat.astype(jnp.bfloat16), 'ctx', scatter_dimens...  55.9 us
    reduce_scatter x1, waiting for transfers between devices, per_device(): lax.psum_scatter(part_keyval.astype(jnp.bfloat16), 'dp', scatter_dimensio...  50 us
  transfers between devices with their start and end apart: 12, of which 11 were waited for; matrix products, arithmetic and copies ran while one was open for 8% of the time, Pallas kernels for 0%

commit v1 on v0

v1 whole, which is shorter than its diff:
```python
import functools

import jax
import jax.numpy as jnp
from jax import lax
from jax.experimental import pallas as pl
from jax.experimental.pallas import tpu as pltpu
from jax.sharding import PartitionSpec as P

HD = 64
NORM_EPS = 1e-06
ROPE_BASE = 10000.0
MASK_FLOOR = -1e30
F32 = jnp.float32
BF16 = jnp.bfloat16
MIB = 1024 * 1024
SIDE = 128


def params(mib):
    return pltpu.CompilerParams(vmem_limit_bytes=mib * MIB)


def cost(flops):
    return pl.CostEstimate(flops=int(flops), bytes_accessed=int(flops) // 512, transcendentals=0)


def up(v):
    return v.astype(F32)


def low(v):
    return v.astype(BF16)


def dot_nn(a, b):
    return lax.dot_general(a, b, (((1,), (0,)), ((), ())), preferred_element_type=F32)


def dot_nt(a, b):
    return lax.dot_general(a, b, (((1,), (1,)), ((), ())), preferred_element_type=F32)


def dot_tn(a, b):
    return lax.dot_general(a, b, (((0,), (0,)), ((), ())), preferred_element_type=F32)


def swap(v, mask):
    count = lax.axis_size("dp")
    return lax.ppermute(v, "dp", [(i, i ^ mask) for i in range(count)])


def halves(v):
    mid = v.shape[0] // 2
    return [v[:mid], v[mid:]]


class Gather:
    def __init__(self, v):
        self.special = lax.axis_size("dp") == 8
        self.stage = 0
        self.live = [v]

    def near(self):
        if self.special and self.stage == 0:
            v = self.live[0]
            self.live = [v, swap(v, 2), swap(v, 4)]
        self.stage = max(self.stage, 1)

    def far(self):
        self.near()
        if self.special and self.stage == 1:
            v, along_x, along_y = self.live
            self.live = self.live + [swap(halves(along_x)[0], 4), swap(halves(along_y)[1], 2)]
        self.stage = max(self.stage, 2)

    def pieces(self):
        self.far()
        if not self.special:
            out = [[self.live[0]]]
            bit = 1
            while bit < lax.axis_size("dp"):
                out = out + [[swap(h, bit) for h in piece] for piece in out]
                bit *= 2
            return out
        v, along_x, along_y, far_a, far_b = self.live
        even = [[v], [along_x], [along_y], [far_a, far_b]]
        out = []
        for piece in even:
            out += [piece, [swap(h, 1) for h in piece]]
        return out


def sync(*items):
    plain = [i.live if isinstance(i, (Gather, Scatter)) else i for i in items]
    plain = lax.optimization_barrier(plain)
    for item, got in zip(items, plain):
        if isinstance(item, (Gather, Scatter)):
            item.live = list(got)
    return plain


def add_low(a, b):
    return low(up(a) + up(b))


class Scatter:
    def __init__(self, even, odd):
        self.special = lax.axis_size("dp") == 8
        self.rows = even.shape[0] * 2 // lax.axis_size("dp")
        self.live = [even, odd]

    def core(self):
        even, odd = self.live
        self.live = [even, swap(odd, 1)]

    def part(self, n, lo, hi):
        at = slice(n * self.rows + lo, n * self.rows + hi)
        return up(self.live[0][at]) + up(self.live[1][at])

    def far(self):
        if not self.special:
            held = add_low(self.live[0], self.live[1])
            bit = lax.axis_size("dp") // 2
            while bit >= 2:
                cut = held.shape[0] // 2
                held = add_low(held[:cut], swap(held[cut:], bit))
                bit //= 2
            self.live = [held]
            return
        mid, rows = self.rows // 2, self.rows
        from_x = swap(low(self.part(3, 0, mid)), 2)
        from_y = swap(low(self.part(3, mid, rows)), 4)
        self.live = self.live + [from_x, from_y]

    def near(self):
        if not self.special:
            return
        mid, rows = self.rows // 2, self.rows
        from_x, from_y = self.live[2:]
        for_x = [low(self.part(1, 0, mid)), low(self.part(1, mid, rows) + up(from_y))]
        for_y = [low(self.part(2, 0, mid) + up(from_x)), low(self.part(2, mid, rows))]
        for_x, for_y = jnp.concatenate(for_x, 0), jnp.concatenate(for_y, 0)
        self.live = [low(self.part(0, 0, rows)), swap(for_x, 2), swap(for_y, 4)]


def total_of(parts):
    out = up(parts[0])
    for p in parts[1:]:
        out = out + up(p)
    return out


def shift(v, step):
    count = lax.axis_size("ctx")
    return lax.ppermute(
        v, "ctx", [(i, i + step) for i in range(count) if 0 <= i + step < count]
    )


class LineSums:
    def __init__(self):
        self.count = lax.axis_size("ctx")
        self.index = lax.axis_index("ctx")
        self.plain = self.count % 2 == 1 or self.count > 4
        self.mid = self.count // 2
        self.stages = 2 * self.mid - 1
        self.waiting = []
        self.moving = [[], []]
        self.done = {}
        self.marks = [[], []]

    def add(self, name, v):
        if self.plain:
            self.done[name] = lax.psum(v, "ctx")
        else:
            self.waiting.append((name, v))

    def send(self, v, stage):
        n, mid = self.count, self.mid
        if stage < mid - 1:
            pairs = [(stage, stage + 1), (n - 1 - stage, n - 2 - stage)]
        elif stage == mid - 1:
            pairs = [(mid - 1, mid), (mid, mid - 1)]
        else:
            k = 2 * mid - 2 - stage
            pairs = [(k + 1, k), (n - 2 - k, n - 1 - k)]
        return lax.ppermute(v, "ctx", pairs)

    def merge(self, v, got, stage):
        if stage <= self.mid - 1:
            return (up(v) + up(got)).astype(v.dtype)
        k = 2 * self.mid - 2 - stage
        return jnp.where((self.index == k) | (self.index == self.count - 1 - k), got, v)

    def busy(self):
        return bool(self.waiting or self.moving[0] or self.moving[1])

    def step(self, *critical):
        if self.plain:
            return critical
        ended = self.moving.pop(0)
        ready = []
        for name, v, got, stage in ended:
            ready.append((name, self.merge(v, got, stage), stage + 1))
        if self.waiting:
            name, v = self.waiting.pop(0)
            ready.append((name, v, 0))
        values, critical = lax.optimization_barrier(([v for _, v, _ in ready], tuple(critical)))
        self.moving.append([])
        for (name, _, stage), v in zip(ready, values):
            if stage == self.stages:
                self.done[name] = v
            else:
                self.moving[-1].append((name, v, self.send(v, stage), stage))
        return critical


def lay_rows(pieces, counts, index, put):
    n = 0
    for k, parts in enumerate(counts):
        rows = sum(pieces[n + i].shape[0] for i in range(parts))
        start = (index ^ k) * rows
        for i in range(parts):
            put(pl.multiple_of(start, 16), pieces[n + i])
            start = start + pieces[n + i].shape[0]
        n += parts


def turn(v, cosine, sine):
    lane = lax.broadcasted_iota(jnp.int32, v.shape, 1)
    first = lax.rem(lane, HD) < HD // 2
    partner = jnp.where(
        first, pltpu.roll(v, 2 * HD - HD // 2, 1), pltpu.roll(v, HD // 2, 1)
    )
    return v * cosine + partner * sine


def project_kernel(counts, blocks, experts, q_width, index_ref, *refs):
    pieces = refs[: sum(counts)]
    seq = refs[sum(counts) : sum(counts) + blocks]
    cos_ref, sin_ref = refs[sum(counts) + blocks : sum(counts) + blocks + 2]
    q_ref, kv_ref, hn_ref, wq_ref, wkv_ref, router_ref, gains_ref, small_ref = refs[
        sum(counts) + blocks + 2 :
    ]
    kv_width = wkv_ref.shape[1]

    def put(start, ref):
        at = pl.ds(start, ref.shape[0])
        wq_ref[at, :] = ref[:, :q_width]
        wkv_ref[at, :] = ref[:, q_width : q_width + kv_width]
        small_ref[at, :] = ref[:, q_width + kv_width :]

    lay_rows(pieces, counts, index_ref[0], put)
    small = up(small_ref[...])
    lane = lax.broadcasted_iota(jnp.int32, small.shape, 1)
    router_ref[...] = low(jnp.where(lane < experts, small, 0.0))
    gains_ref[...] = jnp.transpose(small)[experts : experts + 8]
    gain = gains_ref[0:1, :]
    rows = seq[0].shape[0]
    for r in range(blocks):
        x = up(seq[r][...])
        inv = lax.rsqrt(jnp.mean(x * x, -1, keepdims=True) + NORM_EPS)
        hn_ref[r * rows : (r + 1) * rows, :] = low(x * inv * gain)
    two = 2 * HD
    for c in range(0, q_width, 2 * two):
        raw = dot_nn(hn_ref[:rows, :], wq_ref[:, c : c + 2 * two])
        for d in (0, two):
            rot = turn(raw[:, d : d + two], cos_ref[:rows, :], sin_ref[:rows, :])
            q_ref[:, c + d : c + d + two] = low(up(low(rot)) * (HD ** (-0.5)))
    for r in range(blocks):
        at = slice(r * rows, (r + 1) * rows)
        raw = dot_nn(hn_ref[at, :], wkv_ref[...])
        for d in range(0, kv_width // 2, two):
            kv_ref[at, d : d + two] = low(
                turn(raw[:, d : d + two], cos_ref[at, :], sin_ref[at, :])
            )
        kv_ref[at, kv_width // 2 :] = low(raw[:, kv_width // 2 :])


def project(index, pieces, seq, cosine, sine, experts, q_width):
    counts = [len(p) for p in pieces]
    flat = [h for p in pieces for h in p]
    rows, width = seq[0].shape
    kv_width = flat[0].shape[1] - q_width - 128
    whole = pl.BlockSpec(memory_space=pltpu.VMEM)
    keys = rows * len(seq)
    return pl.pallas_call(
        functools.partial(project_kernel, counts, len(seq), experts, q_width),
        in_specs=[pl.BlockSpec(memory_space=pltpu.SMEM)] + [whole] * (len(flat) + len(seq) + 2),
        out_specs=[whole] * 7,
        out_shape=[
            jax.ShapeDtypeStruct((rows, q_width), BF16),
            jax.ShapeDtypeStruct((keys, kv_width), BF16),
            jax.ShapeDtypeStruct((keys, width), BF16),
            jax.ShapeDtypeStruct((width, q_width), BF16),
            jax.ShapeDtypeStruct((width, kv_width), BF16),
            jax.ShapeDtypeStruct((width, 128), BF16),
            jax.ShapeDtypeStruct((8, width), F32),
        ],
        scratch_shapes=[pltpu.VMEM((width, 128), BF16)],
        compiler_params=params(36),
        cost_estimate=cost(8 * width * (rows * q_width + keys * kv_width)),
        name="project",
    )(index, *flat, *seq, cosine, sine)


def after_attend_kernel(counts, index_ref, *refs):
    pieces = refs[: sum(counts)]
    attn_ref, tok_ref, gains_ref, wo_ref, resid_ref, hn_ref, low_ref = refs[sum(counts) :]

    def put(start, ref):
        wo_ref[pl.ds(start, ref.shape[0]), :] = ref[...]

    lay_rows(pieces, counts, index_ref[0], put)
    attn = low(attn_ref[...])
    low_ref[...] = attn
    resid = up(tok_ref[...]) + dot_nn(attn, wo_ref[...])
    resid_ref[...] = resid
    inv = lax.rsqrt(jnp.mean(resid * resid, -1, keepdims=True) + NORM_EPS)
    hn_ref[...] = low(resid * inv * gains_ref[1:2, :])


def after_attend(index, pieces, attn, tokens, gains):
    counts = [len(p) for p in pieces]
    flat = [h for p in pieces for h in p]
    rows, width = tokens.shape
    heads = attn.shape[1]
    whole = pl.BlockSpec(memory_space=pltpu.VMEM)
    return pl.pallas_call(
        functools.partial(after_attend_kernel, counts),
        in_specs=[pl.BlockSpec(memory_space=pltpu.SMEM)] + [whole] * (len(flat) + 3),
        out_specs=[whole] * 4,
        out_shape=[
            jax.ShapeDtypeStruct((heads, width), BF16),
            jax.ShapeDtypeStruct((rows, width), F32),
            jax.ShapeDtypeStruct((rows, width), BF16),
            jax.ShapeDtypeStruct((rows, heads), BF16),
        ],
        compiler_params=params(24),
        cost_estimate=cost(12 * rows * heads * width),
        name="after_attend",
    )(index, *flat, attn, tokens, gains)


def router_back_kernel(count, experts, *refs):
    parts = refs[:count]
    (
        gates_ref,
        router_ref,
        gains_ref,
        resid_ref,
        cot_ref,
        wo_ref,
        grad_ref,
        attn_ref,
        heads_ref,
        logits_ref,
        gain_ref,
    ) = refs[count:]
    width = resid_ref.shape[1]
    total = up(parts[0][...])
    for p in parts[1:]:
        total = total + up(p[...])
    side = total[:, width:]
    lane = lax.broadcasted_iota(jnp.int32, side.shape, 1)
    gate_grads = jnp.where(lane < experts, side + pltpu.roll(side, SIDE // 2, 1), 0.0)
    gates = gates_ref[...]
    mean = jnp.sum(gates * gate_grads, -1, keepdims=True)
    grad_logits = low(gates * (gate_grads - mean))
    logits_ref[...] = grad_logits
    grad_hn = total[:, :width] + dot_nt(grad_logits, router_ref[...])
    resid = resid_ref[...]
    inv = lax.rsqrt(jnp.mean(resid * resid, -1, keepdims=True) + NORM_EPS)
    normed = resid * inv
    gain_ref[...] = jnp.broadcast_to(jnp.sum(grad_hn * normed, 0, keepdims=True), gain_ref.shape)
    scaled = grad_hn * gains_ref[1:2, :]
    grad = up(cot_ref[...]) + inv * (scaled - normed * jnp.mean(scaled * normed, -1, keepdims=True))
    grad_ref[...] = grad
    grad_low = low(grad)
    attn_ref[...] = grad_low
    heads_ref[...] = dot_nt(grad_low, wo_ref[...])


def router_back(parts, gates, router, gains, resid, cot, wo, experts):
    rows, width = resid.shape
    heads = wo.shape[0]
    whole = pl.BlockSpec(memory_space=pltpu.VMEM)
    return pl.pallas_call(
        functools.partial(router_back_kernel, len(parts), experts),
        in_specs=[whole] * (len(parts) + 6),
        out_specs=[whole] * 5,
        out_shape=[
            jax.ShapeDtypeStruct((rows, width), F32),
            jax.ShapeDtypeStruct((rows, width), BF16),
            jax.ShapeDtypeStruct((rows, heads), F32),
            jax.ShapeDtypeStruct((rows, SIDE), BF16),
            jax.ShapeDtypeStruct((8, width), F32),
        ],
        compiler_params=params(28),
        cost_estimate=cost(14 * rows * heads * width),
        name="router_back",
    )(*parts, gates, router, gains, resid, cot, wo)


def transposed(v):
    return jnp.transpose(up(v))


def key_bias(place_ref, keys, rows):
    j = lax.broadcasted_iota(jnp.int32, (keys, rows), 0)
    i = lax.broadcasted_iota(jnp.int32, (keys, rows), 1)
    block = lax.div(j, rows)
    place = (place_ref[0] - block) * rows + (j - block * rows)
    allowed = (place >= 0) & (place <= place_ref[0] * rows + i) & (place < place_ref[1])
    return jnp.where(allowed, 0.0, MASK_FLOOR)


def widened(part, group):
    zero = jnp.zeros_like(part)
    return jnp.concatenate([part, zero] if group == 0 else [zero, part], 0)


def attend_kernel(groups, place_ref, q_ref, k_ref, v_ref, out_ref, max_ref, total_ref, bias_ref):
    rows = q_ref.shape[0]
    keys = k_ref.shape[0]

    @pl.when(pl.program_id(0) == 0)
    def _():
        bias_ref[...] = key_bias(place_ref, keys, rows)

    q_t = low(transposed(q_ref[...]))
    v_t = low(transposed(v_ref[...]))
    outs, maxes, totals = [], [], []
    for group in range(2):
        parts = [
            widened(q_t[(group * groups + h) * HD : (group * groups + h + 1) * HD], group)
            for h in range(groups)
        ]
        scores = dot_nn(k_ref[...], jnp.concatenate(parts, 1))
        weights = []
        for h in range(groups):
            s = scores[:, h * rows : (h + 1) * rows] + bias_ref[...]
            top = jnp.max(s, 0, keepdims=True)
            w = jnp.exp(s - top)
            totals.append(jnp.sum(w, 0, keepdims=True))
            maxes.append(top)
            weights.append(low(w))
        mixed = dot_nn(v_t, jnp.concatenate(weights, 1))
        for h in range(groups):
            part = mixed[group * HD : (group + 1) * HD, h * rows : (h + 1) * rows]
            outs.append(part / totals[group * groups + h])
    out_ref[...] = jnp.transpose(jnp.concatenate(outs, 0))
    pad = [jnp.ones((8 - 2 * groups, rows), F32)] if 2 * groups < 8 else []
    max_ref[0] = jnp.concatenate(maxes + pad, 0)
    total_ref[0] = jnp.concatenate(totals + pad, 0)


def attend(place, queries, keyval, groups):
    rows, width = queries.shape
    keys, kv = keyval.shape
    steps = kv // 2 // (2 * HD)
    heads = 2 * groups * HD
    return pl.pallas_call(
        functools.partial(attend_kernel, groups),
        grid_spec=pltpu.PrefetchScalarGridSpec(
            num_scalar_prefetch=1,
            grid=(steps,),
            in_specs=[
                pl.BlockSpec((rows, heads), lambda i, s: (0, i)),
                pl.BlockSpec((keys, 2 * HD), lambda i, s: (0, i)),
                pl.BlockSpec((keys, 2 * HD), lambda i, s: (0, steps + i)),
            ],
            out_specs=[
                pl.BlockSpec((rows, heads), lambda i, s: (0, i)),
                pl.BlockSpec((1, 8, rows), lambda i, s: (i, 0, 0)),
                pl.BlockSpec((1, 8, rows), lambda i, s: (i, 0, 0)),
            ],
            scratch_shapes=[pltpu.VMEM((keys, rows), F32)],
        ),
        out_shape=[
            jax.ShapeDtypeStruct((rows, width), F32),
            jax.ShapeDtypeStruct((steps, 8, rows), F32),
            jax.ShapeDtypeStruct((steps, 8, rows), F32),
        ],
        compiler_params=params(28),
        cost_estimate=cost(40 * rows * keys * width),
        name="attend",
    )(place, queries, keyval, keyval)


def attend_back_kernel(
    groups,
    place_ref,
    q_ref,
    k_ref,
    v_ref,
    grad_ref,
    out_ref,
    max_ref,
    total_ref,
    cos_ref,
    sin_ref,
    gq_ref,
    gk_ref,
    gv_ref,
    bias_ref,
):
    rows = q_ref.shape[0]
    keys = k_ref.shape[0]
    chunk = 256

    @pl.when(pl.program_id(0) == 0)
    def _():
        bias_ref[...] = key_bias(place_ref, keys, rows)

    q_t = low(transposed(q_ref[...]))
    k_t = low(transposed(k_ref[...]))
    grad_t = transposed(grad_ref[...])
    out_t = transposed(out_ref[...])
    q_parts, g_parts, deltas, tops, grads = [], [], [], [], []
    for group in range(2):
        q_part, g_part, delta = [], [], []
        for h in range(groups):
            n = group * groups + h
            total = total_ref[0, n : n + 1]
            grad = grad_t[n * HD : (n + 1) * HD]
            q_part.append(widened(q_t[n * HD : (n + 1) * HD], group))
            g_part.append(widened(low(grad / total), group))
            delta.append(jnp.sum(out_t[n * HD : (n + 1) * HD] * grad, 0, keepdims=True) / total)
        q_parts.append(jnp.concatenate(q_part, 1))
        g_parts.append(jnp.concatenate(g_part, 1))
        deltas.append(jnp.concatenate(delta, 1))
        tops.append(
            jnp.concatenate(
                [max_ref[0, group * groups + h : group * groups + h + 1] for h in range(groups)], 1
            )
        )
        grads.append(jnp.zeros((2 * HD, groups * rows), F32))
    for start in range(0, keys, chunk):
        bias = bias_ref[start : start + chunk]
        bias = jnp.concatenate([bias] * groups, 1)
        grad_k = jnp.zeros((chunk, 2 * HD), F32)
        grad_v = jnp.zeros((chunk, 2 * HD), F32)
        for group in range(2):
            scores = dot_nn(k_ref[start : start + chunk], q_parts[group])
            w = jnp.exp(scores + bias - tops[group])
            gp = dot_nn(v_ref[start : start + chunk], g_parts[group])
            gs = low(w * (gp - deltas[group]))
            grad_v = grad_v + dot_nt(low(w), g_parts[group])
            grad_k = grad_k + dot_nt(gs, q_parts[group])
            grads[group] = grads[group] + dot_nn(k_t[:, start : start + chunk], gs)
        at = slice(start, start + chunk)
        gk_ref[at] = low(turn(grad_k, cos_ref[at, :], -sin_ref[at, :]))
        gv_ref[at] = low(grad_v)
    parts = []
    for group in range(2):
        for h in range(groups):
            parts.append(grads[group][group * HD : (group + 1) * HD, h * rows : (h + 1) * rows])
    grad_q = jnp.transpose(jnp.concatenate(parts, 0)) * (HD ** (-0.5))
    for d in range(0, 2 * groups * HD, 2 * HD):
        gq_ref[:, d : d + 2 * HD] = low(
            turn(grad_q[:, d : d + 2 * HD], cos_ref[:rows, :], -sin_ref[:rows, :])
        )


def attend_back(place, queries, keyval, grad_heads, attn, tops, totals, cosine, sine, groups):
    rows, width = queries.shape
    keys, kv = keyval.shape
    steps = kv // 2 // (2 * HD)
    heads = 2 * groups * HD
    head_spec = pl.BlockSpec((rows, heads), lambda i, s: (0, i))
    key_spec = pl.BlockSpec((keys, 2 * HD), lambda i, s: (0, i))
    stat_spec = pl.BlockSpec((1, 8, rows), lambda i, s: (i, 0, 0))
    return pl.pallas_call(
        functools.partial(attend_back_kernel, groups),
        grid_spec=pltpu.PrefetchScalarGridSpec(
            num_scalar_prefetch=1,
            grid=(steps,),
            in_specs=[
                head_spec,
                key_spec,
                pl.BlockSpec((keys, 2 * HD), lambda i, s: (0, steps + i)),
                head_spec,
                head_spec,
                stat_spec,
                stat_spec,
                pl.BlockSpec((keys, 2 * HD), lambda i, s: (0, 0)),
                pl.BlockSpec((keys, 2 * HD), lambda i, s: (0, 0)),
            ],
            out_specs=[head_spec, key_spec, key_spec],
            scratch_shapes=[pltpu.VMEM((keys, rows), F32)],
        ),
        out_shape=[
            jax.ShapeDtypeStruct((rows, width), BF16),
            jax.ShapeDtypeStruct((keys, kv // 2), BF16),
            jax.ShapeDtypeStruct((keys, kv // 2), BF16),
        ],
        compiler_params=params(36),
        cost_estimate=cost(64 * rows * keys * width),
        name="attend_back",
    )(place, queries, keyval, keyval, grad_heads, attn, tops, totals, cosine, sine)


def expert_kernel(counts, cap, tile, experts, number_ref, *refs):
    parts = refs[: sum(counts)]
    cots = refs[sum(counts) : 2 * sum(counts)]
    (
        router_ref,
        wgu_ref,
        wd_ref,
        out_ref,
        gin_ref,
        gwgu_ref,
        gwd_ref,
        slots_ref,
        gates_ref,
        x_ref,
        c_ref,
        ggu_ref,
        act_ref,
        sg_ref,
        turned_ref,
    ) = refs[2 * sum(counts) :]
    blocks = len(counts)
    width = wd_ref.shape[1]
    rows = parts[0].shape[0]
    hidden = wd_ref.shape[0]
    total = blocks * cap
    expert = number_ref[1]
    below = lax.broadcasted_iota(jnp.int32, (rows, rows), 1) <= lax.broadcasted_iota(
        jnp.int32, (rows, rows), 0
    )
    below = low(jnp.where(below, 1.0, 0.0))
    place = lax.broadcasted_iota(jnp.int32, (cap, rows), 0)
    n = 0
    for b in range(blocks):
        hn, cot = parts[n : n + counts[b]], cots[n : n + counts[b]]
        n += counts[b]
        hits = jnp.concatenate([part[:, width:] for part in cot], 0)
        named = up(hits) > 0.5
        order = jnp.where(named, dot_nn(below, hits) - 1.0, -1.0)
        logits = [dot_nn(part[...], router_ref[...]) for part in hn]
        logits = jnp.where(named, jnp.concatenate(logits, 0), MASK_FLOOR)
        gates = jnp.where(named, jnp.exp(logits - jnp.max(logits, -1, keepdims=True)), 0.0)
        gates = gates / jnp.sum(gates, -1, keepdims=True)
        if b == 0:
            gates_ref[...] = gates
        turned_ref[0] = jnp.transpose(order)
        turned_ref[1] = jnp.transpose(gates)
        slot = turned_ref[0, pl.ds(expert, 1), :].astype(jnp.int32)
        slots_ref[b : b + 1, :] = slot
        hit = place == slot
        pick = low(jnp.where(hit, 1.0, 0.0))
        at = slice(b * cap, (b + 1) * cap)
        for from_parts, to_ref in ((hn, x_ref), (cot, c_ref)):
            taken, start = None, 0
            for part in from_parts:
                piece = dot_nn(pick[:, start : start + part.shape[0]], part[:, :width])
                taken = piece if taken is None else taken + piece
                start += part.shape[0]
            to_ref[at, :] = low(taken)
        gate = jnp.sum(
            jnp.where(hit, turned_ref[1, pl.ds(expert, 1), :], 0.0), 1, keepdims=True
        )
        sg_ref[at, :] = jnp.broadcast_to(gate, (cap, 128))

    def middle(t, carry):
        at = pl.ds(pl.multiple_of(t * tile, 16), tile)
        gate_up = dot_nn(x_ref[at, :], wgu_ref[...])
        g = gate_up[:, :hidden]
        u = gate_up[:, hidden:]
        sigma = jax.nn.sigmoid(g)
        silu = g * sigma
        act = low(silu * u)
        slot_gate = sg_ref[at, :][:, :1]
        back = dot_nt(c_ref[at, :], wd_ref[...])
        gate_grad = jnp.sum(up(act) * back, 1, keepdims=True)
        back = back * slot_gate
        act_ref[at, :] = low(up(act) * slot_gate)
        ggu_ref[at, :hidden] = low(back * u * (sigma * (1.0 + g * (1.0 - sigma))))
        ggu_ref[at, hidden:] = low(back * silu)
        out_ref[at, :] = low(dot_nn(act, wd_ref[...]) * slot_gate)
        gin_ref[at, :width] = low(dot_nt(ggu_ref[at, :], wgu_ref[...]))
        lane = lax.broadcasted_iota(jnp.int32, (tile, SIDE), 1)
        high = up(low(gate_grad))
        side = jnp.where(lane == expert, high, 0.0)
        side = jnp.where(lane == expert + SIDE // 2, gate_grad - high, side)
        gin_ref[at, width:] = low(side)
        return carry

    lax.fori_loop(0, total // tile, middle, 0)
    step = 256

    def down_grad(t, carry):
        at = pl.ds(pl.multiple_of(t * step, step), step)
        gwd_ref[at, :] = low(dot_tn(act_ref[:, at], c_ref[...]))
        return carry

    lax.fori_loop(0, hidden // step, down_grad, 0)

    def up_grad(t, carry):
        at = pl.ds(pl.multiple_of(t * step, step), step)
        gwgu_ref[at, :] = low(dot_tn(x_ref[:, at], ggu_ref[...]))
        return carry

    lax.fori_loop(0, width // step, up_grad, 0)


def run_expert(number, pieces, cots, router, wgu, wd, cap, experts):
    counts = [len(p) for p in pieces]
    flat = [h for p in pieces for h in p] + [h for p in cots for h in p]
    blocks = len(counts)
    rows = flat[0].shape[0]
    width = wd.shape[1]
    hidden = wd.shape[0]
    total = blocks * cap
    tile = max(t for t in range(16, 401, 16) if total % t == 0)
    whole = pl.BlockSpec(memory_space=pltpu.VMEM)
    return pl.pallas_call(
        functools.partial(expert_kernel, counts, cap, tile, experts),
        in_specs=[pl.BlockSpec(memory_space=pltpu.SMEM)] + [whole] * (len(flat) + 3),
        out_specs=[whole] * 6,
        out_shape=[
            jax.ShapeDtypeStruct((total, width), BF16),
            jax.ShapeDtypeStruct((total, width + SIDE), BF16),
            jax.ShapeDtypeStruct((width, 2 * hidden), BF16),
            jax.ShapeDtypeStruct((hidden, width), BF16),
            jax.ShapeDtypeStruct((blocks, rows), jnp.int32),
            jax.ShapeDtypeStruct((rows, SIDE), F32),
        ],
        scratch_shapes=[
            pltpu.VMEM((total, width), BF16),
            pltpu.VMEM((total, width), BF16),
            pltpu.VMEM((total, 2 * hidden), BF16),
            pltpu.VMEM((total, hidden), BF16),
            pltpu.VMEM((total, 128), F32),
            pltpu.VMEM((2, SIDE, rows), F32),
        ],
        compiler_params=params(52),
        cost_estimate=cost(44 * total * width * hidden),
        name="expert",
    )(number, *flat, router, wgu, wd)


def combine_kernel(count, cap, first, stride, number_ref, *refs):
    slots, parts, out_ref = refs[:count], refs[count : 2 * count], refs[2 * count]
    b = pl.program_id(0) * stride + first
    rows = slots[0].shape[1]
    place = lax.broadcasted_iota(jnp.int32, (cap, rows), 0)
    acc = None
    for e in range(count):
        pick = low(jnp.where(place == slots[e][pl.ds(b, 1), :], 1.0, 0.0))
        part = dot_tn(pick, parts[e][...])
        acc = part if acc is None else acc + part
    out_ref[...] = low(acc)


def combine(number, slots, parts, cap, chosen, order):
    blocks, rows = slots[0].shape
    count = len(parts)
    width = parts[0].shape[1]
    first, stride = chosen.start, chosen.step
    return pl.pallas_call(
        functools.partial(combine_kernel, count, cap, first, stride),
        grid_spec=pltpu.PrefetchScalarGridSpec(
            num_scalar_prefetch=1,
            grid=(len(chosen),),
            in_specs=[pl.BlockSpec((blocks, rows), lambda n, s: (0, 0))] * count
            + [pl.BlockSpec((cap, width), lambda n, s: (n * stride + first, 0))] * count,
            out_specs=pl.BlockSpec((rows, width), lambda n, s: (order(n, s[0]), 0)),
        ),
        out_shape=jax.ShapeDtypeStruct((len(chosen) * rows, width), BF16),
        compiler_params=params(20),
        cost_estimate=cost(10 * len(chosen) * cap * rows * width),
        name="combine",
    )(number, *slots, *parts)


def weight_grad_kernel(count, index_ref, hn_ref, gq_ref, gk_ref, gv_ref, even_ref, odd_ref):
    rows = gq_ref.shape[0]
    size = even_ref.shape[1]
    step = 256

    def put(value, col):
        for j in range(count):
            k = index_ref[0] ^ j
            block = low(value[j * size : (j + 1) * size])

            @pl.when(lax.rem(k, 2) == 0)
            def _():
                even_ref[k // 2, :, col : col + step] = block

            @pl.when(lax.rem(k, 2) == 1)
            def _():
                odd_ref[k // 2, :, col : col + step] = block

    col = 0
    for ref, taken in ((gq_ref, rows), (gk_ref, hn_ref.shape[0]), (gv_ref, hn_ref.shape[0])):
        for c in range(0, ref.shape[1], step):
            put(dot_tn(hn_ref[:taken, :], ref[:, c : c + step]), col)
            col += step


def weight_grad(index, hn, gq, gk, gv):
    count = lax.axis_size("dp")
    width = hn.shape[1]
    cols = gq.shape[1] + gk.shape[1] + gv.shape[1]
    shape = jax.ShapeDtypeStruct((count // 2, width // count, cols), BF16)
    whole = pl.BlockSpec(memory_space=pltpu.VMEM)
    even, odd = pl.pallas_call(
        functools.partial(weight_grad_kernel, count),
        in_specs=[pl.BlockSpec(memory_space=pltpu.SMEM)] + [whole] * 4,
        out_specs=[whole] * 2,
        out_shape=[shape, shape],
        compiler_params=params(32),
        cost_estimate=cost(8 * width * (hn.shape[0] * 2 * gk.shape[1] + gq.shape[0] * gq.shape[1])),
        name="weight_grad",
    )(index, hn, gq, gk, gv)
    return even.reshape(-1, cols), odd.reshape(-1, cols)


def rope_tables(places):
    half = HD // 2
    frequency = ROPE_BASE ** (-jnp.arange(half, dtype=F32) * 2.0 / HD)
    angles = places.astype(F32)[:, None] * frequency[None, :]
    cosine, sine = jnp.cos(angles), jnp.sin(angles)
    return jnp.concatenate([cosine] * 4, 1), jnp.concatenate([-sine, sine] * 2, 1)


def per_device(
    tokens,
    lengths,
    routes,
    cotangent,
    gain_attn,
    gain_moe,
    w_query,
    w_keyval,
    w_output,
    w_router,
    w_gate_up,
    w_down,
):
    rows = tokens.shape[1]
    width = tokens.shape[2]
    experts = w_router.shape[1]
    local_experts = w_gate_up.shape[0]
    kv_width = w_keyval.shape[1] // 2
    head_total = w_query.shape[1]
    groups = head_total // kv_width
    dp_count = lax.axis_size("dp")
    ctx_count = lax.axis_size("ctx")
    dp_index = lax.axis_index("dp").astype(jnp.int32)
    ctx_index = lax.axis_index("ctx").astype(jnp.int32)
    cap = -(-(rows * 9 // 16) // 16) * 16
    length = lengths[0]
    places = ctx_index * rows + jnp.arange(rows, dtype=jnp.int32)
    valid = (places < length)[:, None]
    index = jnp.reshape(dp_index, (1,))

    pad = jnp.zeros((w_router.shape[0], 128 - experts - 2), BF16)
    first_w = Gather(
        jnp.concatenate(
            [w_query, w_keyval, w_router, gain_attn[:, None], gain_moe[:, None], pad], 1
        )
    )
    output_g = Gather(w_output)

    seq = [tokens[0]]
    for n in range(ctx_count - 1):
        seq.append(shift(seq[-1], 1))
        if n == 0:
            first_w.near()
        elif n == 1:
            first_w.far()
        elif n == 2:
            output_g.near()
        seq[-1] = sync(seq[-1], first_w, output_g)[0]
    back = jnp.arange(ctx_count, dtype=jnp.int32)[:, None] * rows
    cosine, sine = rope_tables((places[None, :] - back).reshape(-1))

    hits = jnp.any(routes[0][..., None] == jnp.arange(SIDE, dtype=jnp.int32), 1)
    grad_y = jnp.where(valid, cotangent[0], BF16(0))
    cot = Gather(jnp.concatenate([grad_y, hits.astype(BF16)], 1))

    first_pieces = first_w.pieces()
    projected = project(index, first_pieces, seq, cosine, sine, experts, head_total)
    output_g.far()
    projected = sync(projected, output_g, cot)[0]
    queries, keyval, hn_seq, query_w, keyval_w, router_w, gains = projected

    place = jnp.stack([ctx_index, length])
    attended = attend(place, queries, keyval, groups)
    output_pieces = output_g.pieces()
    cot.near()
    attended = sync(attended, cot)[0]
    attn, tops, totals = attended
    cot.far()
    output_w, resid, hn_two, attn_low = sync(
        after_attend(index, output_pieces, attn, tokens[0], gains), cot
    )[0]

    hn_g = Gather(hn_two)
    hn_g.near()
    cot_pieces = cot.pieces()
    cot_pieces = sync(cot_pieces, hn_g)[0]
    hn_pieces = hn_g.pieces()
    sums = LineSums()
    outs, gins, slots = [], [], []
    chunks = 2 if ctx_count == 4 else 1
    for e in range(local_experts):
        number = jnp.stack([dp_index, dp_index * local_experts + e])
        out, gin, gwgu, gwd, slot, gates = run_expert(
            number, hn_pieces, cot_pieces, router_w, w_gate_up[e], w_down[e], cap, experts
        )
        outs.append(out)
        gins.append(gin)
        slots.append(slot)
        for c, v in enumerate(jnp.split(gwd, chunks, 0)):
            sums.add(("down", e, c), v)
        for c, v in enumerate(jnp.split(gwgu, 2 * chunks, 0)):
            sums.add(("up", e, c), v)
        if e + 1 < local_experts:
            hn_pieces, cot_pieces = sums.step(hn_pieces, cot_pieces)
            hn_pieces, cot_pieces = sums.step(hn_pieces, cot_pieces)
    gins, slots = sums.step(gins, slots)
    gins, slots = sums.step(gins, slots)
    half = dp_count // 2
    odd = combine(index, slots, gins, cap, range(1, dp_count, 2), lambda n, i: n)
    even = combine(index, slots, gins, cap, range(0, dp_count, 2), lambda n, i: n)
    gin_s = Scatter(even, odd)
    gin_s.core()
    gin_s.live = sums.step(gin_s.live)[0]
    gin_s.far()
    sync(gin_s)
    gin_s.near()
    gin_s.live, gates = sums.step(gin_s.live, gates)

    backed = router_back(gin_s.live, gates, router_w, gains, resid, grad_y, output_w, experts)
    grad_resid, grad_attn, grad_heads, grad_logits, part_gain_two = sums.step(*backed)
    part_output = low(dot_tn(attn_low, grad_attn))
    share_output = lax.psum_scatter(part_output, "dp", scatter_dimension=0, tiled=True)

    grad_query, grad_keys, grad_values = sums.step(
        *attend_back(
            place, queries, keyval, grad_heads, attn, tops, totals, cosine, sine, groups
        )
    )
    grad_kv = jnp.concatenate([grad_keys, grad_values], 1)
    blocks = [grad_kv[r * rows : (r + 1) * rows] for r in range(ctx_count)]
    even, odd = weight_grad(index, hn_seq, grad_query, grad_keys, grad_values)
    first_s = Scatter(even, odd)
    first_s.core()
    held = shift(blocks[-1], -1) if ctx_count > 1 else blocks[0]
    first_s.live, held = sums.step(first_s.live, held)
    first_s.far()
    for r in range(ctx_count - 2, -1, -1):
        held = add_low(held, blocks[r])
        if r:
            held = shift(held, -1)
        if r == 1:
            sync(first_s)
            first_s.near()
        if r > 0:
            first_s.live, held = sums.step(first_s.live, held)
    share_first = low(total_of(first_s.live))
    sums.add("first", share_first)
    sums.add("output", share_output)

    grad_hn_one = dot_nt(grad_query, query_w) + dot_nt(held, keyval_w)
    inputs = up(tokens[0])
    inv_one = lax.rsqrt(jnp.mean(inputs * inputs, -1, keepdims=True) + NORM_EPS)
    normed_one = inputs * inv_one
    scaled_one = grad_hn_one * gains[0:1]
    grad_inputs = grad_resid + inv_one * (
        scaled_one - normed_one * jnp.mean(scaled_one * normed_one, -1, keepdims=True)
    )
    grad_inputs = low(grad_inputs)

    part_router = dot_tn(hn_two, grad_logits)[:, :experts]
    part_gains = jnp.stack([jnp.sum(grad_hn_one * normed_one, 0), part_gain_two[0]], 1)
    part_small = jnp.concatenate([part_router, part_gains], 1)
    grad_inputs, part_small = sums.step(grad_inputs, part_small)
    share_small = lax.psum_scatter(part_small, "dp", scatter_dimension=0, tiled=True)

    out_tokens = combine(index, slots, outs, cap, range(0, dp_count, 1), lambda n, i: n ^ i)
    (out_tokens,) = sums.step(out_tokens)
    moe = lax.psum_scatter(out_tokens, "dp", scatter_dimension=0, tiled=True)
    outcome = low(jnp.where(valid, resid + up(moe), 0.0))
    sums.step()
    (share_small,) = sums.step(share_small)
    sums.add("small", share_small)

    while sums.busy():
        sums.step()
    total_small = sums.done["small"]
    total_first = up(sums.done["first"])
    down = [
        jnp.concatenate([up(sums.done["down", e, c]) for c in range(chunks)], 0)
        for e in range(local_experts)
    ]
    gate_up = [
        jnp.concatenate([up(sums.done["up", e, c]) for c in range(2 * chunks)], 0)
        for e in range(local_experts)
    ]
    return (
        outcome[None],
        grad_inputs[None],
        total_small[:, experts],
        total_small[:, experts + 1],
        total_first[:, :head_total],
        total_first[:, head_total:],
        up(sums.done["output"]),
        total_small[:, :experts],
        jnp.stack(gate_up),
        jnp.stack(down),
    )


def solution(mesh):
    in_specs = (
        P("dp", "ctx", None),
        P("dp"),
        P("dp", "ctx", None),
        P("dp", "ctx", None),
        P("dp"),
        P("dp"),
        P("dp", None),
        P("dp", None),
        P("dp", None),
        P("dp", None),
        P("dp", None, None),
        P("dp", None, None),
    )
    out_specs = (
        P("dp", "ctx", None),
        P("dp", "ctx", None),
        P("dp"),
        P("dp"),
        P("dp", None),
        P("dp", None),
        P("dp", None),
        P("dp", None),
        P("dp", None, None),
        P("dp", None, None),
    )
    return jax.shard_map(
        per_device, mesh=mesh, in_specs=in_specs, out_specs=out_specs, check_vma=False
    )
```

time: 1560 us -> 749 us (0.48)
  waiting for transfers between devices: 736 us -> 260 us
  blocking collectives: 293 us -> 0 us
  local copies, waits for them, and re-layouts: 286 us -> 53.5 us
  starting transfers between devices: 10.6 us -> 174 us
  Pallas kernels: 0 us -> 150 us
  matrix products: 128 us -> 7.71 us
    psum x1 -> x0, waiting for transfers between devices: 344 us -> none  [per_device(): lax.psum(share_query.astype(jnp.bfloat16), 'ctx').astype(jnp.float32)]
    ppermute x0 -> x97, waiting for transfers between devices: none -> 260 us  [the longest x45 156 us: send(): return lax.ppermute(v, 'ctx', pairs)]
    reduce_scatter x4 -> x2, waiting for transfers between devices: 190 us -> 0.01 us  [the longest x1 0.01 us: per_device(): lax.psum_scatter(part_output, 'dp', scatter_dimension=0, tiled=True)]
    ppermute x0 -> x97, starting transfers between devices: none -> 174 us  [the longest x45 125 us: send(): return lax.ppermute(v, 'ctx', pairs)]
    all_to_all x2 -> x0, blocking collectives: 168 us -> none  [the longest x1 84 us: per_device(): lax.all_to_all(expert_in, 'dp', split_axis=0, concat_axis=1, tiled=True)]
    pallas_call x0 -> x11, Pallas kernels: none -> 150 us  [the longest x2 74 us: run_expert(): pl.pallas_call(functools.partial(expert_kernel, counts, cap, tile, expert...]
    gather x6 -> x0, local copies, waits for them, and re-layouts: 139 us -> none  [the longest x1 45.9 us: per_device(): received = expert_out[route, slot_index].astype(jnp.float32)]
    dot_general x25 -> x4, matrix products: 128 us -> 7.71 us  [the longest x2 4.98 us: dot_tn(): lax.dot_general(a, b, (((0,), (0,)), ((), ())), preferred_element_type=F32)]
  transfers between devices with their start and end apart: 12 -> 100, of which waited for: 11 -> 39; matrix products, arithmetic and copies ran while one was open for 8% -> 14% of each run, Pallas kernels for 0% -> 13%
where the time goes in v1:
time: 749 us; the launch traced here: 739 us
  waiting for transfers between devices  260 us (35%)
  starting transfers between devices  174 us (23%)
  Pallas kernels  150 us (20%)
  other arithmetic  76.6 us (10%)
  local copies, waits for them, and re-layouts  53.5 us (7%)
  between operations  16.9 us (2%)
  matrix products  7.71 us (1%)
    ppermute x45, waiting for transfers between devices, send(): return lax.ppermute(v, 'ctx', pairs)  156 us
    ppermute x45, starting transfers between devices, send(): return lax.ppermute(v, 'ctx', pairs)  125 us
    ppermute x46, waiting for transfers between devices, swap(): return lax.ppermute(v, 'dp', [(i, i ^ mask) for i in range(count)])  81.2 us
    pallas_call x2, Pallas kernels, run_expert(): pl.pallas_call(functools.partial(expert_kernel, counts, cap, tile, expert...  74 us
    ppermute x46, starting transfers between devices, swap(): return lax.ppermute(v, 'dp', [(i, i ^ mask) for i in range(count)])  31.3 us
    convert_element_type x28, other arithmetic, merge(): return (up(v) + up(got)).astype(v.dtype)  29.9 us
    unnamed x224, local copies, waits for them, and re-layouts  25.6 us
    ppermute x6, waiting for transfers between devices, shift(): lax.ppermute(v, 'ctx', [(i, i + step) for i in range(count) if 0 <= i + s...  22.7 us
  transfers between devices with their start and end apart: 100, of which 39 were waited for; matrix products, arithmetic and copies ran while one was open for 14% of the time, Pallas kernels for 13%

profile of v1, /device:TPU:0, one launch (start us, length us, event | category | flops | bytes accessed | tf_op | source)
XLA Modules:
  0.0 739.0 jit_solution(11583918646703801443)
XLA Ops:
  16.4 4.4 collective-permute-start
  20.8 15.3 %collective-permute-done.refs_11_ = bf16[256,1536]{1,0:T(8,128)(2,1)} collective-permute-done((bf16[256,1536]{1,0:T(8,128)(2,1)S(1)}, bf16[256,1536]{1,0:T(8,128)(2,1)}, u32[]{:S(2)}, u32[]{:S(2)}) %collective-permute-start) | collective-permute-done | bytes 786464 | tf_op jit(solution)/shard_map/ppermute | solution.py:156
  39.2 4.4 collective-permute-start.3
  47.2 9.3 %collective-permute-done.4.refs_6_ = bf16[96,2688]{1,0:T(8,128)(2,1)S(1)} collective-permute-done((bf16[96,2688]{1,0:T(8,128)(2,1)}, bf16[96,2688]{1,0:T(8,128)(2,1)S(1)}, u32[]{:S(2)}, u32[]{:S(2)}) %collective-permute-start.4) | collective-permute-done | bytes 516128 | tf_op jit(solution)/shard_map/ppermute | solution.py:50
  58.8 5.0 collective-permute-start.6
  69.4 7.3 collective-permute-done.7.refs_2_
  87.2 10.7 %project.1 = (bf16[256,1536]{1,0:T(8,128)(2,1)S(1)}, bf16[1024,1024]{1,0:T(8,128)(2,1)S(1)}, bf16[1024,1536]{1,0:T(8,128)(2,1)}, bf16[1536,1536]{1,0:T(8,128)(2,...) custom-call(s32[1]{0:T(128)} %bitcast.1.index_ref.number_ref, ...), custom_call_target="tpu_custom_call" | custom-call | flops 17716740096 | bytes 34603008 | tf_op jit(solution)/shard_map/project/pallas_call | solution.py:288
  100.6 17.9 %collective-permute-done.21.refs_12_ = bf16[256,1664]{1,0:T(8,128)(2,1)S(1)} collective-permute-done((bf16[256,1664]{1,0:T(8,128)(2,1)S(1)}, bf16[256,1664]{1,0:T(8,128)(2,1)S(1)}, u32[]{:S(2)}, u32[]{:S(2)}) %collective-permute-start.21) | collective-permute-done | bytes 852000 | tf_op jit(solution)/shard_map/ppermute | solution.py:50
  119.6 12.7 %attend.1 = (f32[256,1536]{1,0:T(8,128)S(1)}, f32[4,8,256]{2,1,0:T(8,128)S(1)}, f32[4,8,256]{2,1,0:T(8,128)S(1)}) custom-call(s32[2]{0:T(128)S(1)} %pad_add_fusion.place_ref, bf16[256,1536]{1,0:T(8,128)(2,1)S(1)} %get-tuple-element.284.q_ref, bf16[1024,1024]{1,0:T(8,128)(2,1)S(1)} %get-tuple-element.285.k_ref.v_ref, ...), custom_call_target="tpu_custom_call" | custom-call | flops 16106127360 | bytes 31457280 | tf_op jit(solution)/shard_map/attend/pallas_call | solution.py:464
  133.9 3.7 after_attend.1
  149.0 17.3 %collective-permute-done.30.refs_2_ = bf16[256,1536]{1,0:T(8,128)(2,1)S(1)} collective-permute-done((bf16[256,1536]{1,0:T(8,128)(2,1)S(1)}, bf16[256,1536]{1,0:T(8,128)(2,1)S(1)}, u32[]{:S(2)}, u32[]{:S(2)}) %collective-permute-start.30) | collective-permute-done | bytes 786464 | tf_op jit(solution)/shard_map/ppermute | solution.py:50
  170.0 3.3 slice_bitcast_fusion
  174.0 3.3 collective-permute-done.35.refs_6_
  179.0 3.8 slice_bitcast_fusion.2
  184.2 37.0 %expert.2 = (bf16[1152,1536]{1,0:T(8,128)(2,1)}, bf16[1152,1664]{1,0:T(8,128)(2,1)}, bf16[1536,1024]{1,0:T(8,128)(2,1)}, bf16[512,1536]{1,0:T(8,128)(2,1)}, s32[8,256]{1,0:T(8,128)S(1)}, /*index=5*/f32[256,128]{1,0:T(8,128)}) custom-call(s32[2]{0:T(128)S(1)} %pad_add_fusion.1.number_ref, bf16[256,1536]{1,0:T(8,128)(2,1)} %copy-done.20, ...), custom_call_target="tpu_custom_call" | custom-call | flops 39862665216 | bytes 77856768 | tf_op jit(solution)/shard_map/expert/pallas_call | solution.py:720
  222.6 4.4 collective-permute-start.42
  228.4 37.0 %expert.3 = (bf16[1152,1536]{1,0:T(8,128)(2,1)}, bf16[1152,1664]{1,0:T(8,128)(2,1)}, bf16[1536,1024]{1,0:T(8,128)(2,1)}, bf16[512,1536]{1,0:T(8,128)(2,1)}, s32[...) custom-call(s32[2]{0:T(128)S(1)} %pad_add_fusion.2.number_ref, bf16[256,1536]{1,0:T(8,128)(2,1)} %copy-done.20, ...), custom_call_target="tpu_custom_call" | custom-call | flops 39862665216 | bytes 77856768 | tf_op jit(solution)/shard_map/expert/pallas_call | solution.py:720
  275.4 3.6 collective-permute-start.41
  292.3 4.9 collective-permute-done.41
  297.6 15.2 %collective-permute-done.48 = bf16[384,1024]{1,0:T(8,128)(2,1)S(1)} collective-permute-done((bf16[384,1024]{1,0:T(8,128)(2,1)S(1)}, bf16[384,1024]{1,0:T(8,128)(2,1)S(1)}, u32[]{:S(2)}, u32[]{:S(2)}) %collective-permute-start.48) | collective-permute-done | bytes 786464 | tf_op jit(solution)/shard_map/ppermute | solution.py:188
  317.3 4.4 collective-permute-start.46
  332.1 4.8 collective-permute-done.46
  342.8 5.1 collective-permute-done.52.refs_2_
  354.7 4.4 collective-permute-start.58
  361.2 20.9 %attend_back.1 = (bf16[256,1536]{1,0:T(8,128)(2,1)S(1)}, bf16[1024,512]{1,0:T(8,128)(2,1)S(1)}, bf16[1024,512]{1,0:T(8,128)(2,1)S(1)}) custom-call(s32[2]{0:T(128)S(1)} %pad_add_fusion.place_ref, bf16[256,1536]{1,0:T(8,128)(2,1)S(1)} %copy-done.47, bf16[1024,1024]{1,0:T(8,128)(2,1)S(1)} %copy-done.43, bf16[1024,1024]{1,0:T(8,128)(2,1)S(1)} %copy-done.43, ...), custom_call_target="tpu_custom_call" | custom-call | flops 25769803776 | bytes 50331648 | tf_op jit(solution)/shard_map/attend_back/pallas_call | solution.py:575
  385.9 14.7 %weight_grad.1 = (bf16[4,192,2560]{2,1,0:T(8,128)(2,1)S(1)}, bf16[4,192,2560]{2,1,0:T(8,128)(2,1)}) custom-call(s32[1]{0:T(128)} %bitcast.1.index_ref.number_ref, bf16[1024,1536]{1,0:T(8,128)(2,1)S(1)} %copy-done.39, bf16[256,1536]{1,0:T(8,128)(2,1)S(1)} %get-tuple-element.415.gq_ref, bf16[1024,512]{1,0:T(8,128)(2,1)S(1)} %get-tuple-element.416.gk_ref, ...), custom_call_target="tpu_custom_call" | custom-call | flops 17716740096 | bytes 34603008 | tf_op jit(solution)/shard_map/weight_grad/pallas_call | solution.py:811
  405.0 4.9 combine.5
  412.6 5.5 collective-permute-start.55
  420.9 4.7 convolution_convert_fusion
  430.1 11.1 %collective-permute-start.66 = (bf16[256,1536]{1,0:T(8,128)(2,1)S(1)}, bf16[256,1536]{1,0:T(8,128)(2,1)S(1)}, u32[]{:S(2)}, u32[]{:S(2)}) collective-permute-start(bf16[256,1536]{1,0:T(8,128)(2,1)S(1)} %copy-done.74), channel_id=1, source_target_pairs={{0,1},{3,2},{4,5},{7,6},{8,9},{11,10},{12,13},{15,14},{16,17},{19,... | collective-permute-start | bytes 2359304 | tf_op jit(solution)/shard_map/ppermute | solution.py:188
  448.3 6.2 collective-permute-done.66
  459.5 10.8 %collective-permute-done.64 = bf16[384,1024]{1,0:T(8,128)(2,1)S(1)} collective-permute-done((bf16[384,1024]{1,0:T(8,128)(2,1)S(1)}, bf16[384,1024]{1,0:T(8,128)(2,1)S(1)}, u32[]{:S(2)}, u32[]{:S(2)}) %collective-permute-start.64) | collective-permute-done | bytes 786464 | tf_op jit(solution)/shard_map/ppermute | solution.py:188
  474.8 6.7 collective-permute-done.69
  488.5 10.0 %collective-permute-start.78 = (bf16[384,1024]{1,0:T(8,128)(2,1)S(1)}, bf16[384,1024]{1,0:T(8,128)(2,1)S(1)}, u32[]{:S(2)}, u32[]{:S(2)}) collective-permute-start(bf16[384,1024]{1,0:T(8,128)(2,1)S(1)} %copy-done.61), channel_id=1, source_target_pairs={{0,1},{3,2},{4,5},{7,6},{8,9},{11,10},{12,13},{15,14},{16,17},{19,... | collective-permute-start | bytes 2359304 | tf_op jit(solution)/shard_map/ppermute | solution.py:188
  503.9 6.9 collective-permute-done.78
  512.9 11.4 %collective-permute-done.76 = bf16[384,1024]{1,0:T(8,128)(2,1)S(1)} collective-permute-done((bf16[384,1024]{1,0:T(8,128)(2,1)S(1)}, bf16[384,1024]{1,0:T(8,128)(2,1)S(1)}, u32[]{:S(2)}, u32[]{:S(2)}) %collective-permute-start.76) | collective-permute-done | bytes 786464 | tf_op jit(solution)/shard_map/ppermute | solution.py:188
  534.3 5.3 collective-permute-start.81
  542.4 16.4 %collective-permute-start.75 = (bf16[384,1024]{1,0:T(8,128)(2,1)}, bf16[384,1024]{1,0:T(8,128)(2,1)}, u32[]{:S(2)}, u32[]{:S(2)}) collective-permute-start(bf16[384,1024]{1,0:T(8,128)(2,1)} %get-tuple-element.440), channel_id=1, source_target_pairs={{0,1},{3,2},{4,5},{7,6},{8,9},{11,10},{12,13},{15,14},{16,17},{19,... | collective-permute-start | bytes 2359304 | tf_op jit(solution)/shard_map/ppermute | solution.py:188
  564.1 22.0 %collective-permute-done.73 = bf16[256,1536]{1,0:T(8,128)(2,1)} collective-permute-done((bf16[256,1536]{1,0:T(8,128)(2,1)}, bf16[256,1536]{1,0:T(8,128)(2,1)}, u32[]{:S(2)}, u32[]{:S(2)}) %collective-permute-start.73) | collective-permute-done | bytes 786464 | tf_op jit(solution)/shard_map/ppermute | solution.py:188
  599.8 15.6 %collective-permute-start.84 = (bf16[192,1536]{1,0:T(8,128)(2,1)}, bf16[192,1536]{1,0:T(8,128)(2,1)}, u32[]{:S(2)}, u32[]{:S(2)}) collective-permute-start(bf16[192,1536]{1,0:T(8,128)(2,1)} %reduce-scatter.8.cloned.1.call-done), channel_id=1, source_target_pairs={{0,1},{3,2},{4,5},{7,6},{8,9},{11,10},{12,13},{15,14},{16,17},{19,... | collective-permute-start | bytes 1769480 | tf_op jit(solution)/shard_map/ppermute | solution.py:188
  630.7 16.4 %collective-permute-done.85 = bf16[384,1024]{1,0:T(8,128)(2,1)S(1)} collective-permute-done((bf16[384,1024]{1,0:T(8,128)(2,1)}, bf16[384,1024]{1,0:T(8,128)(2,1)S(1)}, u32[]{:S(2)}, u32[]{:S(2)}) %collective-permute-start.85) | collective-permute-done | bytes 786464 | tf_op jit(solution)/shard_map/ppermute | solution.py:188
  647.5 9.0 %collective-permute-done.82 = bf16[384,1024]{1,0:T(8,128)(2,1)S(1)} collective-permute-done((bf16[384,1024]{1,0:T(8,128)(2,1)}, bf16[384,1024]{1,0:T(8,128)(2,1)S(1)}, u32[]{:S(2)}, u32[]{:S(2)}) %collective-permute-start.82) | collective-permute-done | bytes 786464 | tf_op jit(solution)/shard_map/ppermute | solution.py:188
  658.1 3.4 collective-permute-start.90
  668.1 15.8 %collective-permute-done.88 = bf16[384,1024]{1,0:T(8,128)(2,1)S(1)} collective-permute-done((bf16[384,1024]{1,0:T(8,128)(2,1)S(1)}, bf16[384,1024]{1,0:T(8,128)(2,1)S(1)}, u32[]{:S(2)}, u32[]{:S(2)}) %collective-permute-start.88) | collective-permute-done | bytes 786464 | tf_op jit(solution)/shard_map/ppermute | solution.py:188
  685.9 14.8 %collective-permute-done.94 = bf16[384,1024]{1,0:T(8,128)(2,1)S(1)} collective-permute-done((bf16[384,1024]{1,0:T(8,128)(2,1)S(1)}, bf16[384,1024]{1,0:T(8,128)(2,1)S(1)}, u32[]{:S(2)}, u32[]{:S(2)}) %collective-permute-start.94) | collective-permute-done | bytes 786464 | tf_op jit(solution)/shard_map/ppermute | solution.py:188
  702.8 10.5 %collective-permute-done.91 = bf16[192,1536]{1,0:T(8,128)(2,1)S(1)} collective-permute-done((bf16[192,1536]{1,0:T(8,128)(2,1)S(1)}, bf16[192,1536]{1,0:T(8,128)(2,1)S(1)}, u32[]{:S(2)}, u32[]{:S(2)}) %collective-permute-start.91) | collective-permute-done | bytes 589856 | tf_op jit(solution)/shard_map/ppermute | solution.py:188
  714.7 5.6 maximum_convert_fusion
  721.4 5.0 collective-permute-done.93
  (511 shorter events, 229.4 us)
Async XLA Ops:
  7.2 592.6 %reduce-scatter.8.cloned.1.call-start = ((), (), s32[]{:S(2)}) async-start(), calls=%async_computation.4 | async-start | bytes 5308416 | tf_op jit(solution)/shard_map/reduce_scatter | solution.py:943
  11.9 25.8 %collective-permute-start.1 = (bf16[192,2688]{1,0:T(8,128)(2,1)S(1)}, bf16[192,2688]{1,0:T(8,128)(2,1)S(1)}, u32[]{:S(2)}, u32[]{:S(2)}) collective-permute-start(bf16[192,2688]{1,0:T(8,128)(2,1)S(1)} %concatenate.46.refs_0_), channel_id=1, source_target_pairs={{0,8},{4,12},{8,0},{12,4},{16,24},{20,28},{24,16},{28,20},{1,9},{5... | collective-permute-start | bytes 3096584 | tf_op jit(solution)/shard_map/ppermute | solution.py:50
  14.9 24.3 %collective-permute-start.2 = (bf16[192,2688]{1,0:T(8,128)(2,1)S(1)}, bf16[192,2688]{1,0:T(8,128)(2,1)S(1)}, u32[]{:S(2)}, u32[]{:S(2)}) collective-permute-start(bf16[192,2688]{1,0:T(8,128)(2,1)S(1)} %concatenate.46.refs_0_), channel_id=1, source_target_pairs={{0,16},{4,20},{8,24},{12,28},{16,0},{20,4},{24,8},{28,12},{1,17},{... | collective-permute-start | bytes 3096584 | tf_op jit(solution)/shard_map/ppermute | solution.py:50
  100.0 33.9 %collective-permute-start.16 = (bf16[192,1536]{1,0:T(8,128)(2,1)S(1)}, bf16[192,1536]{1,0:T(8,128)(2,1)S(1)}, u32[]{:S(2)}, u32[]{:S(2)}) collective-permute-start(bf16[192,1536]{1,0:T(8,128)(2,1)S(1)} %copy-done.29), channel_id=1, source_target_pairs={{0,4},{4,0},{8,12},{12,8},{16,20},{20,16},{24,28},{28,24},{1,5},{5... | collective-permute-start | bytes 1769480 | tf_op jit(solution)/shard_map/ppermute | solution.py:50
  100.0 33.9 %collective-permute-start.17 = (bf16[192,1536]{1,0:T(8,128)(2,1)S(1)}, bf16[192,1536]{1,0:T(8,128)(2,1)S(1)}, u32[]{:S(2)}, u32[]{:S(2)}) collective-permute-start(bf16[192,1536]{1,0:T(8,128)(2,1)S(1)} %collective-permute-done.7.refs_2_), channel_id=1, source_target_pairs={{0,4},{4,0},{8,12},{12,8},{16,20},{20,16},{24,28},{28,24},{1,5},{5... | collective-permute-start | bytes 1769480 | tf_op jit(solution)/shard_map/ppermute | solution.py:50
  100.5 33.4 %collective-permute-start.18 = (bf16[192,1536]{1,0:T(8,128)(2,1)}, bf16[192,1536]{1,0:T(8,128)(2,1)S(1)}, u32[]{:S(2)}, u32[]{:S(2)}) collective-permute-start(bf16[192,1536]{1,0:T(8,128)(2,1)} %collective-permute-done.8.refs_4_), channel_id=1, source_target_pairs={{0,4},{4,0},{8,12},{12,8},{16,20},{20,16},{24,28},{28,24},{1,5},{5... | collective-permute-start | bytes 1769480 | tf_op jit(solution)/shard_map/ppermute | solution.py:50
  145.5 21.5 %collective-permute-start.25 = (bf16[256,1664]{1,0:T(8,128)(2,1)S(1)}, bf16[256,1664]{1,0:T(8,128)(2,1)S(1)}, u32[]{:S(2)}, u32[]{:S(2)}) collective-permute-start(bf16[256,1664]{1,0:T(8,128)(2,1)S(1)} %pad_maximum_fusion.2.refs_10_), channel_id=1, source_target_pairs={{0,4},{4,0},{8,12},{12,8},{16,20},{20,16},{24,28},{28,24},{1,5},{5... | collective-permute-start | bytes 2555912 | tf_op jit(solution)/shard_map/ppermute | solution.py:50
  145.5 21.5 %collective-permute-start.26 = (bf16[256,1664]{1,0:T(8,128)(2,1)S(1)}, bf16[256,1664]{1,0:T(8,128)(2,1)S(1)}, u32[]{:S(2)}, u32[]{:S(2)}) collective-permute-start(bf16[256,1664]{1,0:T(8,128)(2,1)S(1)} %collective-permute-done.21.refs_12_), channel_id=1, source_target_pairs={{0,4},{4,0},{8,12},{12,8},{16,20},{20,16},{24,28},{28,24},{1,5},{5... | collective-permute-start | bytes 2555912 | tf_op jit(solution)/shard_map/ppermute | solution.py:50
  222.6 45.6 %collective-permute-start.42 = (bf16[256,1536]{1,0:T(8,128)(2,1)S(1)}, bf16[256,1536]{1,0:T(8,128)(2,1)S(1)}, u32[]{:S(2)}, u32[]{:S(2)}) collective-permute-start(bf16[256,1536]{1,0:T(8,128)(2,1)S(1)} %get-tuple-element.369), channel_id=1, source_target_pairs={{0,1},{3,2},{4,5},{7,6},{8,9},{11,10},{12,13},{15,14},{16,17},{19,... | collective-permute-start | bytes 2359304 | tf_op jit(solution)/shard_map/ppermute | solution.py:188
  227.1 40.1 %collective-permute-start.39 = (bf16[256,1536]{1,0:T(8,128)(2,1)S(1)}, bf16[256,1536]{1,0:T(8,128)(2,1)S(1)}, u32[]{:S(2)}, u32[]{:S(2)}) collective-permute-start(bf16[256,1536]{1,0:T(8,128)(2,1)S(1)} %get-tuple-element.321), channel_id=1, source_target_pairs={{0,1},{3,2},{4,5},{7,6},{8,9},{11,10},{12,13},{15,14},{16,17},{19,... | collective-permute-start | bytes 2359304 | tf_op jit(solution)/shard_map/ppermute | solution.py:188
  273.3 39.7 %collective-permute-start.43 = (bf16[1024,1664]{1,0:T(8,128)(2,1)S(1)}, bf16[1024,1664]{1,0:T(8,128)(2,1)}, u32[]{:S(2)}, u32[]{:S(2)}) collective-permute-start(bf16[1024,1664]{1,0:T(8,128)(2,1)S(1)} %combine.4), channel_id=1, source_target_pairs={{0,4},{4,0},{8,12},{12,8},{16,20},{20,16},{24,28},{28,24},{1,5},{5... | collective-permute-start | bytes 10223624 | tf_op jit(solution)/shard_map/ppermute | solution.py:50
  275.4 21.8 %collective-permute-start.41 = (bf16[384,1024]{1,0:T(8,128)(2,1)}, bf16[384,1024]{1,0:T(8,128)(2,1)S(1)}, u32[]{:S(2)}, u32[]{:S(2)}) collective-permute-start(bf16[384,1024]{1,0:T(8,128)(2,1)} %get-tuple-element.368), channel_id=1, source_target_pairs={{0,1},{3,2},{4,5},{7,6},{8,9},{11,10},{12,13},{15,14},{16,17},{19,... | collective-permute-start | bytes 2359304 | tf_op jit(solution)/shard_map/ppermute | solution.py:188
  281.7 31.1 %collective-permute-start.48 = (bf16[384,1024]{1,0:T(8,128)(2,1)S(1)}, bf16[384,1024]{1,0:T(8,128)(2,1)S(1)}, u32[]{:S(2)}, u32[]{:S(2)}) collective-permute-start(bf16[384,1024]{1,0:T(8,128)(2,1)S(1)} %copy-done.71), channel_id=1, source_target_pairs={{0,1},{3,2},{4,5},{7,6},{8,9},{11,10},{12,13},{15,14},{16,17},{19,... | collective-permute-start | bytes 2359304 | tf_op jit(solution)/shard_map/ppermute | solution.py:188
  283.0 34.1 %collective-permute-start.47 = (bf16[256,1536]{1,0:T(8,128)(2,1)S(1)}, bf16[256,1536]{1,0:T(8,128)(2,1)S(1)}, u32[]{:S(2)}, u32[]{:S(2)}) collective-permute-start(bf16[256,1536]{1,0:T(8,128)(2,1)S(1)} %copy-done.81), channel_id=1, source_target_pairs={{1,2},{2,1},{5,6},{6,5},{9,10},{10,9},{13,14},{14,13},{17,18},{18,... | collective-permute-start | bytes 2359304 | tf_op jit(solution)/shard_map/ppermute | solution.py:188
  354.7 27.5 %collective-permute-start.58 = (bf16[384,1024]{1,0:T(8,128)(2,1)S(1)}, bf16[384,1024]{1,0:T(8,128)(2,1)S(1)}, u32[]{:S(2)}, u32[]{:S(2)}) collective-permute-start(bf16[384,1024]{1,0:T(8,128)(2,1)S(1)} %copy-done.62), channel_id=1, source_target_pairs={{0,1},{3,2},{4,5},{7,6},{8,9},{11,10},{12,13},{15,14},{16,17},{19,... | collective-permute-start | bytes 2359304 | tf_op jit(solution)/shard_map/ppermute | solution.py:188
  359.1 24.5 %collective-permute-start.57 = (bf16[384,1024]{1,0:T(8,128)(2,1)S(1)}, bf16[384,1024]{1,0:T(8,128)(2,1)S(1)}, u32[]{:S(2)}, u32[]{:S(2)}) collective-permute-start(bf16[384,1024]{1,0:T(8,128)(2,1)S(1)} %add_convert_fusion.21), channel_id=1, source_target_pairs={{1,2},{2,1},{5,6},{6,5},{9,10},{10,9},{13,14},{14,13},{17,18},{18,... | collective-permute-start | bytes 2359304 | tf_op jit(solution)/shard_map/ppermute | solution.py:188
  359.9 25.0 %collective-permute-start.56 = (bf16[256,1536]{1,0:T(8,128)(2,1)S(1)}, bf16[256,1536]{1,0:T(8,128)(2,1)S(1)}, u32[]{:S(2)}, u32[]{:S(2)}) collective-permute-start(bf16[256,1536]{1,0:T(8,128)(2,1)S(1)} %add_convert_fusion.22), channel_id=1, source_target_pairs={{1,0},{2,3},{5,4},{6,7},{9,8},{10,11},{13,12},{14,15},{17,16},{18,... | collective-permute-start | bytes 2359304 | tf_op jit(solution)/shard_map/ppermute | solution.py:188
  400.5 54.2 %collective-permute-start.59 = (bf16[768,2560]{1,0:T(8,128)(2,1)}, bf16[768,2560]{1,0:T(8,128)(2,1)}, u32[]{:S(2)}, u32[]{:S(2)}) collective-permute-start(bf16[768,2560]{1,0:T(8,128)(2,1)} %bitcast.13), channel_id=1, source_target_pairs={{0,4},{4,0},{8,12},{12,8},{16,20},{20,16},{24,28},{28,24},{1,5},{5... | collective-permute-start | bytes 11796488 | tf_op jit(solution)/shard_map/ppermute | solution.py:50
  412.6 33.1 %collective-permute-start.55 = (bf16[256,1536]{1,0:T(8,128)(2,1)}, bf16[256,1536]{1,0:T(8,128)(2,1)}, u32[]{:S(2)}, u32[]{:S(2)}) collective-permute-start(bf16[256,1536]{1,0:T(8,128)(2,1)} %get-tuple-element.403), channel_id=1, source_target_pairs={{0,1},{3,2},{4,5},{7,6},{8,9},{11,10},{12,13},{15,14},{16,17},{19,... | collective-permute-start | bytes 2359304 | tf_op jit(solution)/shard_map/ppermute | solution.py:188
  419.6 23.0 %collective-permute-start.53 = (bf16[384,1024]{1,0:T(8,128)(2,1)}, bf16[384,1024]{1,0:T(8,128)(2,1)}, u32[]{:S(2)}, u32[]{:S(2)}) collective-permute-start(bf16[384,1024]{1,0:T(8,128)(2,1)} %add_convert_fusion.24), channel_id=1, source_target_pairs={{1,0},{2,3},{5,4},{6,7},{9,8},{10,11},{13,12},{14,15},{17,16},{18,... | collective-permute-start | bytes 2359304 | tf_op jit(solution)/shard_map/ppermute | solution.py:188
  425.7 195.1 %reduce-scatter.10.cloned.1.call-start = ((), (), s32[]{:S(2)}) async-start(), calls=%async_computation.5 | async-start | bytes 884736
  428.6 26.0 %collective-permute-start.60 = (bf16[256,1024]{1,0:T(8,128)(2,1)S(1)}, bf16[256,1024]{1,0:T(8,128)(2,1)S(1)}, u32[]{:S(2)}, u32[]{:S(2)}) collective-permute-start(bf16[256,1024]{1,0:T(8,128)(2,1)S(1)} %slice.209), channel_id=1, source_target_pairs={{1,0},{2,1},{3,2},{5,4},{6,5},{7,6},{9,8},{10,9},{11,10},{13,12},{... | collective-permute-start | bytes 1572872 | tf_op jit(solution)/shard_map/ppermute | solution.py:156
  430.1 24.4 %collective-permute-start.66 = (bf16[256,1536]{1,0:T(8,128)(2,1)S(1)}, bf16[256,1536]{1,0:T(8,128)(2,1)S(1)}, u32[]{:S(2)}, u32[]{:S(2)}) collective-permute-start(bf16[256,1536]{1,0:T(8,128)(2,1)S(1)} %copy-done.74), channel_id=1, source_target_pairs={{0,1},{3,2},{4,5},{7,6},{8,9},{11,10},{12,13},{15,14},{16,17},{19,... | collective-permute-start | bytes 2359304 | tf_op jit(solution)/shard_map/ppermute | solution.py:188
  445.6 24.6 %collective-permute-start.64 = (bf16[384,1024]{1,0:T(8,128)(2,1)S(1)}, bf16[384,1024]{1,0:T(8,128)(2,1)S(1)}, u32[]{:S(2)}, u32[]{:S(2)}) collective-permute-start(bf16[384,1024]{1,0:T(8,128)(2,1)S(1)} %copy-done.65), channel_id=1, source_target_pairs={{1,0},{2,3},{5,4},{6,7},{9,8},{10,11},{13,12},{14,15},{17,16},{18,... | collective-permute-start | bytes 2359304 | tf_op jit(solution)/shard_map/ppermute | solution.py:188
  454.9 26.6 %collective-permute-start.69 = (bf16[256,1024]{1,0:T(8,128)(2,1)S(1)}, bf16[256,1024]{1,0:T(8,128)(2,1)S(1)}, u32[]{:S(2)}, u32[]{:S(2)}) collective-permute-start(bf16[256,1024]{1,0:T(8,128)(2,1)S(1)} %add_convert_fusion.33), channel_id=1, source_target_pairs={{1,0},{2,1},{3,2},{5,4},{6,5},{7,6},{9,8},{10,9},{11,10},{13,12},{... | collective-permute-start | bytes 1572872 | tf_op jit(solution)/shard_map/ppermute | solution.py:156
  471.3 28.3 %collective-permute-start.63 = (bf16[384,1024]{1,0:T(8,128)(2,1)S(1)}, bf16[384,1024]{1,0:T(8,128)(2,1)S(1)}, u32[]{:S(2)}, u32[]{:S(2)}) collective-permute-start(bf16[384,1024]{1,0:T(8,128)(2,1)S(1)} %copy-done.63), channel_id=1, source_target_pairs={{0,1},{3,2},{4,5},{7,6},{8,9},{11,10},{12,13},{15,14},{16,17},{19,... | collective-permute-start | bytes 2359304 | tf_op jit(solution)/shard_map/ppermute | solution.py:188
  473.5 28.6 %collective-permute-start.61 = (bf16[384,1024]{1,0:T(8,128)(2,1)S(1)}, bf16[384,1024]{1,0:T(8,128)(2,1)S(1)}, u32[]{:S(2)}, u32[]{:S(2)}) collective-permute-start(bf16[384,1024]{1,0:T(8,128)(2,1)S(1)} %add_convert_fusion.20), channel_id=1, source_target_pairs={{1,0},{2,3},{5,4},{6,7},{9,8},{10,11},{13,12},{14,15},{17,16},{18,... | collective-permute-start | bytes 2359304 | tf_op jit(solution)/shard_map/ppermute | solution.py:188
  481.7 44.7 %collective-permute-start.72 = (bf16[256,1024]{1,0:T(8,128)(2,1)S(1)}, bf16[256,1024]{1,0:T(8,128)(2,1)S(1)}, u32[]{:S(2)}, u32[]{:S(2)}) collective-permute-start(bf16[256,1024]{1,0:T(8,128)(2,1)S(1)} %add_convert_fusion.32), channel_id=1, source_target_pairs={{1,0},{2,1},{3,2},{5,4},{6,5},{7,6},{9,8},{10,9},{11,10},{13,12},{... | collective-permute-start | bytes 1572872 | tf_op jit(solution)/shard_map/ppermute | solution.py:156
  485.3 41.1 %collective-permute-start.71 = (bf16[192,2560]{1,0:T(8,128)(2,1)S(1)}, bf16[192,2560]{1,0:T(8,128)(2,1)S(1)}, u32[]{:S(2)}, u32[]{:S(2)}) collective-permute-start(bf16[192,2560]{1,0:T(8,128)(2,1)S(1)} %pad_maximum_fusion.1), channel_id=1, source_target_pairs={{0,16},{4,20},{8,24},{12,28},{16,0},{20,4},{24,8},{28,12},{1,17},{... | collective-permute-start | bytes 2949128 | tf_op jit(solution)/shard_map/ppermute | solution.py:50
  488.5 22.3 %collective-permute-start.78 = (bf16[384,1024]{1,0:T(8,128)(2,1)S(1)}, bf16[384,1024]{1,0:T(8,128)(2,1)S(1)}, u32[]{:S(2)}, u32[]{:S(2)}) collective-permute-start(bf16[384,1024]{1,0:T(8,128)(2,1)S(1)} %copy-done.61), channel_id=1, source_target_pairs={{0,1},{3,2},{4,5},{7,6},{8,9},{11,10},{12,13},{15,14},{16,17},{19,... | collective-permute-start | bytes 2359304 | tf_op jit(solution)/shard_map/ppermute | solution.py:188
  499.6 24.7 %collective-permute-start.76 = (bf16[384,1024]{1,0:T(8,128)(2,1)S(1)}, bf16[384,1024]{1,0:T(8,128)(2,1)S(1)}, u32[]{:S(2)}, u32[]{:S(2)}) collective-permute-start(bf16[384,1024]{1,0:T(8,128)(2,1)S(1)} %add_convert_fusion.14), channel_id=1, source_target_pairs={{1,0},{2,3},{5,4},{6,7},{9,8},{10,11},{13,12},{14,15},{17,16},{18,... | collective-permute-start | bytes 2359304 | tf_op jit(solution)/shard_map/ppermute | solution.py:188
  502.2 23.1 %collective-permute-start.77 = (bf16[256,1536]{1,0:T(8,128)(2,1)S(1)}, bf16[256,1536]{1,0:T(8,128)(2,1)S(1)}, u32[]{:S(2)}, u32[]{:S(2)}) collective-permute-start(bf16[256,1536]{1,0:T(8,128)(2,1)S(1)} %add_convert_fusion.13), channel_id=1, source_target_pairs={{1,2},{2,1},{5,6},{6,5},{9,10},{10,9},{13,14},{14,13},{17,18},{18,... | collective-permute-start | bytes 2359304 | tf_op jit(solution)/shard_map/ppermute | solution.py:188
  534.3 58.5 %collective-permute-start.81 = (bf16[384,1024]{1,0:T(8,128)(2,1)S(1)}, bf16[384,1024]{1,0:T(8,128)(2,1)}, u32[]{:S(2)}, u32[]{:S(2)}) collective-permute-start(bf16[384,1024]{1,0:T(8,128)(2,1)S(1)} %copy-done.60), channel_id=1, source_target_pairs={{0,1},{3,2},{4,5},{7,6},{8,9},{11,10},{12,13},{15,14},{16,17},{19,... | collective-permute-start | bytes 2359304 | tf_op jit(solution)/shard_map/ppermute | solution.py:188
  539.5 55.6 %collective-permute-start.80 = (bf16[384,1024]{1,0:T(8,128)(2,1)}, bf16[384,1024]{1,0:T(8,128)(2,1)}, u32[]{:S(2)}, u32[]{:S(2)}) collective-permute-start(bf16[384,1024]{1,0:T(8,128)(2,1)} %add_convert_fusion.9), channel_id=1, source_target_pairs={{1,2},{2,1},{5,6},{6,5},{9,10},{10,9},{13,14},{14,13},{17,18},{18,... | collective-permute-start | bytes 2359304 | tf_op jit(solution)/shard_map/ppermute | solution.py:188
  541.1 56.6 %collective-permute-start.79 = (bf16[256,1536]{1,0:T(8,128)(2,1)}, bf16[256,1536]{1,0:T(8,128)(2,1)}, u32[]{:S(2)}, u32[]{:S(2)}) collective-permute-start(bf16[256,1536]{1,0:T(8,128)(2,1)} %add_convert_fusion.10), channel_id=1, source_target_pairs={{1,0},{2,3},{5,4},{6,7},{9,8},{10,11},{13,12},{14,15},{17,16},{18,... | collective-permute-start | bytes 2359304 | tf_op jit(solution)/shard_map/ppermute | solution.py:188
  542.4 46.6 %collective-permute-start.75 = (bf16[384,1024]{1,0:T(8,128)(2,1)}, bf16[384,1024]{1,0:T(8,128)(2,1)}, u32[]{:S(2)}, u32[]{:S(2)}) collective-permute-start(bf16[384,1024]{1,0:T(8,128)(2,1)} %get-tuple-element.440), channel_id=1, source_target_pairs={{0,1},{3,2},{4,5},{7,6},{8,9},{11,10},{12,13},{15,14},{16,17},{19,... | collective-permute-start | bytes 2359304 | tf_op jit(solution)/shard_map/ppermute | solution.py:188
  558.7 27.4 %collective-permute-start.73 = (bf16[256,1536]{1,0:T(8,128)(2,1)}, bf16[256,1536]{1,0:T(8,128)(2,1)}, u32[]{:S(2)}, u32[]{:S(2)}) collective-permute-start(bf16[256,1536]{1,0:T(8,128)(2,1)} %add_convert_fusion.16), channel_id=1, source_target_pairs={{1,0},{2,3},{5,4},{6,7},{9,8},{10,11},{13,12},{14,15},{17,16},{18,... | collective-permute-start | bytes 2359304 | tf_op jit(solution)/shard_map/ppermute | solution.py:188
  561.2 168.6 %reduce-scatter.6.cloned.1.call-start = ((), (), s32[]{:S(2)}) async-start(), calls=%async_computation.3 | async-start | bytes 7077888 | tf_op jit(solution)/shard_map/reduce_scatter | solution.py:989
  599.8 26.7 %collective-permute-start.84 = (bf16[192,1536]{1,0:T(8,128)(2,1)}, bf16[192,1536]{1,0:T(8,128)(2,1)}, u32[]{:S(2)}, u32[]{:S(2)}) collective-permute-start(bf16[192,1536]{1,0:T(8,128)(2,1)} %reduce-scatter.8.cloned.1.call-done), channel_id=1, source_target_pairs={{0,1},{3,2},{4,5},{7,6},{8,9},{11,10},{12,13},{15,14},{16,17},{19,... | collective-permute-start | bytes 1769480 | tf_op jit(solution)/shard_map/ppermute | solution.py:188
  621.7 34.9 %collective-permute-start.87 = (bf16[192,2560]{1,0:T(8,128)(2,1)}, bf16[192,2560]{1,0:T(8,128)(2,1)S(1)}, u32[]{:S(2)}, u32[]{:S(2)}) collective-permute-start(bf16[192,2560]{1,0:T(8,128)(2,1)} %add_convert_fusion.2), channel_id=1, source_target_pairs={{0,1},{3,2},{4,5},{7,6},{8,9},{11,10},{12,13},{15,14},{16,17},{19,... | collective-permute-start | bytes 2949128 | tf_op jit(solution)/shard_map/ppermute | solution.py:188
  624.5 22.6 %collective-permute-start.85 = (bf16[384,1024]{1,0:T(8,128)(2,1)}, bf16[384,1024]{1,0:T(8,128)(2,1)S(1)}, u32[]{:S(2)}, u32[]{:S(2)}) collective-permute-start(bf16[384,1024]{1,0:T(8,128)(2,1)} %add_convert_fusion.12), channel_id=1, source_target_pairs={{1,0},{2,3},{5,4},{6,7},{9,8},{10,11},{13,12},{14,15},{17,16},{18,... | collective-permute-start | bytes 2359304 | tf_op jit(solution)/shard_map/ppermute | solution.py:188
  625.8 21.4 %collective-permute-start.83 = (bf16[384,1024]{1,0:T(8,128)(2,1)}, bf16[384,1024]{1,0:T(8,128)(2,1)S(1)}, u32[]{:S(2)}, u32[]{:S(2)}) collective-permute-start(bf16[384,1024]{1,0:T(8,128)(2,1)} %add_convert_fusion.7), channel_id=1, source_target_pairs={{1,2},{2,1},{5,6},{6,5},{9,10},{10,9},{13,14},{14,13},{17,18},{18,... | collective-permute-start | bytes 2359304 | tf_op jit(solution)/shard_map/ppermute | solution.py:188
  626.5 30.0 %collective-permute-start.82 = (bf16[384,1024]{1,0:T(8,128)(2,1)}, bf16[384,1024]{1,0:T(8,128)(2,1)S(1)}, u32[]{:S(2)}, u32[]{:S(2)}) collective-permute-start(bf16[384,1024]{1,0:T(8,128)(2,1)} %add_convert_fusion.8), channel_id=1, source_target_pairs={{1,0},{2,3},{5,4},{6,7},{9,8},{10,11},{13,12},{14,15},{17,16},{18,... | collective-permute-start | bytes 2359304 | tf_op jit(solution)/shard_map/ppermute | solution.py:188
  661.5 22.4 %collective-permute-start.88 = (bf16[384,1024]{1,0:T(8,128)(2,1)S(1)}, bf16[384,1024]{1,0:T(8,128)(2,1)S(1)}, u32[]{:S(2)}, u32[]{:S(2)}) collective-permute-start(bf16[384,1024]{1,0:T(8,128)(2,1)S(1)} %add_convert_fusion.6), channel_id=1, source_target_pairs={{1,0},{2,3},{5,4},{6,7},{9,8},{10,11},{13,12},{14,15},{17,16},{18,... | collective-permute-start | bytes 2359304 | tf_op jit(solution)/shard_map/ppermute | solution.py:188
  665.9 34.9 %collective-permute-start.95 = (bf16[192,2560]{1,0:T(8,128)(2,1)S(1)}, bf16[192,2560]{1,0:T(8,128)(2,1)S(1)}, u32[]{:S(2)}, u32[]{:S(2)}) collective-permute-start(bf16[192,2560]{1,0:T(8,128)(2,1)S(1)} %add_convert_fusion.1), channel_id=1, source_target_pairs={{1,2},{2,1},{5,6},{6,5},{9,10},{10,9},{13,14},{14,13},{17,18},{18,... | collective-permute-start | bytes 2949128 | tf_op jit(solution)/shard_map/ppermute | solution.py:188
  666.6 34.1 %collective-permute-start.94 = (bf16[384,1024]{1,0:T(8,128)(2,1)S(1)}, bf16[384,1024]{1,0:T(8,128)(2,1)S(1)}, u32[]{:S(2)}, u32[]{:S(2)}) collective-permute-start(bf16[384,1024]{1,0:T(8,128)(2,1)S(1)} %add_convert_fusion.5), channel_id=1, source_target_pairs={{1,0},{2,3},{5,4},{6,7},{9,8},{10,11},{13,12},{14,15},{17,16},{18,... | collective-permute-start | bytes 2359304 | tf_op jit(solution)/shard_map/ppermute | solution.py:188
  684.6 28.7 %collective-permute-start.91 = (bf16[192,1536]{1,0:T(8,128)(2,1)S(1)}, bf16[192,1536]{1,0:T(8,128)(2,1)S(1)}, u32[]{:S(2)}, u32[]{:S(2)}) collective-permute-start(bf16[192,1536]{1,0:T(8,128)(2,1)S(1)} %add_convert_fusion.29), channel_id=1, source_target_pairs={{1,0},{2,3},{5,4},{6,7},{9,8},{10,11},{13,12},{14,15},{17,16},{18,... | collective-permute-start | bytes 1769480 | tf_op jit(solution)/shard_map/ppermute | solution.py:188
  701.1 26.5 %collective-permute-start.96 = (bf16[192,2560]{1,0:T(8,128)(2,1)S(1)}, bf16[192,2560]{1,0:T(8,128)(2,1)S(1)}, u32[]{:S(2)}, u32[]{:S(2)}) collective-permute-start(bf16[192,2560]{1,0:T(8,128)(2,1)S(1)} %add_convert_fusion), channel_id=1, source_target_pairs={{1,0},{2,3},{5,4},{6,7},{9,8},{10,11},{13,12},{14,15},{17,16},{18,... | collective-permute-start | bytes 2949128 | tf_op jit(solution)/shard_map/ppermute | solution.py:188
  (162 other events, 1976.8 us)
Sparse Core Ops, SparseCore 0:
  425.8 57.1 reduce-scatter.7
  561.3 37.8 reduce-scatter.9
  603.0 61.7 reduce-scatter.5

commit v2 on v1

v2 whole, which is shorter than its diff:
```python
import functools

import jax
import jax.numpy as jnp
from jax import lax
from jax.experimental import pallas as pl
from jax.experimental.pallas import tpu as pltpu
from jax.sharding import PartitionSpec as P

HD = 64
NORM_EPS = 1e-06
ROPE_BASE = 10000.0
MASK_FLOOR = -1e30
F32 = jnp.float32
BF16 = jnp.bfloat16
MIB = 1024 * 1024
SIDE = 128
WHOLE = pl.BlockSpec()


def params(mib):
    return pltpu.CompilerParams(vmem_limit_bytes=mib * MIB)


def hbm(*arrays_in):
    return [pltpu.with_memory_space_constraint(v, pltpu.HBM) for v in arrays_in]


def cost(flops):
    return pl.CostEstimate(flops=int(flops) // 64, bytes_accessed=1024, transcendentals=0)


def up(v):
    return v.astype(F32)


def low(v):
    return v.astype(BF16)


def dot_nn(a, b):
    return lax.dot_general(a, b, (((1,), (0,)), ((), ())), preferred_element_type=F32)


def dot_nt(a, b):
    return lax.dot_general(a, b, (((1,), (1,)), ((), ())), preferred_element_type=F32)


def dot_tn(a, b):
    return lax.dot_general(a, b, (((0,), (0,)), ((), ())), preferred_element_type=F32)


def swap(v, mask):
    count = lax.axis_size("dp")
    return lax.ppermute(v, "dp", [(i, i ^ mask) for i in range(count)])


def halves(v):
    mid = v.shape[0] // 2
    return [v[:mid], v[mid:]]


class Gather:
    def __init__(self, v):
        self.special = lax.axis_size("dp") == 8
        self.stage = 0
        self.live = [v]

    def near(self):
        if self.special and self.stage == 0:
            v = self.live[0]
            self.live = [v, swap(v, 2), swap(v, 4)]
        self.stage = max(self.stage, 1)

    def far(self):
        self.near()
        if self.special and self.stage == 1:
            v, along_x, along_y = self.live
            self.live = self.live + [swap(halves(along_x)[0], 4), swap(halves(along_y)[1], 2)]
        self.stage = max(self.stage, 2)

    def pieces(self):
        self.far()
        if not self.special:
            out = [[self.live[0]]]
            bit = 1
            while bit < lax.axis_size("dp"):
                out = out + [[swap(h, bit) for h in piece] for piece in out]
                bit *= 2
            return out
        v, along_x, along_y, far_a, far_b = self.live
        even = [[v], [along_x], [along_y], [far_a, far_b]]
        out = []
        for piece in even:
            out += [piece, [swap(h, 1) for h in piece]]
        return out


def sync(*items):
    plain = [i.live if isinstance(i, Gather) else i for i in items]
    plain = lax.optimization_barrier(plain)
    for item, got in zip(items, plain):
        if isinstance(item, Gather):
            item.live = list(got)
    return plain


def add_low(a, b):
    return low(up(a) + up(b))


def shift(v, step):
    count = lax.axis_size("ctx")
    return lax.ppermute(
        v, "ctx", [(i, i + step) for i in range(count) if 0 <= i + step < count]
    )


class LineSums:
    DEPTH = 1

    def __init__(self):
        count = lax.axis_size("ctx")
        index = lax.axis_index("ctx")
        self.plain = count != 4
        self.outer = (index == 0) | (index == count - 1)
        self.waiting = []
        self.flights = [[] for _ in range(self.DEPTH)]
        self.done = {}

    def add(self, name, v):
        if self.plain:
            self.done[name] = lax.psum(v, "ctx")
        else:
            self.waiting.append((name, v))

    def busy(self):
        return bool(self.waiting or any(self.flights))

    def step(self, *critical, take=1, flush=False):
        if self.plain:
            return critical
        got = self.flights.pop(0)
        while flush and self.flights:
            got = got + self.flights.pop(0)
        ready = {"first": [], "inner": [], "last": []}
        for kind, name, v, arrived in got:
            if kind == "first":
                ready["inner"].append((name, add_low(v, arrived)))
            elif kind == "inner":
                ready["last"].append((name, add_low(v, arrived)))
            else:
                self.done[name] = (v, arrived)
        for _ in range(take):
            if self.waiting:
                ready["first"].append(self.waiting.pop(0))
        shared = []
        for first in list(ready["first"]):
            for last in list(ready["last"]):
                if first[1].shape == last[1].shape:
                    shared.append((first[0], last[0], first[1], jnp.where(self.outer, first[1], last[1])))
                    ready["first"] = [r for r in ready["first"] if r is not first]
                    ready["last"] = [r for r in ready["last"] if r is not last]
                    break
        both = [(own, payload) for _, _, own, payload in shared]
        alone = {kind: [v for _, v in entries] for kind, entries in ready.items()}
        held = lax.optimization_barrier((both, alone, self.done, critical))
        both, alone, self.done, critical = held
        flight = []
        for (first, last, _, _), (own, payload) in zip(shared, both):
            back = lax.ppermute(payload, "ctx", [(0, 1), (1, 0), (2, 3), (3, 2)])
            flight.append(("first", first, own, back))
            flight.append(("last", last, payload, back))
        routes = {
            "first": [(0, 1), (3, 2)],
            "inner": [(1, 2), (2, 1)],
            "last": [(1, 0), (2, 3)],
        }
        for kind, pairs in routes.items():
            for (name, _), v in zip(ready[kind], alone[kind]):
                flight.append((kind, name, v, lax.ppermute(v, "ctx", pairs)))
        self.flights.append(flight)
        return critical

    def total(self, name):
        if self.plain:
            return up(self.done[name])
        v, arrived = self.done[name]
        return up(jnp.where(self.outer, arrived, v))


def lay_rows(pieces, counts, index, put):
    n = 0
    for k, parts in enumerate(counts):
        rows = sum(pieces[n + i].shape[0] for i in range(parts))
        start = (index ^ k) * rows
        for i in range(parts):
            put(pl.multiple_of(start, 16), pieces[n + i])
            start = start + pieces[n + i].shape[0]
        n += parts


def turn(v, cosine, sine):
    lane = lax.broadcasted_iota(jnp.int32, v.shape, 1)
    first = lax.rem(lane, HD) < HD // 2
    partner = jnp.where(
        first, pltpu.roll(v, 2 * HD - HD // 2, 1), pltpu.roll(v, HD // 2, 1)
    )
    return v * cosine + partner * sine


def normed_rows(parts, gain):
    x = jnp.concatenate([up(p[...]) for p in parts], 0)
    return low(x * lax.rsqrt(jnp.mean(x * x, -1, keepdims=True) + NORM_EPS) * gain)


def key_rows(hn, wkv_ref, cosine, sine):
    raw = dot_nn(hn, wkv_ref[...])
    two = 2 * HD
    keys = raw.shape[1] // 2
    turned = [turn(raw[:, d : d + two], cosine, sine) for d in range(0, keys, two)]
    return low(jnp.concatenate(turned + [raw[:, keys:]], 1))


def project_kernel(counts, blocks, experts, index_ref, *refs):
    pieces = refs[: sum(counts)]
    seq = refs[sum(counts) : sum(counts) + 2 * blocks]
    cos_ref, sin_ref = refs[sum(counts) + 2 * blocks : sum(counts) + 2 * blocks + 2]
    q_ref, kv_ref, hn_ref, wq_ref, wkv_ref, router_ref, gains_ref, small_ref = refs[
        sum(counts) + 2 * blocks + 2 :
    ]
    q_width, kv_width = wq_ref.shape[1], wkv_ref.shape[1]

    def put(start, ref):
        at = pl.ds(start, ref.shape[0])
        wq_ref[at, :] = ref[:, :q_width]
        wkv_ref[at, :] = ref[:, q_width : q_width + kv_width]
        small_ref[at, :] = ref[:, q_width + kv_width :]

    lay_rows(pieces, counts, index_ref[0], put)
    small = up(small_ref[...])
    lane = lax.broadcasted_iota(jnp.int32, small.shape, 1)
    router_ref[...] = low(jnp.where(lane < experts, small, 0.0))
    gains_ref[...] = jnp.transpose(small)[experts : experts + 8]
    gain = gains_ref[0:1, :]
    rows = 2 * seq[0].shape[0]
    for r in range(blocks):
        at = slice(r * rows, (r + 1) * rows)
        hn = normed_rows(seq[2 * r : 2 * r + 2], gain)
        hn_ref[at, :] = hn
        kv_ref[at, :] = key_rows(hn, wkv_ref, cos_ref[at, :], sin_ref[at, :])
    two = 2 * HD
    for c in range(0, q_width, 2 * two):
        raw = dot_nn(hn_ref[:rows, :], wq_ref[:, c : c + 2 * two])
        for d in (0, two):
            rot = turn(raw[:, d : d + two], cos_ref[:rows, :], sin_ref[:rows, :])
            q_ref[:, c + d : c + d + two] = low(up(low(rot)) * (HD ** (-0.5)))


def project(index, pieces, seq, cosine, sine, experts, q_width):
    counts = [len(p) for p in pieces]
    flat = [h for p in pieces for h in p]
    halves_in = [h for pair in seq[:-1] for h in pair]
    rows, width = 2 * seq[0][0].shape[0], seq[0][0].shape[1]
    kv_width = flat[0].shape[1] - q_width - 128
    keys = rows * len(seq)
    return pl.pallas_call(
        functools.partial(project_kernel, counts, len(seq) - 1, experts),
        in_specs=[pl.BlockSpec(memory_space=pltpu.SMEM)] + [WHOLE] * (len(flat) + len(halves_in) + 2),
        out_specs=[WHOLE] * 7,
        out_shape=[
            jax.ShapeDtypeStruct((rows, q_width), BF16),
            jax.ShapeDtypeStruct((keys, kv_width), BF16),
            jax.ShapeDtypeStruct((keys, width), BF16),
            jax.ShapeDtypeStruct((width, q_width), BF16),
            jax.ShapeDtypeStruct((width, kv_width), BF16),
            jax.ShapeDtypeStruct((width, 128), BF16),
            jax.ShapeDtypeStruct((8, width), F32),
        ],
        scratch_shapes=[pltpu.VMEM((width, 128), BF16)],
        compiler_params=params(40),
        cost_estimate=cost(8 * width * (rows * q_width + keys * kv_width)),
        name="project",
    )(index, *flat, *halves_in, cosine, sine)


def project_last_kernel(
    a_ref, b_ref, gains_ref, wkv_ref, cos_ref, sin_ref, kv_in, hn_in, kv_out, hn_out, kv_ref, hn_ref, sems
):
    rows = kv_ref.shape[0]
    start = kv_out.shape[0] - rows
    hn = normed_rows((a_ref, b_ref), gains_ref[0:1, :])
    hn_ref[...] = hn
    hn_copy = pltpu.make_async_copy(hn_ref, hn_out.at[start : start + rows], sems.at[0])
    hn_copy.start()
    at = slice(start, start + rows)
    kv_ref[...] = key_rows(hn, wkv_ref, cos_ref[at, :], sin_ref[at, :])
    kv_copy = pltpu.make_async_copy(kv_ref, kv_out.at[start : start + rows], sems.at[1])
    kv_copy.start()
    hn_copy.wait()
    kv_copy.wait()


def project_last(last, gains, wkv, cosine, sine, keyval, hn):
    rows = 2 * last[0].shape[0]
    anywhere = pl.BlockSpec(memory_space=pl.ANY)
    return pl.pallas_call(
        project_last_kernel,
        in_specs=[WHOLE] * 6 + [anywhere] * 2,
        out_specs=[anywhere] * 2,
        out_shape=[
            jax.ShapeDtypeStruct(keyval.shape, BF16),
            jax.ShapeDtypeStruct(hn.shape, BF16),
        ],
        scratch_shapes=[
            pltpu.VMEM((rows, keyval.shape[1]), BF16),
            pltpu.VMEM((rows, hn.shape[1]), BF16),
            pltpu.SemaphoreType.DMA((2,)),
        ],
        input_output_aliases={6: 0, 7: 1},
        compiler_params=params(24),
        cost_estimate=cost(8 * rows * keyval.shape[1] * hn.shape[1]),
        name="project_last",
    )(*last, gains, wkv, cosine, sine, *hbm(keyval, hn))


def router_back_kernel(
    experts,
    total_ref,
    gates_ref,
    router_ref,
    gains_ref,
    resid_ref,
    cot_ref,
    wo_ref,
    hn_ref,
    attn_ref,
    grad_ref,
    heads_ref,
    part_ref,
    held_ref,
    sems,
):
    width = resid_ref.shape[1]
    total = up(total_ref[...])
    side = total[:, width:]
    lane = lax.broadcasted_iota(jnp.int32, side.shape, 1)
    gate_grads = jnp.where(lane < experts, side + pltpu.roll(side, SIDE // 2, 1), 0.0)
    gates = gates_ref[...]
    mean = jnp.sum(gates * gate_grads, -1, keepdims=True)
    grad_logits = low(gates * (gate_grads - mean))
    grad_hn = total[:, :width] + dot_nt(grad_logits, router_ref[...])
    resid = resid_ref[...]
    inv = lax.rsqrt(jnp.mean(resid * resid, -1, keepdims=True) + NORM_EPS)
    normed = resid * inv
    gain = jnp.sum(grad_hn * normed, 0, keepdims=True)
    scaled = grad_hn * gains_ref[1:2, :]
    grad = up(cot_ref[...]) + inv * (scaled - normed * jnp.mean(scaled * normed, -1, keepdims=True))
    grad_ref[...] = grad
    grad_low = low(grad)
    heads_ref[...] = dot_nt(grad_low, wo_ref[...])
    copies = []

    def put(cols, value):
        held_ref[:, cols] = low(value)
        copies.append(
            pltpu.make_async_copy(held_ref.at[:, cols], part_ref.at[:, cols], sems.at[len(copies)])
        )
        copies[-1].start()

    small = dot_tn(hn_ref[:, :width], grad_logits)
    lane = lax.broadcasted_iota(jnp.int32, small.shape, 1)
    gain = jnp.transpose(jnp.broadcast_to(gain, (SIDE, width)))
    put(slice(width, width + SIDE), jnp.where(lane == experts, gain, small))
    attn_t = low(transposed(attn_ref[...]))
    for c in range(0, width, 256):
        put(slice(c, c + 256), dot_nn(attn_t, grad_low[:, c : c + 256]))
    for copy in copies:
        copy.wait()


def router_back(total, gates, router, gains, resid, cot, wo, hn, attn, experts):
    rows, width = resid.shape
    heads = wo.shape[0]
    return pl.pallas_call(
        functools.partial(router_back_kernel, experts),
        in_specs=[WHOLE] * 9,
        out_specs=[WHOLE, WHOLE, pl.BlockSpec(memory_space=pl.ANY)],
        out_shape=[
            pltpu.HBM((rows, width), F32),
            pltpu.HBM((rows, heads), F32),
            pltpu.HBM((heads, width + SIDE), BF16),
        ],
        scratch_shapes=[
            pltpu.VMEM((heads, width + SIDE), BF16),
            pltpu.SemaphoreType.DMA((width // 256 + 1,)),
        ],
        compiler_params=params(36),
        cost_estimate=cost(14 * rows * heads * width),
        name="router_back",
    )(*hbm(total, gates, router), gains, *hbm(resid, cot, wo, hn, attn))


def transposed(v):
    return jnp.transpose(up(v))


def key_bias(place_ref, keys, rows):
    j = lax.broadcasted_iota(jnp.int32, (keys, rows), 0)
    i = lax.broadcasted_iota(jnp.int32, (keys, rows), 1)
    block = lax.div(j, rows)
    place = (place_ref[0] - block) * rows + (j - block * rows)
    allowed = (place >= 0) & (place <= place_ref[0] * rows + i) & (place < place_ref[1])
    return jnp.where(allowed, 0.0, MASK_FLOOR)


def widened(part, group):
    zero = jnp.zeros_like(part)
    return jnp.concatenate([part, zero] if group == 0 else [zero, part], 0)


def attend_kernel(
    groups,
    place_ref,
    q_ref,
    k_ref,
    v_ref,
    tok_ref,
    gains_ref,
    router_ref,
    named_ref,
    wo_all_ref,
    out_ref,
    max_ref,
    total_ref,
    resid_ref,
    hn_ref,
    low_ref,
    gates_ref,
    bias_ref,
    wo_ref,
    sem,
):
    rows = q_ref.shape[0]
    keys = k_ref.shape[0]
    width = tok_ref.shape[1]
    step = pl.program_id(0)
    load = pltpu.make_async_copy(wo_all_ref, wo_ref, sem)

    @pl.when(step == 0)
    def _():
        load.start()
        bias_ref[...] = key_bias(place_ref, keys, rows)

    q_t = low(transposed(q_ref[...]))
    v_t = low(transposed(v_ref[...]))
    outs, maxes, totals = [], [], []
    for group in range(2):
        parts = [
            widened(q_t[(group * groups + h) * HD : (group * groups + h + 1) * HD], group)
            for h in range(groups)
        ]
        scores = dot_nn(k_ref[...], jnp.concatenate(parts, 1))
        weights = []
        for h in range(groups):
            s = scores[:, h * rows : (h + 1) * rows] + bias_ref[...]
            top = jnp.max(s, 0, keepdims=True)
            w = jnp.exp(s - top)
            totals.append(jnp.sum(w, 0, keepdims=True))
            maxes.append(top)
            weights.append(low(w))
        mixed = dot_nn(v_t, jnp.concatenate(weights, 1))
        for h in range(groups):
            part = mixed[group * HD : (group + 1) * HD, h * rows : (h + 1) * rows]
            outs.append(part / totals[group * groups + h])
    attn = jnp.transpose(jnp.concatenate(outs, 0))
    out_ref[...] = attn
    heads = 2 * groups * HD
    low_ref[:, pl.ds(pl.multiple_of(step * heads, 2 * HD), heads)] = low(attn)
    pad = [jnp.ones((8 - 2 * groups, rows), F32)] if 2 * groups < 8 else []
    max_ref[0] = jnp.concatenate(maxes + pad, 0)
    total_ref[0] = jnp.concatenate(totals + pad, 0)

    @pl.when(step == pl.num_programs(0) - 1)
    def _():
        load.wait()
        resid = up(tok_ref[...]) + dot_nn(low_ref[...], wo_ref[...])
        resid_ref[...] = resid
        inv = lax.rsqrt(jnp.mean(resid * resid, -1, keepdims=True) + NORM_EPS)
        hn = low(resid * inv * gains_ref[1:2, :])
        hn_ref[:, :width] = hn
        named = up(named_ref[...]) > 0.5
        logits = jnp.where(named, dot_nn(hn, router_ref[...]), MASK_FLOOR)
        gates = jnp.where(named, jnp.exp(logits - jnp.max(logits, -1, keepdims=True)), 0.0)
        gates = gates / jnp.sum(gates, -1, keepdims=True)
        gates_ref[...] = gates
        high = up(low(gates))
        hn_ref[:, width:] = low(high + pltpu.roll(gates - high, SIDE // 2, 1))


def attend(place, queries, keyval, tokens, gains, router, named, wo, groups):
    rows, heads_all = queries.shape
    width = tokens.shape[1]
    keys, kv = keyval.shape
    steps = kv // 2 // (2 * HD)
    heads = 2 * groups * HD

    def same(*shape):
        return pl.BlockSpec(shape, lambda i, s: (0,) * len(shape))

    return pl.pallas_call(
        functools.partial(attend_kernel, groups),
        grid_spec=pltpu.PrefetchScalarGridSpec(
            num_scalar_prefetch=1,
            grid=(steps,),
            in_specs=[
                pl.BlockSpec((rows, heads), lambda i, s: (0, i)),
                pl.BlockSpec((keys, 2 * HD), lambda i, s: (0, i)),
                pl.BlockSpec((keys, 2 * HD), lambda i, s: (0, steps + i)),
                same(rows, width),
                same(8, width),
                same(width, SIDE),
                same(rows, SIDE),
                pl.BlockSpec(memory_space=pl.ANY),
            ],
            out_specs=[
                pl.BlockSpec((rows, heads), lambda i, s: (0, i)),
                pl.BlockSpec((1, 8, rows), lambda i, s: (i, 0, 0)),
                pl.BlockSpec((1, 8, rows), lambda i, s: (i, 0, 0)),
                same(rows, width),
                same(rows, width + SIDE),
                same(rows, heads_all),
                same(rows, SIDE),
            ],
            scratch_shapes=[
                pltpu.VMEM((keys, rows), F32),
                pltpu.VMEM((heads_all, width), BF16),
                pltpu.SemaphoreType.DMA,
            ],
        ),
        out_shape=[
            pltpu.HBM((rows, heads_all), F32),
            jax.ShapeDtypeStruct((steps, 8, rows), F32),
            jax.ShapeDtypeStruct((steps, 8, rows), F32),
            pltpu.HBM((rows, width), F32),
            jax.ShapeDtypeStruct((rows, width + SIDE), BF16),
            pltpu.HBM((rows, heads_all), BF16),
            jax.ShapeDtypeStruct((rows, SIDE), F32),
        ],
        compiler_params=params(40),
        cost_estimate=cost(50 * rows * keys * heads_all),
        name="attend",
    )(place, *hbm(queries, keyval, keyval, tokens), gains, router, named, *hbm(wo))


def attend_back_kernel(
    groups,
    place_ref,
    q_ref,
    k_ref,
    v_ref,
    grad_ref,
    out_ref,
    max_ref,
    total_ref,
    cos_ref,
    sin_ref,
    hn_ref,
    gq_ref,
    gk_ref,
    gv_ref,
    part_ref,
    bias_ref,
    held_ref,
    hn_t_ref,
    sems,
):
    rows = q_ref.shape[0]
    keys = k_ref.shape[0]
    chunk = 256

    @pl.when(pl.program_id(0) == 0)
    def _():
        bias_ref[...] = key_bias(place_ref, keys, rows)
        for start in range(0, keys, rows):
            hn_t_ref[:, start : start + rows] = low(transposed(hn_ref[start : start + rows, :]))

    q_t = low(transposed(q_ref[...]))
    k_t = low(transposed(k_ref[...]))
    grad_t = transposed(grad_ref[...])
    out_t = transposed(out_ref[...])
    q_parts, g_parts, deltas, tops, grads = [], [], [], [], []
    for group in range(2):
        q_part, g_part, delta = [], [], []
        for h in range(groups):
            n = group * groups + h
            total = total_ref[0, n : n + 1]
            grad = grad_t[n * HD : (n + 1) * HD]
            q_part.append(widened(q_t[n * HD : (n + 1) * HD], group))
            g_part.append(widened(low(grad / total), group))
            delta.append(jnp.sum(out_t[n * HD : (n + 1) * HD] * grad, 0, keepdims=True) / total)
        q_parts.append(jnp.concatenate(q_part, 1))
        g_parts.append(jnp.concatenate(g_part, 1))
        deltas.append(jnp.concatenate(delta, 1))
        tops.append(
            jnp.concatenate(
                [max_ref[0, group * groups + h : group * groups + h + 1] for h in range(groups)], 1
            )
        )
        grads.append(jnp.zeros((2 * HD, groups * rows), F32))
    for start in range(0, keys, chunk):
        bias = bias_ref[start : start + chunk]
        bias = jnp.concatenate([bias] * groups, 1)
        grad_k = jnp.zeros((chunk, 2 * HD), F32)
        grad_v = jnp.zeros((chunk, 2 * HD), F32)
        for group in range(2):
            scores = dot_nn(k_ref[start : start + chunk], q_parts[group])
            w = jnp.exp(scores + bias - tops[group])
            gp = dot_nn(v_ref[start : start + chunk], g_parts[group])
            gs = low(w * (gp - deltas[group]))
            grad_v = grad_v + dot_nt(low(w), g_parts[group])
            grad_k = grad_k + dot_nt(gs, q_parts[group])
            grads[group] = grads[group] + dot_nn(k_t[:, start : start + chunk], gs)
        at = slice(start, start + chunk)
        gk_ref[at] = low(turn(grad_k, cos_ref[at, :], -sin_ref[at, :]))
        gv_ref[at] = low(grad_v)
    step, slot = pl.program_id(0), lax.rem(pl.program_id(0), 2)
    steps = part_ref.shape[1] // held_ref.shape[2]
    heads, two = 2 * groups * HD, 2 * HD

    def copies(n, slot):
        spans = ((0, heads), (steps * heads, two), (steps * (heads + two), two))
        out, col = [], 0
        for i, (first, size) in enumerate(spans):
            dst = pl.ds(pl.multiple_of(first + n * size, two), size)
            src = held_ref.at[slot, :, col : col + size]
            out.append(pltpu.make_async_copy(src, part_ref.at[:, dst], sems.at[slot, i]))
            col += size
        return out

    @pl.when(step >= 2)
    def _():
        for copy in copies(step - 2, slot):
            copy.wait()

    both = jnp.concatenate([gk_ref[...], gv_ref[...]], 1)
    held_ref[slot, :, heads:] = low(dot_nn(hn_t_ref[...], both))
    parts = []
    for group in range(2):
        for h in range(groups):
            parts.append(grads[group][group * HD : (group + 1) * HD, h * rows : (h + 1) * rows])
    grad_q = jnp.transpose(jnp.concatenate(parts, 0)) * (HD ** (-0.5))
    for d in range(0, 2 * groups * HD, 2 * HD):
        gq_ref[:, d : d + 2 * HD] = low(
            turn(grad_q[:, d : d + 2 * HD], cos_ref[:rows, :], -sin_ref[:rows, :])
        )
    held_ref[slot, :, :heads] = low(dot_nn(hn_t_ref[:, :rows], gq_ref[...]))
    for copy in copies(step, slot):
        copy.start()

    @pl.when(step == steps - 1)
    def _():
        for copy in copies(step, slot):
            copy.wait()

    @pl.when((step == steps - 1) & (step >= 1))
    def _():
        for copy in copies(step - 1, 1 - slot):
            copy.wait()


def attend_back(place, queries, keyval, grad_heads, attn, tops, totals, cosine, sine, hn, groups):
    rows, width = queries.shape
    keys, kv = keyval.shape
    steps = kv // 2 // (2 * HD)
    heads = 2 * groups * HD
    model = hn.shape[1]
    head_spec = pl.BlockSpec((rows, heads), lambda i, s: (0, i))
    key_spec = pl.BlockSpec((keys, 2 * HD), lambda i, s: (0, i))
    stat_spec = pl.BlockSpec((1, 8, rows), lambda i, s: (i, 0, 0))
    return pl.pallas_call(
        functools.partial(attend_back_kernel, groups),
        grid_spec=pltpu.PrefetchScalarGridSpec(
            num_scalar_prefetch=1,
            grid=(steps,),
            in_specs=[
                head_spec,
                key_spec,
                pl.BlockSpec((keys, 2 * HD), lambda i, s: (0, steps + i)),
                head_spec,
                head_spec,
                stat_spec,
                stat_spec,
                pl.BlockSpec((keys, 2 * HD), lambda i, s: (0, 0)),
                pl.BlockSpec((keys, 2 * HD), lambda i, s: (0, 0)),
                pl.BlockSpec((keys, model), lambda i, s: (0, 0)),
            ],
            out_specs=[
                head_spec,
                key_spec,
                key_spec,
                pl.BlockSpec(memory_space=pl.ANY),
            ],
            scratch_shapes=[
                pltpu.VMEM((keys, rows), F32),
                pltpu.VMEM((2, model, heads + 4 * HD), BF16),
                pltpu.VMEM((model, keys), BF16),
                pltpu.SemaphoreType.DMA((2, 3)),
            ],
        ),
        out_shape=[
            jax.ShapeDtypeStruct((rows, width), BF16),
            jax.ShapeDtypeStruct((keys, kv // 2), BF16),
            jax.ShapeDtypeStruct((keys, kv // 2), BF16),
            pltpu.HBM((model, width + kv), BF16),
        ],
        compiler_params=params(44),
        cost_estimate=cost(64 * rows * keys * width),
        name="attend_back",
    )(place, *hbm(queries, keyval, keyval, grad_heads, attn, tops, totals, cosine, sine, hn))


def slot_pick(slot, cap):
    place = lax.broadcasted_iota(jnp.int32, (cap, slot.shape[1]), 0).astype(F32)
    return place == slot


def weight_chunks(grads, x_ref, c_ref, ggu_ref, act_ref):
    hidden, width = act_ref.shape[1], c_ref.shape[1]
    size, wide = grads[0].shape
    rest = width - wide
    half = hidden // 2
    for h in range(2):
        at = slice(h * half, (h + 1) * half)
        part = low(dot_tn(act_ref[:, at], c_ref[...]))
        grads[0][at, :] = part[:, :wide]
        grads[0][hidden:, h * rest : (h + 1) * rest] = part[:, wide:]
    step = size // 2
    for c, ref in enumerate(grads[1:]):
        for h in range(2):
            cols = slice(c * size + h * step, c * size + (h + 1) * step)
            ref[h * step : (h + 1) * step, :] = low(dot_tn(x_ref[:, cols], ggu_ref[...]))


def expert_kernel(counts, cap, tile, e, earlier, last, number_ref, *refs):
    parts, refs = refs[: sum(counts)], refs[sum(counts) :]
    cot_ref, wgu_all_ref, wd_all_ref = refs[:3]
    gin_before, refs = refs[3 : 3 + earlier], refs[3 + earlier :]
    out_ref, slots_ref, result_ref = refs[:3]
    grads = refs[3:6]
    x_ref, c_ref, ggu_ref, act_ref, sg_ref, wgu_ref, wd_ref, sems = refs[6:14]
    if last:
        gin_ref, load_ref, store_ref = refs[14:]
    else:
        gin_ref = result_ref
    loads = [
        pltpu.make_async_copy(wgu_all_ref.at[e], wgu_ref, sems.at[0]),
        pltpu.make_async_copy(wd_all_ref.at[e], wd_ref, sems.at[1]),
    ]
    for load in loads:
        load.start()
    blocks = len(counts)
    hidden, width = wd_ref.shape
    rows = cot_ref.shape[0] // blocks
    total = blocks * cap
    index, expert = number_ref[0], number_ref[1]
    lane = lax.broadcasted_iota(jnp.int32, (8, SIDE), 1)
    pick_slot = low(jnp.where(lane == expert, 1.0, 0.0))
    pick_gate = low(jnp.where((lane == expert) | (lane == expert + SIDE // 2), 1.0, 0.0))
    n = 0
    for b in range(blocks):
        hn = parts[n : n + counts[b]]
        n += counts[b]
        src = pl.ds(pl.multiple_of((index ^ b) * rows, rows), rows)
        slot = dot_nt(pick_slot, cot_ref[src, width:])[:1] - 1.0
        gate = [dot_nt(pick_gate, part[:, width:]) for part in hn]
        gate = (jnp.concatenate(gate, 1) if len(gate) > 1 else gate[0])[:1]
        slots_ref[b : b + 1, :] = slot
        hit = slot_pick(slot, cap)
        pick = low(jnp.where(hit, 1.0, 0.0))
        at = slice(b * cap, (b + 1) * cap)
        taken, start = None, 0
        for part in hn:
            piece = dot_nn(pick[:, start : start + part.shape[0]], part[:, :width])
            taken = piece if taken is None else taken + piece
            start += part.shape[0]
        x_ref[at, :] = low(taken)
        c_ref[at, :] = low(dot_nn(pick, cot_ref[src, :width]))
        gate = jnp.sum(jnp.where(hit, gate, 0.0), 1, keepdims=True)
        sg_ref[at, :] = jnp.broadcast_to(gate, (cap, 128))

    def middle(t, carry):
        at = pl.ds(pl.multiple_of(t * tile, 16), tile)
        gate_up = dot_nn(x_ref[at, :], wgu_ref[...])
        g = gate_up[:, :hidden]
        u = gate_up[:, hidden:]
        sigma = jax.nn.sigmoid(g)
        silu = g * sigma
        act = low(silu * u)
        slot_gate = sg_ref[at, :][:, :1]
        back = dot_nt(c_ref[at, :], wd_ref[...])
        gate_grad = jnp.sum(up(act) * back, 1, keepdims=True)
        back = back * slot_gate
        act_ref[at, :] = low(up(act) * slot_gate)
        ggu_ref[at, :hidden] = low(back * u * (sigma * (1.0 + g * (1.0 - sigma))))
        ggu_ref[at, hidden:] = low(back * silu)
        out_ref[at, :] = low(dot_nn(act, wd_ref[...]) * slot_gate)
        gin_ref[at, :width] = low(dot_nt(ggu_ref[at, :], wgu_ref[...]))
        lane = lax.broadcasted_iota(jnp.int32, (tile, SIDE), 1)
        high = up(low(gate_grad))
        side = jnp.where(lane == expert, high, 0.0)
        side = jnp.where(lane == expert + SIDE // 2, gate_grad - high, side)
        gin_ref[at, width:] = low(side)
        return carry

    for load in loads:
        load.wait()
    lax.fori_loop(0, total // tile, middle, 0)
    if not last:
        weight_chunks(grads, x_ref, c_ref, ggu_ref, act_ref)
        return

    def load_before(b):
        return [
            pltpu.make_async_copy(
                ref.at[b * cap : (b + 1) * cap], load_ref.at[b % 2, i], sems.at[2 + 2 * i + b % 2]
            )
            for i, ref in enumerate(gin_before)
        ]

    def store(b):
        dst = pl.ds(pl.multiple_of((index ^ b) * rows, rows), rows)
        return pltpu.make_async_copy(
            store_ref.at[b % 2], result_ref.at[dst], sems.at[2 + 2 * earlier + b % 2]
        )

    for load in load_before(0):
        load.start()
    for b in range(blocks):
        if b + 1 < blocks:
            for load in load_before(b + 1):
                load.start()
        src = pl.ds(pl.multiple_of((index ^ b) * rows, rows), rows)
        order = up(cot_ref[src, width:])
        lane = lax.broadcasted_iota(jnp.int32, order.shape, 1)
        place = lax.broadcasted_iota(jnp.int32, (rows, cap), 1).astype(F32)

        def pick(number):
            slot = jnp.sum(jnp.where(lane == number, order, 0.0), 1, keepdims=True) - 1.0
            return low(jnp.where(place == slot, 1.0, 0.0))

        acc = dot_nn(pick(expert), gin_ref[b * cap : (b + 1) * cap, :])
        for i, load in enumerate(load_before(b)):
            load.wait()
            acc = acc + dot_nn(pick(expert - earlier + i), load_ref[b % 2, i])
        if b >= 2:
            store(b - 2).wait()
        store_ref[b % 2] = low(acc)
        store(b).start()
    weight_chunks(grads, x_ref, c_ref, ggu_ref, act_ref)
    for b in range(max(blocks - 2, 0), blocks):
        store(b).wait()


def unpack_down(chunk, hidden):
    rest = chunk.shape[1] // 2
    right = jnp.concatenate([chunk[hidden:, :rest], chunk[hidden:, rest:]], 0)
    return jnp.concatenate([chunk[:hidden], right], 1)


def run_expert(number, pieces, cot, w_gate_up, w_down, e, cap, gins):
    counts = [len(p) for p in pieces]
    flat = [h for p in pieces for h in p]
    blocks = len(counts)
    rows = cot.shape[0] // blocks
    hidden, width = w_down.shape[1:]
    total = blocks * cap
    tile = max(t for t in range(16, 401, 16) if total % t == 0)
    last = e + 1 == w_down.shape[0]
    earlier = len(gins) if last else 0
    anywhere = pl.BlockSpec(memory_space=pl.ANY)
    chunk = jax.ShapeDtypeStruct((width // 2, 2 * hidden), BF16)
    work = [(total, width), (total, width), (total, 2 * hidden), (total, hidden)]
    gin_shape = (total, width + SIDE)
    scratch = [pltpu.VMEM(shape, BF16) for shape in work] + [
        pltpu.VMEM((total, 128), F32),
        pltpu.VMEM((width, 2 * hidden), BF16),
        pltpu.VMEM((hidden, width), BF16),
        pltpu.SemaphoreType.DMA((4 + 2 * earlier,)),
    ]
    if last:
        scratch += [
            pltpu.VMEM(gin_shape, BF16),
            pltpu.VMEM((2, max(earlier, 1), cap, width + SIDE), BF16),
            pltpu.VMEM((2, rows, width + SIDE), BF16),
        ]
    result = pltpu.HBM((blocks * rows, width + SIDE) if last else gin_shape, BF16)
    got = pl.pallas_call(
        functools.partial(expert_kernel, counts, cap, tile, e, earlier, last),
        in_specs=[pl.BlockSpec(memory_space=pltpu.SMEM)]
        + [WHOLE] * (len(flat) + 1)
        + [anywhere] * (2 + earlier),
        out_specs=[WHOLE, WHOLE, anywhere if last else WHOLE] + [WHOLE] * 3,
        out_shape=[
            pltpu.HBM((total, width), BF16),
            jax.ShapeDtypeStruct((blocks, rows), F32),
            result,
        ]
        + [chunk] * 3,
        scratch_shapes=scratch,
        compiler_params=params(56),
        cost_estimate=cost(44 * total * width * hidden),
        name="expert",
    )(number, *flat, cot, w_gate_up, w_down, *gins[:earlier])
    return got[0], got[1], got[2], got[3:]


def combine_kernel(count, cap, first, stride, number_ref, *refs):
    slots, parts, out_ref = refs[:count], refs[count : 2 * count], refs[2 * count]
    b = pl.program_id(0) * stride + first
    rows = slots[0].shape[1]
    place = lax.broadcasted_iota(jnp.int32, (cap, rows), 0).astype(F32)
    acc = None
    for e in range(count):
        pick = low(jnp.where(place == slots[e][pl.ds(b, 1), :], 1.0, 0.0))
        part = dot_tn(pick, parts[e][...])
        acc = part if acc is None else acc + part
    out_ref[...] = low(acc)


def combine(number, slots, parts, cap, chosen, order):
    blocks, rows = slots[0].shape
    count = len(parts)
    width = parts[0].shape[1]
    first, stride = chosen.start, chosen.step
    return pl.pallas_call(
        functools.partial(combine_kernel, count, cap, first, stride),
        grid_spec=pltpu.PrefetchScalarGridSpec(
            num_scalar_prefetch=1,
            grid=(len(chosen),),
            in_specs=[pl.BlockSpec((blocks, rows), lambda n, s: (0, 0))] * count
            + [pl.BlockSpec((cap, width), lambda n, s: (n * stride + first, 0))] * count,
            out_specs=pl.BlockSpec((rows, width), lambda n, s: (order(n, s[0]), 0)),
        ),
        out_shape=pltpu.HBM((len(chosen) * rows, width), BF16),
        compiler_params=params(20),
        cost_estimate=cost(10 * len(chosen) * cap * rows * width),
        name="combine",
    )(number, *slots, *parts)


def rope_tables(places):
    half = HD // 2
    frequency = ROPE_BASE ** (-jnp.arange(half, dtype=F32) * 2.0 / HD)
    angles = places.astype(F32)[:, None] * frequency[None, :]
    cosine, sine = jnp.cos(angles), jnp.sin(angles)
    return jnp.concatenate([cosine] * 4, 1), jnp.concatenate([-sine, sine] * 2, 1)


def per_device(
    tokens,
    lengths,
    routes,
    cotangent,
    gain_attn,
    gain_moe,
    w_query,
    w_keyval,
    w_output,
    w_router,
    w_gate_up,
    w_down,
):
    rows = tokens.shape[1]
    width = tokens.shape[2]
    experts = w_router.shape[1]
    local_experts = w_gate_up.shape[0]
    kv_width = w_keyval.shape[1] // 2
    head_total = w_query.shape[1]
    groups = head_total // kv_width
    dp_count = lax.axis_size("dp")
    ctx_count = lax.axis_size("ctx")
    dp_index = lax.axis_index("dp").astype(jnp.int32)
    ctx_index = lax.axis_index("ctx").astype(jnp.int32)
    cap = -(-(rows * 9 // 16) // 16) * 16
    length = lengths[0]
    places = ctx_index * rows + jnp.arange(rows, dtype=jnp.int32)
    valid = (places < length)[:, None]
    index = jnp.reshape(dp_index, (1,))

    pad = jnp.zeros((w_router.shape[0], 128 - experts - 2), BF16)
    first_w = Gather(
        jnp.concatenate(
            [w_query, w_keyval, w_router, gain_attn[:, None], gain_moe[:, None], pad], 1
        )
    )

    named = jnp.any(routes[0][..., None] == jnp.arange(SIDE, dtype=jnp.int32), 1).astype(BF16)
    order = dot_nn(jnp.tril(jnp.ones((rows, rows), BF16)), named) * up(named)
    grad_y = jnp.where(valid, cotangent[0], BF16(0))
    cot = jnp.concatenate([grad_y, low(order)], 1)

    seq = [halves(tokens[0])]
    back = jnp.arange(ctx_count, dtype=jnp.int32)[:, None] * rows
    tables = rope_tables((places[None, :] - back).reshape(-1))

    def next_block(part):
        return shift(seq[-1][part], 1)

    first_w.near()
    seq.append([next_block(0), next_block(1)])
    early = next_block(0)
    output_w = lax.all_gather(w_output, "dp", axis=0, tiled=True)
    _, tables, cot, seq[1], early = sync(first_w, tables, cot, seq[1], early)
    cot_all = lax.all_gather(cot, "dp", axis=0, tiled=True)
    first_w.far()
    seq.append([early, next_block(1)])
    early = next_block(0)
    _, seq[2], early = sync(first_w, seq[2], early)
    seq.append([early, next_block(1)])
    for _ in range(ctx_count - 4):
        seq.append([next_block(0), next_block(1)])
    cosine, sine = tables
    projected = project(index, first_w.pieces(), seq, cosine, sine, experts, head_total)
    queries, keyval, hn_seq, query_w, keyval_w, router_w, gains = projected
    keyval, hn_seq = project_last(seq[-1], gains, keyval_w, cosine, sine, keyval, hn_seq)

    place = jnp.stack([ctx_index, length])
    attn, tops, totals, resid, hn_two, attn_low, gates = attend(
        place, queries, keyval, tokens[0], gains, router_w, named, output_w, groups
    )

    hn_g = Gather(hn_two)
    hn_g.near()
    sync(hn_g)
    hn_pieces = hn_g.pieces()
    sums = LineSums()
    outs, gins, slots = [], [], []
    for e in range(local_experts):
        number = jnp.stack([dp_index, dp_index * local_experts + e])
        out, slot, gin, grads = run_expert(
            number, hn_pieces, cot_all, w_gate_up, w_down, e, cap, gins
        )
        outs.append(out)
        gins.append(gin)
        slots.append(slot)
        if e + 1 < local_experts:
            for c, v in enumerate(grads):
                sums.add(f"{e}.{c}", v)
            hn_pieces, cot_all = sums.step(hn_pieces, cot_all)
    for c, v in enumerate(grads):
        sums.add(f"{local_experts - 1}.{c}", v)
    (gin_tokens,) = sums.step(gins[-1])
    gin_sum = lax.psum_scatter(gin_tokens, "dp", scatter_dimension=0, tiled=True)
    outs, slots = sums.step(outs, slots)
    out_tokens = combine(index, slots, outs, cap, range(0, dp_count, 1), lambda n, i: n ^ i)
    gin_sum, out_tokens = sums.step(gin_sum, out_tokens)

    grad_resid, grad_heads, part_output = router_back(
        gin_sum, gates, router_w, gains, resid, grad_y, output_w, hn_two, attn_low, experts
    )

    backed = attend_back(
        place, queries, keyval, grad_heads, attn, tops, totals, cosine, sine, hn_seq, groups
    )
    backed = sums.step(*backed, part_output)
    grad_query, grad_keys, grad_values, part_first, part_output = backed
    share_first = lax.psum_scatter(part_first, "dp", scatter_dimension=0, tiled=True)
    (part_output,) = sums.step(part_output)
    share_output = lax.psum_scatter(part_output, "dp", scatter_dimension=0, tiled=True)
    share_query, share_keyval = share_first[:, :head_total], share_first[:, head_total:]
    gain_grad = jnp.sum(up(share_query) * up(w_query), 1, keepdims=True) + jnp.sum(
        up(share_keyval) * up(w_keyval), 1, keepdims=True
    )
    gain_grad = jnp.broadcast_to(gain_grad / up(gain_attn)[:, None], (w_query.shape[0], SIDE))
    share_keyval = jnp.concatenate([share_keyval, low(gain_grad)], 1)
    sums.add("query", share_query)
    sums.add("keyval", share_keyval)
    sums.step(take=2)
    sums.add("output", share_output)
    grad_kv = jnp.concatenate([grad_keys, grad_values], 1)
    blocks = [grad_kv[r * rows : (r + 1) * rows] for r in range(ctx_count)]
    held = blocks[-1]
    for r in range(ctx_count - 2, -1, -1):
        pairs = [(i, i - 1) for i in range(r + 1, ctx_count)]
        held = add_low(lax.ppermute(held, "ctx", pairs), blocks[r])
        if r:
            held, out_tokens = sums.step(held, out_tokens)
    moe = lax.psum_scatter(out_tokens, "dp", scatter_dimension=0, tiled=True)

    grad_hn_one = dot_nt(grad_query, query_w) + dot_nt(held, keyval_w)
    inputs = up(tokens[0])
    inv_one = lax.rsqrt(jnp.mean(inputs * inputs, -1, keepdims=True) + NORM_EPS)
    normed_one = inputs * inv_one
    scaled_one = grad_hn_one * gains[0:1]
    grad_inputs = grad_resid + inv_one * (
        scaled_one - normed_one * jnp.mean(scaled_one * normed_one, -1, keepdims=True)
    )
    grad_inputs = low(grad_inputs)

    outcome = low(jnp.where(valid, resid + up(moe), 0.0))

    wanted = [f"{e}.{c}" for e in range(local_experts) for c in range(3)]
    while not all(name in sums.done for name in wanted):
        sums.step(take=2)
    gate_up, down = jnp.zeros(w_gate_up.shape, F32), []
    for e in range(local_experts):
        chunks = [sums.total(f"{e}.{c}") for c in range(3)]
        for c, part in enumerate(chunks[1:]):
            gate_up = lax.dynamic_update_slice(gate_up, part[None], (e, c * part.shape[0], 0))
        down.append(unpack_down(chunks[0], w_down.shape[1]))
    down = jnp.stack(down)
    gate_up, down, grad_inputs = sums.step(gate_up, down, grad_inputs)
    if "query" not in sums.done:
        sums.step()
    total_query, total_keyval = sums.total("query"), sums.total("keyval")
    ready = (total_query, total_keyval[:, : 2 * kv_width], total_keyval[:, 2 * kv_width])
    total_query, total_keyval, total_gain = sums.step(*ready)
    while sums.busy():
        sums.step()
    total_output = sums.total("output")
    return (
        outcome[None],
        grad_inputs[None],
        total_gain,
        total_output[:, width + experts],
        total_query,
        total_keyval,
        total_output[:, :width],
        total_output[:, width : width + experts],
        gate_up,
        down,
    )


def solution(mesh):
    in_specs = (
        P("dp", "ctx", None),
        P("dp"),
        P("dp", "ctx", None),
        P("dp", "ctx", None),
        P("dp"),
        P("dp"),
        P("dp", None),
        P("dp", None),
        P("dp", None),
        P("dp", None),
        P("dp", None, None),
        P("dp", None, None),
    )
    out_specs = (
        P("dp", "ctx", None),
        P("dp", "ctx", None),
        P("dp"),
        P("dp"),
        P("dp", None),
        P("dp", None),
        P("dp", None),
        P("dp", None),
        P("dp", None, None),
        P("dp", None, None),
    )
    return jax.shard_map(
        per_device, mesh=mesh, in_specs=in_specs, out_specs=out_specs, check_vma=False
    )
```

time: 749 us -> 621 us (0.83)
  starting transfers between devices: 174 us -> 101 us
  waiting for transfers between devices: 260 us -> 236 us
  local copies, waits for them, and re-layouts: 53.5 us -> 40.7 us
  other arithmetic: 76.6 us -> 64.7 us
    ppermute x45 -> x26, starting transfers between devices: 125 us -> 63.6 us  [the longest x19 48.7 us: step(): flight.append((kind, name, v, lax.ppermute(v, 'ctx', pairs)))]
    ppermute x46 -> x18, waiting for transfers between devices: 81.2 us -> 39 us  [swap(): return lax.ppermute(v, 'dp', [(i, i ^ mask) for i in range(count)])]
    convert_element_type x29 -> x1, other arithmetic: 29.9 us -> 0.64 us  [per_device(): jnp.any(routes[0][..., None] == jnp.arange(SIDE, dtype=jnp.int32), 1)]
    ppermute x46 -> x18, starting transfers between devices: 31.3 us -> 12 us  [swap(): return lax.ppermute(v, 'dp', [(i, i ^ mask) for i in range(count)])]
    reduce_scatter x1, waiting for transfers between devices: 0.01 us -> 15 us  [per_device(): lax.psum_scatter(part_output, 'dp', scatter_dimension=0, tiled=True)]
    convert_element_type x10 -> x18, other arithmetic: 14.5 us -> 27.5 us  [low(): return v.astype(BF16)]
    pallas_call x6 -> x5, Pallas kernels: 106 us -> 94.5 us  [the longest x2 68.9 us: run_expert(): pl.pallas_call(functools.partial(expert_kernel, counts, cap, tile, e, ear...]
    pallas_call x1, Pallas kernels: 20.9 us -> 30.2 us  [attend_back(): pl.pallas_call(functools.partial(attend_back_kernel, groups), grid_spec=p...]
  transfers between devices with their start and end apart: 100 -> 56, of which waited for: 39 -> 25; matrix products, arithmetic and copies ran while one was open for 14% -> 12% of each run, Pallas kernels for 13% -> 20%
where the time goes in v2:
time: 621 us; the launch traced here: 611 us
  waiting for transfers between devices  236 us (38%)
  Pallas kernels  148 us (24%)
  starting transfers between devices  101 us (16%)
  other arithmetic  64.7 us (10%)
  local copies, waits for them, and re-layouts  40.7 us (7%)
  between operations  16.3 us (3%)
    ppermute x4, waiting for transfers between devices, step(): back = lax.ppermute(payload, 'ctx', [(0, 1), (1, 0), (2, 3), (3, 2)])  85.6 us
    ppermute x19, waiting for transfers between devices, step(): flight.append((kind, name, v, lax.ppermute(v, 'ctx', pairs)))  76.8 us
    pallas_call x2, Pallas kernels, run_expert(): pl.pallas_call(functools.partial(expert_kernel, counts, cap, tile, e, ear...  68.9 us
    ppermute x19, starting transfers between devices, step(): flight.append((kind, name, v, lax.ppermute(v, 'ctx', pairs)))  48.7 us
    ppermute x18, waiting for transfers between devices, swap(): return lax.ppermute(v, 'dp', [(i, i ^ mask) for i in range(count)])  39 us
    pallas_call x1, Pallas kernels, attend_back(): pl.pallas_call(functools.partial(attend_back_kernel, groups), grid_spec=p...  30.2 us
    convert_element_type x18, other arithmetic, low(): return v.astype(BF16)  27.5 us
    unnamed x156, local copies, waits for them, and re-layouts  26.6 us
  transfers between devices with their start and end apart: 56, of which 25 were waited for; matrix products, arithmetic and copies ran while one was open for 12% of the time, Pallas kernels for 20%

profile of v2, /device:TPU:0, one launch (start us, length us, event | category | flops | bytes accessed | tf_op | source)
XLA Modules:
  0.0 610.8 jit_solution(3363813770981296123)
XLA Ops:
  12.5 3.0 collective-permute-start
  18.3 4.2 collective-permute-start.2
  22.5 3.5 collective-permute-start.3
  31.3 5.2 collective-permute-start.4
  39.7 6.8 %collective-permute-done.4.refs_14_ = bf16[128,1536]{1,0:T(8,128)(2,1)} collective-permute-done((bf16[128,1536]{1,0:T(8,128)(2,1)}, bf16[128,1536]{1,0:T(8,128)(2,1)}, u32[]{:S(2)}, u32[]{:S(2)}) %collective-permute-start.4) | collective-permute-done | bytes 393248 | tf_op jit(solution)/shard_map/ppermute | solution.py:114
  47.4 3.3 collective-permute-done.1.refs_4_
  50.8 2.7 collective-permute-start.5
  54.6 4.1 collective-permute-start.7
  58.7 2.8 collective-permute-start.8
  61.6 4.4 collective-permute-done.7.refs_15_
  66.0 4.2 collective-permute-done.8.a_ref
  72.8 3.7 collective-permute-done.12.refs_8_
  77.3 5.0 collective-permute-start.14
  87.7 11.8 %project.1 = (bf16[256,1536]{1,0:T(8,128)(2,1)S(1)}, bf16[1024,1024]{1,0:T(8,128)(2,1)}, bf16[1024,1536]{1,0:T(8,128)(2,1)}, bf16[1536,1536]{1,0:T(8,128)(2,1)},...) custom-call(s32[1]{0:T(128)} %bitcast.2.index_ref.number_ref, ...), custom_call_target="tpu_custom_call" | custom-call | flops 276824064 | bytes 1024 | tf_op jit(solution)/shard_map/project/pallas_call | solution.py:267
  102.4 3.0 project_last.1
  105.5 16.9 %attend.1 = (f32[256,1536]{1,0:T(8,128)}, f32[4,8,256]{2,1,0:T(8,128)S(1)}, f32[4,8,256]{2,1,0:T(8,128)S(1)}, f32[256,1536]{1,0:T(8,128)}, bf16[256,1664]{1,0:T(...) custom-call(s32[2]{0:T(128)S(1)} %copy-done.25, bf16[256,1536]{1,0:T(8,128)(2,1)} %copy-done.7, ...), custom_call_target="tpu_custom_call" | custom-call | flops 314572800 | bytes 1024 | tf_op jit(solution)/shard_map/attend/pallas_call | solution.py:511
  124.5 18.7 %collective-permute-done.15.refs_2_ = bf16[256,1664]{1,0:T(8,128)(2,1)S(1)} collective-permute-done((bf16[256,1664]{1,0:T(8,128)(2,1)S(1)}, bf16[256,1664]{1,0:T(8,128)(2,1)S(1)}, u32[]{:S(2)}, u32[]{:S(2)}) %collective-permute-start.15) | collective-permute-done | bytes 852000 | tf_op jit(solution)/shard_map/ppermute | solution.py:55
  146.1 9.1 %collective-permute-done.20.refs_6_ = bf16[128,1664]{1,0:T(8,128)(2,1)S(1)} collective-permute-done((bf16[128,1664]{1,0:T(8,128)(2,1)S(1)}, bf16[128,1664]{1,0:T(8,128)(2,1)S(1)}, u32[]{:S(2)}, u32[]{:S(2)}) %collective-permute-start.20) | collective-permute-done | bytes 426016 | tf_op jit(solution)/shard_map/ppermute | solution.py:55
  158.0 28.6 %expert.2 = (bf16[1152,1536]{1,0:T(8,128)(2,1)}, f32[8,256]{1,0:T(8,128)}, bf16[1152,1664]{1,0:T(8,128)(2,1)}, bf16[768,1024]{1,0:T(8,128)(2,1)}, bf16[768,1024]{1,0:T(8,128)(2,1)}, /*index=5*/bf16[768,1024]{1,0:T(8,128)(2,1)}) custom-call(s32[2]{0:T(128)} %get-tuple-element.390.number_ref, bf16[256,1664]{1,0:T(8,128)(2,1)} %copy-done.4, ...), custom_call_target="tpu_custom_call" | custom-call | flops 622854144 | bytes 1024 | tf_op jit(solution)/shard_map/expert/pallas_call | solution.py:898
  186.6 2.9 collective-permute-start.24
  189.5 40.3 %expert.3 = (bf16[1152,1536]{1,0:T(8,128)(2,1)}, f32[8,256]{1,0:T(8,128)}, bf16[2048,1664]{1,0:T(8,128)(2,1)}, bf16[768,1024]{1,0:T(8,128)(2,1)}, bf16[768,1024]{1,0:T(8,128)(2,1)}, /*index=5*/bf16[768,1024]{1,0:T(8,128)(2,1)}) custom-call(s32[2]{0:T(128)} %get-tuple-element.389.number_ref, bf16[256,1664]{1,0:T(8,128)(2,1)} %copy-done.4, ...), custom_call_target="tpu_custom_call" | custom-call | flops 622854144 | bytes 1024 | tf_op jit(solution)/shard_map/expert/pallas_call | solution.py:898
  235.1 31.1 %collective-permute-done.26 = bf16[768,1024]{1,0:T(8,128)(2,1)} collective-permute-done((bf16[768,1024]{1,0:T(8,128)(2,1)}, bf16[768,1024]{1,0:T(8,128)(2,1)}, u32[]{:S(2)}, u32[]{:S(2)}) %collective-permute-start.26) | collective-permute-done | bytes 1572896 | tf_op jit(solution)/shard_map/ppermute | solution.py:181
  266.2 4.0 add_convert_fusion.9
  270.2 2.6 fusion.9
  277.2 6.7 %combine.1 = bf16[2048,1536]{1,0:T(8,128)(2,1)} custom-call(s32[1]{0:T(128)} %bitcast.2.index_ref.number_ref, f32[8,256]{1,0:T(8,128)S(1)} %copy-done.23, f32[8,256]{1,0:T(8,128)S(1)} %copy-done.24, bf16[1152,1536]{1,0:T(8,128)(2,1)S(1)} %copy-done.5, bf16[1152,1536]{1,0:T(8,128)(2,1)S(1)} %copy-done.6), custom_call_target="tpu_custom_call" | custom-call | flops 70778880 | bytes 1024 | tf_op jit(solution)/shard_map/combine/pallas_call | solution.py:936
  283.9 25.5 %collective-permute-done.28 = bf16[768,1024]{1,0:T(8,128)(2,1)} collective-permute-done((bf16[768,1024]{1,0:T(8,128)(2,1)S(1)}, bf16[768,1024]{1,0:T(8,128)(2,1)}, u32[]{:S(2)}, u32[]{:S(2)}) %collective-permute-start.28) | collective-permute-done | bytes 1572896 | tf_op jit(solution)/shard_map/ppermute | solution.py:171
  309.4 3.7 add_convert_fusion.7
  313.1 4.1 fusion.10
  319.7 10.8 %router_back.1 = (f32[256,1536]{1,0:T(8,128)}, f32[256,1536]{1,0:T(8,128)}, bf16[1536,1664]{1,0:T(8,128)(2,1)}) custom-call(bf16[256,1664]{1,0:T(8,128)(2,1)} %reduce-scatter.5.cloned.1.call-done.total_ref, f32[256,128]{1,0:T(8,128)} %copy-done.20, bf16[1536,128]{1,0:T(8,128)(2,1)} %copy-done.8, f32[8,1536]{1,0:T(8,128)S(1)} %get-tuple-element.191.gains_ref, ...), custom_call_target="tpu_custom_call" | custom-call | flops 132120576 | bytes 1024 | tf_op jit(solution)/shard_map/router_back/pallas_call | solution.py:385
  330.5 30.2 %attend_back.1 = (bf16[256,1536]{1,0:T(8,128)(2,1)S(1)}, bf16[1024,512]{1,0:T(8,128)(2,1)S(1)}, bf16[1024,512]{1,0:T(8,128)(2,1)S(1)}, bf16[1536,2560]{1,0:T(8,128)(2,1)}) custom-call(s32[2]{0:T(128)S(1)} %copy-done.25, bf16[256,1536]{1,0:T(8,128)(2,1)} %copy-done.7, bf16[1024,1024]{1,0:T(8,128)(2,1)} %get-tuple-element.195.k_ref.v_ref, ...), custom_call_target="tpu_custom_call" | custom-call | flops 402653184 | bytes 1024 | tf_op jit(solution)/shard_map/attend_back/pallas_call | solution.py:681
  363.2 3.6 fusion.11
  366.9 3.2 collective-permute-start.32
  370.8 32.2 %collective-permute-done.32 = bf16[768,1024]{1,0:T(8,128)(2,1)S(1)} collective-permute-done((bf16[768,1024]{1,0:T(8,128)(2,1)}, bf16[768,1024]{1,0:T(8,128)(2,1)S(1)}, u32[]{:S(2)}, u32[]{:S(2)}) %collective-permute-start.32) | collective-permute-done | bytes 1572896 | tf_op jit(solution)/shard_map/ppermute | solution.py:171
  403.0 3.9 add_convert_fusion.3
  410.0 3.3 collective-permute-start.33
  417.2 27.9 %collective-permute-done.33 = bf16[768,1024]{1,0:T(8,128)(2,1)S(1)} collective-permute-done((bf16[768,1024]{1,0:T(8,128)(2,1)}, bf16[768,1024]{1,0:T(8,128)(2,1)S(1)}, u32[]{:S(2)}, u32[]{:S(2)}) %collective-permute-start.33) | collective-permute-done | bytes 1572896 | tf_op jit(solution)/shard_map/ppermute | solution.py:171
  452.5 10.2 %collective-permute-start.36 = (bf16[192,1152]{1,0:T(8,128)(2,1)S(1)}, bf16[192,1152]{1,0:T(8,128)(2,1)S(1)}, u32[]{:S(2)}, u32[]{:S(2)}) collective-permute-start(bf16[192,1152]{1,0:T(8,128)(2,1)S(1)} %pad_maximum_fusion.4), channel_id=1, source_target_pairs={{0,1},{3,2},{4,5},{7,6},{8,9},{11,10},{12,13},{15,14},{16,17},{19,... | collective-permute-start | bytes 1327112 | tf_op jit(solution)/shard_map/ppermute | solution.py:181
  464.0 5.8 collective-permute-start.35
  472.5 6.2 %collective-permute-done.35 = bf16[192,1536]{1,0:T(8,128)(2,1)S(1)} collective-permute-done((bf16[192,1536]{1,0:T(8,128)(2,1)S(1)}, bf16[192,1536]{1,0:T(8,128)(2,1)S(1)}, u32[]{:S(2)}, u32[]{:S(2)}) %collective-permute-start.35) | collective-permute-done | bytes 589856 | tf_op jit(solution)/shard_map/ppermute | solution.py:181
  480.9 15.0 %reduce-scatter.7.cloned.1.call-done = bf16[192,1664]{1,0:T(8,128)(2,1)} async-done(((bf16[1536,1664]{1,0:T(8,128)(2,1)}), bf16[192,1664]{1,0:T(8,128)(2,1)}) %reduce-scatter.7.cloned.1.call-update) | async-done | bytes 638992 | tf_op jit(solution)/shard_map/reduce_scatter | solution.py:1070
  499.3 11.7 %collective-permute-start.40 = (bf16[192,1664]{1,0:T(8,128)(2,1)}, bf16[192,1664]{1,0:T(8,128)(2,1)S(1)}, u32[]{:S(2)}, u32[]{:S(2)}) collective-permute-start(bf16[192,1664]{1,0:T(8,128)(2,1)} %reduce-scatter.7.cloned.1.call-done), channel_id=1, source_target_pairs={{0,1},{3,2},{4,5},{7,6},{8,9},{11,10},{12,13},{15,14},{16,17},{19,... | collective-permute-start | bytes 1916936 | tf_op jit(solution)/shard_map/ppermute | solution.py:181
  514.9 9.1 %collective-permute-done.40 = bf16[192,1664]{1,0:T(8,128)(2,1)S(1)} collective-permute-done((bf16[192,1664]{1,0:T(8,128)(2,1)}, bf16[192,1664]{1,0:T(8,128)(2,1)S(1)}, u32[]{:S(2)}, u32[]{:S(2)}) %collective-permute-start.40) | collective-permute-done | bytes 639008 | tf_op jit(solution)/shard_map/ppermute | solution.py:181
  525.0 16.7 %collective-permute-done.43 = bf16[768,1024]{1,0:T(8,128)(2,1)} collective-permute-done((bf16[768,1024]{1,0:T(8,128)(2,1)}, bf16[768,1024]{1,0:T(8,128)(2,1)}, u32[]{:S(2)}, u32[]{:S(2)}) %collective-permute-start.43) | collective-permute-done | bytes 1572896 | tf_op jit(solution)/shard_map/ppermute | solution.py:181
  545.2 2.6 copy-done.43
  562.8 2.6 convert_dynamic-update-slice_fusion
  566.1 3.5 pad_maximum_fusion
  569.5 4.9 copy-done.27
  585.1 13.2 %collective-permute-done.49 = bf16[192,1664]{1,0:T(8,128)(2,1)S(1)} collective-permute-done((bf16[192,1664]{1,0:T(8,128)(2,1)S(1)}, bf16[192,1664]{1,0:T(8,128)(2,1)S(1)}, u32[]{:S(2)}, u32[]{:S(2)}) %collective-permute-start.49) | collective-permute-done | bytes 639008 | tf_op jit(solution)/shard_map/ppermute | solution.py:181
  (321 shorter events, 115.7 us)
Async XLA Ops:
  7.2 98.3 %all-gather.3.cloned.1.call-start = ((), (), s32[]{:S(2)}) async-start(), calls=%async_computation.4 | async-start | bytes 5308416 | tf_op jit(solution)/shard_map/all_gather | solution.py:1013
  7.9 150.1 %all-gather.5.cloned.1.call-start = ((), (), s32[]{:S(2)}) async-start(), calls=%async_computation.5 | async-start | bytes 7667712 | tf_op jit(solution)/shard_map/all_gather | solution.py:1015
  12.5 34.8 %collective-permute-start = (bf16[192,2688]{1,0:T(8,128)(2,1)S(1)}, bf16[192,2688]{1,0:T(8,128)(2,1)S(1)}, u32[]{:S(2)}, u32[]{:S(2)}) collective-permute-start(bf16[192,2688]{1,0:T(8,128)(2,1)S(1)} %concatenate.30.refs_0_), channel_id=1, source_target_pairs={{0,8},{4,12},{8,0},{12,4},{16,24},{20,28},{24,16},{28,20},{1,9},{5... | collective-permute-start | bytes 3096584 | tf_op jit(solution)/shard_map/ppermute | solution.py:55
  15.5 35.2 %collective-permute-start.1 = (bf16[192,2688]{1,0:T(8,128)(2,1)S(1)}, bf16[192,2688]{1,0:T(8,128)(2,1)}, u32[]{:S(2)}, u32[]{:S(2)}) collective-permute-start(bf16[192,2688]{1,0:T(8,128)(2,1)S(1)} %concatenate.30.refs_0_), channel_id=1, source_target_pairs={{0,16},{4,20},{8,24},{12,28},{16,0},{20,4},{24,8},{28,12},{1,17},{... | collective-permute-start | bytes 3096584 | tf_op jit(solution)/shard_map/ppermute | solution.py:55
  18.3 13.0 %collective-permute-start.2 = (bf16[128,1536]{1,0:T(8,128)(2,1)S(1)}, bf16[128,1536]{1,0:T(8,128)(2,1)}, u32[]{:S(2)}, u32[]{:S(2)}) collective-permute-start(bf16[128,1536]{1,0:T(8,128)(2,1)S(1)} %get-tuple-element.383.refs_10_), channel_id=1, source_target_pairs={{0,1},{1,2},{2,3},{4,5},{5,6},{6,7},{8,9},{9,10},{10,11},{12,13},{... | collective-permute-start | bytes 1179656 | tf_op jit(solution)/shard_map/ppermute | solution.py:114
  22.5 17.2 %collective-permute-start.3 = (bf16[128,1536]{1,0:T(8,128)(2,1)S(1)}, bf16[128,1536]{1,0:T(8,128)(2,1)}, u32[]{:S(2)}, u32[]{:S(2)}) collective-permute-start(bf16[128,1536]{1,0:T(8,128)(2,1)S(1)} %get-tuple-element.382.refs_11_), channel_id=1, source_target_pairs={{0,1},{1,2},{2,3},{4,5},{5,6},{6,7},{8,9},{9,10},{10,11},{12,13},{... | collective-permute-start | bytes 1179656 | tf_op jit(solution)/shard_map/ppermute | solution.py:114
  31.3 15.2 %collective-permute-start.4 = (bf16[128,1536]{1,0:T(8,128)(2,1)}, bf16[128,1536]{1,0:T(8,128)(2,1)}, u32[]{:S(2)}, u32[]{:S(2)}) collective-permute-start(bf16[128,1536]{1,0:T(8,128)(2,1)} %collective-permute-done.2.refs_12_), channel_id=1, source_target_pairs={{0,1},{1,2},{2,3},{4,5},{5,6},{6,7},{8,9},{9,10},{10,11},{12,13},{... | collective-permute-start | bytes 1179656 | tf_op jit(solution)/shard_map/ppermute | solution.py:114
  50.7 266.5 %reduce-scatter.5.cloned.1.call-start = ((), (), s32[]{:S(2)}) async-start(), calls=%async_computation.6 | async-start | bytes 7667712 | tf_op jit(solution)/shard_map/reduce_scatter | solution.py:1054
  50.8 20.1 %collective-permute-start.5 = (bf16[96,2688]{1,0:T(8,128)(2,1)S(1)}, bf16[96,2688]{1,0:T(8,128)(2,1)S(1)}, u32[]{:S(2)}, u32[]{:S(2)}) collective-permute-start(bf16[96,2688]{1,0:T(8,128)(2,1)S(1)} %slice.82), channel_id=1, source_target_pairs={{0,16},{4,20},{8,24},{12,28},{16,0},{20,4},{24,8},{28,12},{1,17},{... | collective-permute-start | bytes 1548296 | tf_op jit(solution)/shard_map/ppermute | solution.py:55
  54.6 16.4 %collective-permute-start.6 = (bf16[96,2688]{1,0:T(8,128)(2,1)S(1)}, bf16[96,2688]{1,0:T(8,128)(2,1)}, u32[]{:S(2)}, u32[]{:S(2)}) collective-permute-start(bf16[96,2688]{1,0:T(8,128)(2,1)S(1)} %slice.83), channel_id=1, source_target_pairs={{0,8},{4,12},{8,0},{12,4},{16,24},{20,28},{24,16},{28,20},{1,9},{5... | collective-permute-start | bytes 1548296 | tf_op jit(solution)/shard_map/ppermute | solution.py:55
  58.7 11.5 %collective-permute-start.8 = (bf16[128,1536]{1,0:T(8,128)(2,1)}, bf16[128,1536]{1,0:T(8,128)(2,1)S(1)}, u32[]{:S(2)}, u32[]{:S(2)}) collective-permute-start(bf16[128,1536]{1,0:T(8,128)(2,1)} %collective-permute-done.4.refs_14_), channel_id=1, source_target_pairs={{0,1},{1,2},{2,3},{4,5},{5,6},{6,7},{8,9},{9,10},{10,11},{12,13},{... | collective-permute-start | bytes 1179656 | tf_op jit(solution)/shard_map/ppermute | solution.py:114
  70.9 12.6 %collective-permute-start.10 = (bf16[192,2688]{1,0:T(8,128)(2,1)S(1)}, bf16[192,2688]{1,0:T(8,128)(2,1)}, u32[]{:S(2)}, u32[]{:S(2)}) collective-permute-start(bf16[192,2688]{1,0:T(8,128)(2,1)S(1)} %collective-permute-done.refs_2_), channel_id=1, source_target_pairs={{0,4},{4,0},{8,12},{12,8},{16,20},{20,16},{24,28},{28,24},{1,5},{5... | collective-permute-start | bytes 3096584 | tf_op jit(solution)/shard_map/ppermute | solution.py:55
  70.9 12.6 %collective-permute-start.11 = (bf16[192,2688]{1,0:T(8,128)(2,1)}, bf16[192,2688]{1,0:T(8,128)(2,1)}, u32[]{:S(2)}, u32[]{:S(2)}) collective-permute-start(bf16[192,2688]{1,0:T(8,128)(2,1)} %collective-permute-done.1.refs_4_), channel_id=1, source_target_pairs={{0,4},{4,0},{8,12},{12,8},{16,20},{20,16},{24,28},{28,24},{1,5},{5... | collective-permute-start | bytes 3096584 | tf_op jit(solution)/shard_map/ppermute | solution.py:55
  71.4 12.1 %collective-permute-start.9 = (bf16[192,2688]{1,0:T(8,128)(2,1)S(1)}, bf16[192,2688]{1,0:T(8,128)(2,1)}, u32[]{:S(2)}, u32[]{:S(2)}) collective-permute-start(bf16[192,2688]{1,0:T(8,128)(2,1)S(1)} %concatenate.30.refs_0_), channel_id=1, source_target_pairs={{0,4},{4,0},{8,12},{12,8},{16,20},{20,16},{24,28},{28,24},{1,5},{5... | collective-permute-start | bytes 3096584 | tf_op jit(solution)/shard_map/ppermute | solution.py:55
  77.3 23.1 %collective-permute-start.14 = (bf16[128,1536]{1,0:T(8,128)(2,1)}, bf16[128,1536]{1,0:T(8,128)(2,1)}, u32[]{:S(2)}, u32[]{:S(2)}) collective-permute-start(bf16[128,1536]{1,0:T(8,128)(2,1)} %collective-permute-done.7.refs_15_), channel_id=1, source_target_pairs={{0,1},{1,2},{2,3},{4,5},{5,6},{6,7},{8,9},{9,10},{10,11},{12,13},{... | collective-permute-start | bytes 1179656 | tf_op jit(solution)/shard_map/ppermute | solution.py:114
  122.4 20.8 %collective-permute-start.15 = (bf16[256,1664]{1,0:T(8,128)(2,1)S(1)}, bf16[256,1664]{1,0:T(8,128)(2,1)S(1)}, u32[]{:S(2)}, u32[]{:S(2)}) collective-permute-start(bf16[256,1664]{1,0:T(8,128)(2,1)S(1)} %get-tuple-element.204.refs_0_.hn_ref), channel_id=1, source_target_pairs={{0,8},{4,12},{8,0},{12,4},{16,24},{20,28},{24,16},{28,20},{1,9},{5... | collective-permute-start | bytes 2555912 | tf_op jit(solution)/shard_map/ppermute | solution.py:55
  124.3 20.4 %collective-permute-start.16 = (bf16[256,1664]{1,0:T(8,128)(2,1)S(1)}, bf16[256,1664]{1,0:T(8,128)(2,1)S(1)}, u32[]{:S(2)}, u32[]{:S(2)}) collective-permute-start(bf16[256,1664]{1,0:T(8,128)(2,1)S(1)} %get-tuple-element.204.refs_0_.hn_ref), channel_id=1, source_target_pairs={{0,16},{4,20},{8,24},{12,28},{16,0},{20,4},{24,8},{28,12},{1,17},{... | collective-permute-start | bytes 2555912 | tf_op jit(solution)/shard_map/ppermute | solution.py:55
  145.6 12.4 %collective-permute-start.17 = (bf16[256,1664]{1,0:T(8,128)(2,1)S(1)}, bf16[256,1664]{1,0:T(8,128)(2,1)}, u32[]{:S(2)}, u32[]{:S(2)}) collective-permute-start(bf16[256,1664]{1,0:T(8,128)(2,1)S(1)} %get-tuple-element.204.refs_0_.hn_ref), channel_id=1, source_target_pairs={{0,4},{4,0},{8,12},{12,8},{16,20},{20,16},{24,28},{28,24},{1,5},{5... | collective-permute-start | bytes 2555912 | tf_op jit(solution)/shard_map/ppermute | solution.py:55
  145.6 12.4 %collective-permute-start.18 = (bf16[256,1664]{1,0:T(8,128)(2,1)S(1)}, bf16[256,1664]{1,0:T(8,128)(2,1)}, u32[]{:S(2)}, u32[]{:S(2)}) collective-permute-start(bf16[256,1664]{1,0:T(8,128)(2,1)S(1)} %collective-permute-done.15.refs_2_), channel_id=1, source_target_pairs={{0,4},{4,0},{8,12},{12,8},{16,20},{20,16},{24,28},{28,24},{1,5},{5... | collective-permute-start | bytes 2555912 | tf_op jit(solution)/shard_map/ppermute | solution.py:55
  146.1 11.9 %collective-permute-start.19 = (bf16[256,1664]{1,0:T(8,128)(2,1)S(1)}, bf16[256,1664]{1,0:T(8,128)(2,1)}, u32[]{:S(2)}, u32[]{:S(2)}) collective-permute-start(bf16[256,1664]{1,0:T(8,128)(2,1)S(1)} %collective-permute-done.16.refs_4_), channel_id=1, source_target_pairs={{0,4},{4,0},{8,12},{12,8},{16,20},{20,16},{24,28},{28,24},{1,5},{5... | collective-permute-start | bytes 2555912 | tf_op jit(solution)/shard_map/ppermute | solution.py:55
  186.6 43.2 %collective-permute-start.24 = (bf16[768,1024]{1,0:T(8,128)(2,1)}, bf16[768,1024]{1,0:T(8,128)(2,1)S(1)}, u32[]{:S(2)}, u32[]{:S(2)}) collective-permute-start(bf16[768,1024]{1,0:T(8,128)(2,1)} %get-tuple-element.221), channel_id=1, source_target_pairs={{0,1},{3,2},{4,5},{7,6},{8,9},{11,10},{12,13},{15,14},{16,17},{19,... | collective-permute-start | bytes 4718600 | tf_op jit(solution)/shard_map/ppermute | solution.py:181
  230.5 217.7 %reduce-scatter.9.cloned.1.call-start = ((), (), s32[]{:S(2)}) async-start(), calls=%async_computation.8 | async-start | bytes 8847360 | tf_op jit(solution)/shard_map/reduce_scatter | solution.py:1068
  230.6 35.6 %collective-permute-start.26 = (bf16[768,1024]{1,0:T(8,128)(2,1)}, bf16[768,1024]{1,0:T(8,128)(2,1)}, u32[]{:S(2)}, u32[]{:S(2)}) collective-permute-start(bf16[768,1024]{1,0:T(8,128)(2,1)} %get-tuple-element.224), channel_id=1, source_target_pairs={{0,1},{3,2},{4,5},{7,6},{8,9},{11,10},{12,13},{15,14},{16,17},{19,... | collective-permute-start | bytes 4718600 | tf_op jit(solution)/shard_map/ppermute | solution.py:181
  233.0 37.1 %collective-permute-start.25 = (bf16[768,1024]{1,0:T(8,128)(2,1)S(1)}, bf16[768,1024]{1,0:T(8,128)(2,1)}, u32[]{:S(2)}, u32[]{:S(2)}) collective-permute-start(bf16[768,1024]{1,0:T(8,128)(2,1)S(1)} %add_convert_fusion.11), channel_id=1, source_target_pairs={{1,2},{2,1},{5,6},{6,5},{9,10},{10,9},{13,14},{14,13},{17,18},{18,... | collective-permute-start | bytes 4718600 | tf_op jit(solution)/shard_map/ppermute | solution.py:181
  272.8 36.5 %collective-permute-start.28 = (bf16[768,1024]{1,0:T(8,128)(2,1)S(1)}, bf16[768,1024]{1,0:T(8,128)(2,1)}, u32[]{:S(2)}, u32[]{:S(2)}) collective-permute-start(bf16[768,1024]{1,0:T(8,128)(2,1)S(1)} %fusion.9), channel_id=1, source_target_pairs={{0,1},{1,0},{2,3},{3,2},{4,5},{5,4},{6,7},{7,6},{8,9},{9,8},{10,11... | collective-permute-start | bytes 4718600 | tf_op jit(solution)/shard_map/ppermute | solution.py:171
  275.3 37.7 %collective-permute-start.27 = (bf16[768,1024]{1,0:T(8,128)(2,1)}, bf16[768,1024]{1,0:T(8,128)(2,1)}, u32[]{:S(2)}, u32[]{:S(2)}) collective-permute-start(bf16[768,1024]{1,0:T(8,128)(2,1)} %add_convert_fusion.9), channel_id=1, source_target_pairs={{1,2},{2,1},{5,6},{6,5},{9,10},{10,9},{13,14},{14,13},{17,18},{18,... | collective-permute-start | bytes 4718600 | tf_op jit(solution)/shard_map/ppermute | solution.py:181
  317.2 43.5 %collective-permute-start.30 = (bf16[768,1024]{1,0:T(8,128)(2,1)}, bf16[768,1024]{1,0:T(8,128)(2,1)S(1)}, u32[]{:S(2)}, u32[]{:S(2)}) collective-permute-start(bf16[768,1024]{1,0:T(8,128)(2,1)} %fusion.10), channel_id=1, source_target_pairs={{0,1},{1,0},{2,3},{3,2},{4,5},{5,4},{6,7},{7,6},{8,9},{9,8},{10,11... | collective-permute-start | bytes 4718600 | tf_op jit(solution)/shard_map/ppermute | solution.py:171
  318.9 43.7 %collective-permute-start.29 = (bf16[768,1024]{1,0:T(8,128)(2,1)}, bf16[768,1024]{1,0:T(8,128)(2,1)S(1)}, u32[]{:S(2)}, u32[]{:S(2)}) collective-permute-start(bf16[768,1024]{1,0:T(8,128)(2,1)} %add_convert_fusion.7), channel_id=1, source_target_pairs={{1,2},{2,1},{5,6},{6,5},{9,10},{10,9},{13,14},{14,13},{17,18},{18,... | collective-permute-start | bytes 4718600 | tf_op jit(solution)/shard_map/ppermute | solution.py:181
  366.8 129.1 %reduce-scatter.7.cloned.1.call-start = ((), (), s32[]{:S(2)}) async-start(), calls=%async_computation.7 | async-start | bytes 5750784 | tf_op jit(solution)/shard_map/reduce_scatter | solution.py:1070
  366.9 36.1 %collective-permute-start.32 = (bf16[768,1024]{1,0:T(8,128)(2,1)}, bf16[768,1024]{1,0:T(8,128)(2,1)S(1)}, u32[]{:S(2)}, u32[]{:S(2)}) collective-permute-start(bf16[768,1024]{1,0:T(8,128)(2,1)} %fusion.11), channel_id=1, source_target_pairs={{0,1},{1,0},{2,3},{3,2},{4,5},{5,4},{6,7},{7,6},{8,9},{9,8},{10,11... | collective-permute-start | bytes 4718600 | tf_op jit(solution)/shard_map/ppermute | solution.py:171
  370.0 36.9 %collective-permute-start.31 = (bf16[768,1024]{1,0:T(8,128)(2,1)}, bf16[768,1024]{1,0:T(8,128)(2,1)S(1)}, u32[]{:S(2)}, u32[]{:S(2)}) collective-permute-start(bf16[768,1024]{1,0:T(8,128)(2,1)} %add_convert_fusion.5), channel_id=1, source_target_pairs={{1,2},{2,1},{5,6},{6,5},{9,10},{10,9},{13,14},{14,13},{17,18},{18,... | collective-permute-start | bytes 4718600 | tf_op jit(solution)/shard_map/ppermute | solution.py:181
  409.2 192.4 %reduce-scatter.11.cloned.1.call-start = ((), (), s32[]{:S(2)}) async-start(), calls=%async_computation.9 | async-start | bytes 7077888 | tf_op jit(solution)/shard_map/reduce_scatter | solution.py:1089
  410.0 35.2 %collective-permute-start.33 = (bf16[768,1024]{1,0:T(8,128)(2,1)}, bf16[768,1024]{1,0:T(8,128)(2,1)S(1)}, u32[]{:S(2)}, u32[]{:S(2)}) collective-permute-start(bf16[768,1024]{1,0:T(8,128)(2,1)} %fusion.12), channel_id=1, source_target_pairs={{0,1},{1,0},{2,3},{3,2},{4,5},{5,4},{6,7},{7,6},{8,9},{9,8},{10,11... | collective-permute-start | bytes 4718600 | tf_op jit(solution)/shard_map/ppermute | solution.py:171
  414.4 55.3 %collective-permute-start.39 = (bf16[256,1024]{1,0:T(8,128)(2,1)}, bf16[256,1024]{1,0:T(8,128)(2,1)}, u32[]{:S(2)}, u32[]{:S(2)}) collective-permute-start(bf16[256,1024]{1,0:T(8,128)(2,1)} %slice.106), channel_id=1, source_target_pairs={{3,2},{7,6},{11,10},{15,14},{19,18},{23,22},{27,26},{31,30}} | collective-permute-start | bytes 1572872 | tf_op jit(solution)/shard_map/ppermute | solution.py:1086
  451.7 27.2 %collective-permute-start.37 = (bf16[768,1024]{1,0:T(8,128)(2,1)S(1)}, bf16[768,1024]{1,0:T(8,128)(2,1)S(1)}, u32[]{:S(2)}, u32[]{:S(2)}) collective-permute-start(bf16[768,1024]{1,0:T(8,128)(2,1)S(1)} %copy-done.51), channel_id=1, source_target_pairs={{1,2},{2,1},{5,6},{6,5},{9,10},{10,9},{13,14},{14,13},{17,18},{18,... | collective-permute-start | bytes 4718600 | tf_op jit(solution)/shard_map/ppermute | solution.py:181
  452.5 20.0 %collective-permute-start.36 = (bf16[192,1152]{1,0:T(8,128)(2,1)S(1)}, bf16[192,1152]{1,0:T(8,128)(2,1)S(1)}, u32[]{:S(2)}, u32[]{:S(2)}) collective-permute-start(bf16[192,1152]{1,0:T(8,128)(2,1)S(1)} %pad_maximum_fusion.4), channel_id=1, source_target_pairs={{0,1},{3,2},{4,5},{7,6},{8,9},{11,10},{12,13},{15,14},{16,17},{19,... | collective-permute-start | bytes 1327112 | tf_op jit(solution)/shard_map/ppermute | solution.py:181
  462.7 33.2 %collective-permute-start.38 = (bf16[768,1024]{1,0:T(8,128)(2,1)S(1)}, bf16[768,1024]{1,0:T(8,128)(2,1)}, u32[]{:S(2)}, u32[]{:S(2)}) collective-permute-start(bf16[768,1024]{1,0:T(8,128)(2,1)S(1)} %add_convert_fusion.1), channel_id=1, source_target_pairs={{1,0},{2,3},{5,4},{6,7},{9,8},{10,11},{13,12},{14,15},{17,16},{18,... | collective-permute-start | bytes 4718600 | tf_op jit(solution)/shard_map/ppermute | solution.py:181
  464.0 14.8 %collective-permute-start.35 = (bf16[192,1536]{1,0:T(8,128)(2,1)S(1)}, bf16[192,1536]{1,0:T(8,128)(2,1)S(1)}, u32[]{:S(2)}, u32[]{:S(2)}) collective-permute-start(bf16[192,1536]{1,0:T(8,128)(2,1)S(1)} %slice.104), channel_id=1, source_target_pairs={{0,1},{3,2},{4,5},{7,6},{8,9},{11,10},{12,13},{15,14},{16,17},{19,... | collective-permute-start | bytes 1769480 | tf_op jit(solution)/shard_map/ppermute | solution.py:181
  495.9 15.1 %collective-permute-start.42 = (bf16[192,1152]{1,0:T(8,128)(2,1)S(1)}, bf16[192,1152]{1,0:T(8,128)(2,1)S(1)}, u32[]{:S(2)}, u32[]{:S(2)}) collective-permute-start(bf16[192,1152]{1,0:T(8,128)(2,1)S(1)} %add_convert_fusion.20), channel_id=1, source_target_pairs={{1,2},{2,1},{5,6},{6,5},{9,10},{10,9},{13,14},{14,13},{17,18},{18,... | collective-permute-start | bytes 1327112 | tf_op jit(solution)/shard_map/ppermute | solution.py:181
  496.5 15.3 %collective-permute-start.44 = (bf16[256,1024]{1,0:T(8,128)(2,1)}, bf16[256,1024]{1,0:T(8,128)(2,1)S(1)}, u32[]{:S(2)}, u32[]{:S(2)}) collective-permute-start(bf16[256,1024]{1,0:T(8,128)(2,1)} %add_convert_fusion.18), channel_id=1, source_target_pairs={{2,1},{3,2},{6,5},{7,6},{10,9},{11,10},{14,13},{15,14},{18,17},{19... | collective-permute-start | bytes 1572872 | tf_op jit(solution)/shard_map/ppermute | solution.py:1086
  497.3 16.7 %collective-permute-start.41 = (bf16[192,1536]{1,0:T(8,128)(2,1)S(1)}, bf16[192,1536]{1,0:T(8,128)(2,1)S(1)}, u32[]{:S(2)}, u32[]{:S(2)}) collective-permute-start(bf16[192,1536]{1,0:T(8,128)(2,1)S(1)} %add_convert_fusion.15), channel_id=1, source_target_pairs={{1,2},{2,1},{5,6},{6,5},{9,10},{10,9},{13,14},{14,13},{17,18},{18,... | collective-permute-start | bytes 1769480 | tf_op jit(solution)/shard_map/ppermute | solution.py:181
  498.0 43.8 %collective-permute-start.43 = (bf16[768,1024]{1,0:T(8,128)(2,1)}, bf16[768,1024]{1,0:T(8,128)(2,1)}, u32[]{:S(2)}, u32[]{:S(2)}) collective-permute-start(bf16[768,1024]{1,0:T(8,128)(2,1)} %add_convert_fusion), channel_id=1, source_target_pairs={{1,0},{2,3},{5,4},{6,7},{9,8},{10,11},{13,12},{14,15},{17,16},{18,... | collective-permute-start | bytes 4718600 | tf_op jit(solution)/shard_map/ppermute | solution.py:181
  499.3 24.8 %collective-permute-start.40 = (bf16[192,1664]{1,0:T(8,128)(2,1)}, bf16[192,1664]{1,0:T(8,128)(2,1)S(1)}, u32[]{:S(2)}, u32[]{:S(2)}) collective-permute-start(bf16[192,1664]{1,0:T(8,128)(2,1)} %reduce-scatter.7.cloned.1.call-done), channel_id=1, source_target_pairs={{0,1},{3,2},{4,5},{7,6},{8,9},{11,10},{12,13},{15,14},{16,17},{19,... | collective-permute-start | bytes 1916936 | tf_op jit(solution)/shard_map/ppermute | solution.py:181
  542.1 32.4 %collective-permute-start.48 = (bf16[256,1024]{1,0:T(8,128)(2,1)}, bf16[256,1024]{1,0:T(8,128)(2,1)}, u32[]{:S(2)}, u32[]{:S(2)}) collective-permute-start(bf16[256,1024]{1,0:T(8,128)(2,1)} %add_convert_fusion.17), channel_id=1, source_target_pairs={{1,0},{2,1},{3,2},{5,4},{6,5},{7,6},{9,8},{10,9},{11,10},{13,12},{... | collective-permute-start | bytes 1572872 | tf_op jit(solution)/shard_map/ppermute | solution.py:1086
  550.4 29.3 %collective-permute-start.45 = (bf16[192,1664]{1,0:T(8,128)(2,1)S(1)}, bf16[192,1664]{1,0:T(8,128)(2,1)S(1)}, u32[]{:S(2)}, u32[]{:S(2)}) collective-permute-start(bf16[192,1664]{1,0:T(8,128)(2,1)S(1)} %copy-done.60), channel_id=1, source_target_pairs={{1,2},{2,1},{5,6},{6,5},{9,10},{10,9},{13,14},{14,13},{17,18},{18,... | collective-permute-start | bytes 1916936 | tf_op jit(solution)/shard_map/ppermute | solution.py:181
  551.2 28.7 %collective-permute-start.47 = (bf16[192,1536]{1,0:T(8,128)(2,1)S(1)}, bf16[192,1536]{1,0:T(8,128)(2,1)S(1)}, u32[]{:S(2)}, u32[]{:S(2)}) collective-permute-start(bf16[192,1536]{1,0:T(8,128)(2,1)S(1)} %copy-done.61), channel_id=1, source_target_pairs={{1,0},{2,3},{5,4},{6,7},{9,8},{10,11},{13,12},{14,15},{17,16},{18,... | collective-permute-start | bytes 1769480 | tf_op jit(solution)/shard_map/ppermute | solution.py:181
  552.6 27.3 %collective-permute-start.46 = (bf16[192,1152]{1,0:T(8,128)(2,1)S(1)}, bf16[192,1152]{1,0:T(8,128)(2,1)}, u32[]{:S(2)}, u32[]{:S(2)}) collective-permute-start(bf16[192,1152]{1,0:T(8,128)(2,1)S(1)} %copy-done.63), channel_id=1, source_target_pairs={{1,0},{2,3},{5,4},{6,7},{9,8},{10,11},{13,12},{14,15},{17,16},{18,... | collective-permute-start | bytes 1327112 | tf_op jit(solution)/shard_map/ppermute | solution.py:181
  582.0 16.3 %collective-permute-start.49 = (bf16[192,1664]{1,0:T(8,128)(2,1)S(1)}, bf16[192,1664]{1,0:T(8,128)(2,1)S(1)}, u32[]{:S(2)}, u32[]{:S(2)}) collective-permute-start(bf16[192,1664]{1,0:T(8,128)(2,1)S(1)} %add_convert_fusion.12), channel_id=1, source_target_pairs={{1,0},{2,3},{5,4},{6,7},{9,8},{10,11},{13,12},{14,15},{17,16},{18,... | collective-permute-start | bytes 1916936 | tf_op jit(solution)/shard_map/ppermute | solution.py:181
  (87 other events, 1048.2 us)
Sparse Core Ops, SparseCore 0:
  9.9 57.9 all-gather.2
  70.3 48.3 all-gather.4
  230.7 63.4 reduce-scatter.4
  366.9 69.0 reduce-scatter.8
  440.0 55.7 reduce-scatter.6
  541.9 59.5 reduce-scatter.10

commit v3 on v2

--- a/solution.py
+++ b/solution.py
@@ -182,6 +182,18 @@
         self.flights.append(flight)
         return critical
 
+    def hold(self, *critical):
+        if self.plain:
+            return critical
+        own = [[entry[2] for entry in flight] for flight in self.flights]
+        own, critical = lax.optimization_barrier((own, critical))
+        for n, flight in enumerate(self.flights):
+            self.flights[n] = [
+                (kind, name, v, arrived)
+                for (kind, name, _, arrived), v in zip(flight, own[n])
+            ]
+        return critical
+
     def total(self, name):
         if self.plain:
             return up(self.done[name])
@@ -333,13 +345,11 @@
     resid_ref,
     cot_ref,
     wo_ref,
-    hn_ref,
-    attn_ref,
     grad_ref,
     heads_ref,
-    part_ref,
-    held_ref,
-    sems,
+    attn_ref,
+    logits_ref,
+    gain_ref,
 ):
     width = resid_ref.shape[1]
     total = up(total_ref[...])
@@ -359,6 +369,15 @@
     grad_ref[...] = grad
     grad_low = low(grad)
     heads_ref[...] = dot_nt(grad_low, wo_ref[...])
+    attn_ref[...] = grad_low
+    logits_ref[...] = grad_logits
+    gain_ref[...] = jnp.broadcast_to(gain, gain_ref.shape)
+
+
+def output_grad_kernel(
+    experts, attn_ref, grad_ref, hn_ref, logits_ref, gain_ref, part_ref, held_ref, sems
+):
+    width = grad_ref.shape[1]
     copies = []
 
     def put(cols, value):
@@ -368,37 +387,52 @@
         )
         copies[-1].start()
 
-    small = dot_tn(hn_ref[:, :width], grad_logits)
+    small = dot_tn(hn_ref[:, :width], logits_ref[...])
     lane = lax.broadcasted_iota(jnp.int32, small.shape, 1)
-    gain = jnp.transpose(jnp.broadcast_to(gain, (SIDE, width)))
+    gain = jnp.transpose(jnp.broadcast_to(gain_ref[:1, :], (SIDE, width)))
     put(slice(width, width + SIDE), jnp.where(lane == experts, gain, small))
     attn_t = low(transposed(attn_ref[...]))
     for c in range(0, width, 256):
-        put(slice(c, c + 256), dot_nn(attn_t, grad_low[:, c : c + 256]))
+        put(slice(c, c + 256), dot_nn(attn_t, grad_ref[:, c : c + 256]))
     for copy in copies:
         copy.wait()
 
 
-def router_back(total, gates, router, gains, resid, cot, wo, hn, attn, experts):
+def output_grad(attn, grad, hn, logits, gain, experts):
+    heads, width = attn.shape[1], grad.shape[1]
+    return pl.pallas_call(
+        functools.partial(output_grad_kernel, experts),
+        in_specs=[WHOLE] * 5,
+        out_specs=pl.BlockSpec(memory_space=pl.ANY),
+        out_shape=pltpu.HBM((heads, width + SIDE), BF16),
+        scratch_shapes=[
+            pltpu.VMEM((heads, width + SIDE), BF16),
+            pltpu.SemaphoreType.DMA((width // 256 + 1,)),
+        ],
+        compiler_params=params(28),
+        cost_estimate=cost(4 * attn.shape[0] * heads * width),
+        name="output_grad",
+    )(*hbm(attn, grad, hn, logits, gain))
+
+
+def router_back(total, gates, router, gains, resid, cot, wo, experts):
     rows, width = resid.shape
     heads = wo.shape[0]
     return pl.pallas_call(
         functools.partial(router_back_kernel, experts),
-        in_specs=[WHOLE] * 9,
-        out_specs=[WHOLE, WHOLE, pl.BlockSpec(memory_space=pl.ANY)],
+        in_specs=[WHOLE] * 7,
+        out_specs=[WHOLE] * 5,
         out_shape=[
             pltpu.HBM((rows, width), F32),
             pltpu.HBM((rows, heads), F32),
-            pltpu.HBM((heads, width + SIDE), BF16),
+            pltpu.HBM((rows, width), BF16),
+            pltpu.HBM((rows, SIDE), BF16),
+            pltpu.HBM((8, width), F32),
         ],
-        scratch_shapes=[
-            pltpu.VMEM((heads, width + SIDE), BF16),
-            pltpu.SemaphoreType.DMA((width // 256 + 1,)),
-        ],
-        compiler_params=params(36),
+        compiler_params=params(30),
         cost_estimate=cost(14 * rows * heads * width),
         name="router_back",
-    )(*hbm(total, gates, router), gains, *hbm(resid, cot, wo, hn, attn))
+    )(*hbm(total, gates, router), gains, *hbm(resid, cot, wo))
 
 
 def transposed(v):
@@ -1054,18 +1088,18 @@
     gin_sum = lax.psum_scatter(gin_tokens, "dp", scatter_dimension=0, tiled=True)
     outs, slots = sums.step(outs, slots)
     out_tokens = combine(index, slots, outs, cap, range(0, dp_count, 1), lambda n, i: n ^ i)
-    gin_sum, out_tokens = sums.step(gin_sum, out_tokens)
-
-    grad_resid, grad_heads, part_output = router_back(
-        gin_sum, gates, router_w, gains, resid, grad_y, output_w, hn_two, attn_low, experts
-    )
+
+    backed = router_back(gin_sum, gates, router_w, gains, resid, grad_y, output_w, experts)
+    *backed, out_tokens = sums.step(*sums.hold(*backed, out_tokens))
+    grad_resid, grad_heads, *for_output = backed
 
     backed = attend_back(
         place, queries, keyval, grad_heads, attn, tops, totals, cosine, sine, hn_seq, groups
     )
-    backed = sums.step(*backed, part_output)
-    grad_query, grad_keys, grad_values, part_first, part_output = backed
+    backed = sums.step(*backed, *for_output)
+    grad_query, grad_keys, grad_values, part_first, grad_attn, grad_logits, gain_two = backed
     share_first = lax.psum_scatter(part_first, "dp", scatter_dimension=0, tiled=True)
+    part_output = output_grad(attn_low, grad_attn, hn_two, grad_logits, gain_two, experts)
     (part_output,) = sums.step(part_output)
     share_output = lax.psum_scatter(part_output, "dp", scatter_dimension=0, tiled=True)
     share_query, share_keyval = share_first[:, :head_total], share_first[:, head_total:]
@@ -1077,16 +1111,36 @@
     sums.add("query", share_query)
     sums.add("keyval", share_keyval)
     sums.step(take=2)
-    sums.add("output", share_output)
+    gate_up, down = jnp.zeros(w_gate_up.shape, F32), jnp.zeros(w_down.shape, F32)
+    placed = set()
+
+    def place_done(gate_up, down):
+        for e in range(local_experts):
+            for c in range(3):
+                if f"{e}.{c}" not in sums.done or f"{e}.{c}" in placed:
+                    continue
+                placed.add(f"{e}.{c}")
+                part = sums.total(f"{e}.{c}")
+                if c == 0:
+                    part = unpack_down(part, w_down.shape[1])
+                    down = lax.dynamic_update_slice(down, part[None], (e, 0, 0))
+                else:
+                    at = (e, (c - 1) * part.shape[0], 0)
+                    gate_up = lax.dynamic_update_slice(gate_up, part[None], at)
+        return gate_up, down
+
     grad_kv = jnp.concatenate([grad_keys, grad_values], 1)
     blocks = [grad_kv[r * rows : (r + 1) * rows] for r in range(ctx_count)]
     held = blocks[-1]
     for r in range(ctx_count - 2, -1, -1):
         pairs = [(i, i - 1) for i in range(r + 1, ctx_count)]
         held = add_low(lax.ppermute(held, "ctx", pairs), blocks[r])
-        if r:
+        if r == max(ctx_count - 2, 1):
             held, out_tokens = sums.step(held, out_tokens)
-    moe = lax.psum_scatter(out_tokens, "dp", scatter_dimension=0, tiled=True)
+            moe = lax.psum_scatter(out_tokens, "dp", scatter_dimension=0, tiled=True)
+            sums.add("output", share_output)
+        elif r:
+            (held,) = sums.step(held)
 
     grad_hn_one = dot_nt(grad_query, query_w) + dot_nt(held, keyval_w)
     inputs = up(tokens[0])
@@ -1102,20 +1156,14 @@
 
     wanted = [f"{e}.{c}" for e in range(local_experts) for c in range(3)]
     while not all(name in sums.done for name in wanted):
-        sums.step(take=2)
-    gate_up, down = jnp.zeros(w_gate_up.shape, F32), []
-    for e in range(local_experts):
-        chunks = [sums.total(f"{e}.{c}") for c in range(3)]
-        for c, part in enumerate(chunks[1:]):
-            gate_up = lax.dynamic_update_slice(gate_up, part[None], (e, c * part.shape[0], 0))
-        down.append(unpack_down(chunks[0], w_down.shape[1]))
-    down = jnp.stack(down)
+        sums.step()
+    gate_up, down = place_done(gate_up, down)
     gate_up, down, grad_inputs = sums.step(gate_up, down, grad_inputs)
-    if "query" not in sums.done:
+    while not ("query" in sums.done and "keyval" in sums.done):
         sums.step()
     total_query, total_keyval = sums.total("query"), sums.total("keyval")
     ready = (total_query, total_keyval[:, : 2 * kv_width], total_keyval[:, 2 * kv_width])
-    total_query, total_keyval, total_gain = sums.step(*ready)
+    total_query, total_keyval, total_gain, outcome = sums.step(*ready, outcome)
     while sums.busy():
         sums.step()
     total_output = sums.total("output")

time: 621 us -> 606 us (0.976)
  waiting for transfers between devices: 236 us -> 227 us
  starting transfers between devices: 101 us -> 93.3 us
    ppermute x4, waiting for transfers between devices: 85.6 us -> 62.6 us  [step(): back = lax.ppermute(payload, 'ctx', [(0, 1), (1, 0), (2, 3), (3, 2)])]
    ppermute x19, waiting for transfers between devices: 76.8 us -> 96.3 us  [step(): flight.append((kind, name, v, lax.ppermute(v, 'ctx', pairs)))]
    reduce_scatter x1, waiting for transfers between devices: 15 us -> 0.01 us  [per_device(): lax.psum_scatter(part_output, 'dp', scatter_dimension=0, tiled=True)]
    reduce_scatter x1, waiting for transfers between devices: 0.01 us -> 10.3 us  [per_device(): lax.psum_scatter(gin_tokens, 'dp', scatter_dimension=0, tiled=True)]
    ppermute x19, starting transfers between devices: 48.7 us -> 41.3 us  [step(): flight.append((kind, name, v, lax.ppermute(v, 'ctx', pairs)))]
    convert_element_type x18 -> x19, other arithmetic: 27.5 us -> 31.1 us  [low(): return v.astype(BF16)]
  transfers between devices with their start and end apart: 56 -> 56, of which waited for: 25 -> 24; matrix products, arithmetic and copies ran while one was open for 12% -> 12% of each run, Pallas kernels for 20% -> 20%
where the time goes in v3:
time: 606 us; the launch traced here: 597 us
  waiting for transfers between devices  227 us (37%)
  Pallas kernels  150 us (25%)
  starting transfers between devices  93.3 us (15%)
  other arithmetic  66.1 us (11%)
  local copies, waits for them, and re-layouts  39.2 us (6%)
  between operations  16.6 us (3%)
    ppermute x19, waiting for transfers between devices, step(): flight.append((kind, name, v, lax.ppermute(v, 'ctx', pairs)))  96.3 us
    pallas_call x2, Pallas kernels, run_expert(): pl.pallas_call(functools.partial(expert_kernel, counts, cap, tile, e, ear...  68.7 us
    ppermute x4, waiting for transfers between devices, step(): back = lax.ppermute(payload, 'ctx', [(0, 1), (1, 0), (2, 3), (3, 2)])  62.6 us
    ppermute x19, starting transfers between devices, step(): flight.append((kind, name, v, lax.ppermute(v, 'ctx', pairs)))  41.3 us
    ppermute x18, waiting for transfers between devices, swap(): return lax.ppermute(v, 'dp', [(i, i ^ mask) for i in range(count)])  39 us
    convert_element_type x19, other arithmetic, low(): return v.astype(BF16)  31.1 us
    pallas_call x1, Pallas kernels, attend_back(): pl.pallas_call(functools.partial(attend_back_kernel, groups), grid_spec=p...  30 us
    unnamed x156, local copies, waits for them, and re-layouts  25.4 us
  transfers between devices with their start and end apart: 56, of which 24 were waited for; matrix products, arithmetic and copies ran while one was open for 12% of the time, Pallas kernels for 20%

profile of v3, /device:TPU:0, one launch (start us, length us, event | category | flops | bytes accessed | tf_op | source)
XLA Modules:
  0.0 596.7 jit_solution(11735371838814348352)
XLA Ops:
  12.5 3.0 collective-permute-start
  18.3 4.2 collective-permute-start.2
  22.5 3.5 collective-permute-start.3
  31.3 5.2 collective-permute-start.4
  39.7 6.8 %collective-permute-done.4.refs_14_ = bf16[128,1536]{1,0:T(8,128)(2,1)} collective-permute-done((bf16[128,1536]{1,0:T(8,128)(2,1)}, bf16[128,1536]{1,0:T(8,128)(2,1)}, u32[]{:S(2)}, u32[]{:S(2)}) %collective-permute-start.4) | collective-permute-done | bytes 393248 | tf_op jit(solution)/shard_map/ppermute | solution.py:114
  47.4 3.3 collective-permute-done.1.refs_4_
  50.8 2.7 collective-permute-start.5
  54.6 4.1 collective-permute-start.7
  58.7 2.9 collective-permute-start.8
  61.6 4.4 collective-permute-done.7.refs_15_
  66.0 4.2 collective-permute-done.8.a_ref
  72.8 3.7 collective-permute-done.12.refs_8_
  77.3 5.0 collective-permute-start.14
  87.7 11.8 %project.1 = (bf16[256,1536]{1,0:T(8,128)(2,1)S(1)}, bf16[1024,1024]{1,0:T(8,128)(2,1)}, bf16[1024,1536]{1,0:T(8,128)(2,1)}, bf16[1536,1536]{1,0:T(8,128)(2,1)},...) custom-call(s32[1]{0:T(128)} %bitcast.index_ref.number_ref, ...), custom_call_target="tpu_custom_call" | custom-call | flops 276824064 | bytes 1024 | tf_op jit(solution)/shard_map/project/pallas_call | solution.py:279
  102.4 3.0 project_last.1
  105.5 16.9 %attend.1 = (f32[256,1536]{1,0:T(8,128)}, f32[4,8,256]{2,1,0:T(8,128)S(1)}, f32[4,8,256]{2,1,0:T(8,128)S(1)}, f32[256,1536]{1,0:T(8,128)}, bf16[256,1664]{1,0:T(...) custom-call(s32[2]{0:T(128)S(1)} %copy-done.25, bf16[256,1536]{1,0:T(8,128)(2,1)} %copy-done.7, ...), custom_call_target="tpu_custom_call" | custom-call | flops 314572800 | bytes 1024 | tf_op jit(solution)/shard_map/attend/pallas_call | solution.py:545
  124.5 18.7 %collective-permute-done.15.refs_2_ = bf16[256,1664]{1,0:T(8,128)(2,1)S(1)} collective-permute-done((bf16[256,1664]{1,0:T(8,128)(2,1)S(1)}, bf16[256,1664]{1,0:T(8,128)(2,1)S(1)}, u32[]{:S(2)}, u32[]{:S(2)}) %collective-permute-start.15) | collective-permute-done | bytes 852000 | tf_op jit(solution)/shard_map/ppermute | solution.py:55
  146.0 9.1 %collective-permute-done.20.refs_6_ = bf16[128,1664]{1,0:T(8,128)(2,1)S(1)} collective-permute-done((bf16[128,1664]{1,0:T(8,128)(2,1)S(1)}, bf16[128,1664]{1,0:T(8,128)(2,1)S(1)}, u32[]{:S(2)}, u32[]{:S(2)}) %collective-permute-start.20) | collective-permute-done | bytes 426016 | tf_op jit(solution)/shard_map/ppermute | solution.py:55
  157.9 28.4 %expert.2 = (bf16[1152,1536]{1,0:T(8,128)(2,1)}, f32[8,256]{1,0:T(8,128)}, bf16[1152,1664]{1,0:T(8,128)(2,1)}, bf16[768,1024]{1,0:T(8,128)(2,1)}, bf16[768,1024]{1,0:T(8,128)(2,1)}, /*index=5*/bf16[768,1024]{1,0:T(8,128)(2,1)}) custom-call(s32[2]{0:T(128)} %get-tuple-element.424.number_ref, bf16[256,1664]{1,0:T(8,128)(2,1)} %copy-done.4, ...), custom_call_target="tpu_custom_call" | custom-call | flops 622854144 | bytes 1024 | tf_op jit(solution)/shard_map/expert/pallas_call | solution.py:932
  186.4 2.9 collective-permute-start.24
  189.3 40.3 %expert.3 = (bf16[1152,1536]{1,0:T(8,128)(2,1)}, f32[8,256]{1,0:T(8,128)}, bf16[2048,1664]{1,0:T(8,128)(2,1)}, bf16[768,1024]{1,0:T(8,128)(2,1)}, bf16[768,1024]{1,0:T(8,128)(2,1)}, /*index=5*/bf16[768,1024]{1,0:T(8,128)(2,1)}) custom-call(s32[2]{0:T(128)} %get-tuple-element.423.number_ref, bf16[256,1664]{1,0:T(8,128)(2,1)} %copy-done.4, ...), custom_call_target="tpu_custom_call" | custom-call | flops 622854144 | bytes 1024 | tf_op jit(solution)/shard_map/expert/pallas_call | solution.py:932
  234.8 31.1 %collective-permute-done.26 = bf16[768,1024]{1,0:T(8,128)(2,1)} collective-permute-done((bf16[768,1024]{1,0:T(8,128)(2,1)}, bf16[768,1024]{1,0:T(8,128)(2,1)}, u32[]{:S(2)}, u32[]{:S(2)}) %collective-permute-start.26) | collective-permute-done | bytes 1572896 | tf_op jit(solution)/shard_map/ppermute | solution.py:181
  265.9 4.0 add_convert_fusion.9
  270.0 2.7 fusion.9
  272.6 2.5 collective-permute-start.28
  276.9 6.7 %combine.1 = bf16[2048,1536]{1,0:T(8,128)(2,1)} custom-call(s32[1]{0:T(128)} %bitcast.index_ref.number_ref, f32[8,256]{1,0:T(8,128)S(1)} %copy-done.23, f32[8,256]{1,0:T(8,128)S(1)} %copy-done.24, bf16[1152,1536]{1,0:T(8,128)(2,1)S(1)} %copy-done.5, bf16[1152,1536]{1,0:T(8,128)(2,1)S(1)} %copy-done.6), custom_call_target="tpu_custom_call" | custom-call | flops 70778880 | bytes 1024 | tf_op jit(solution)/shard_map/combine/pallas_call | solution.py:970
  283.6 10.3 %reduce-scatter.5.cloned.1.call-done.total_ref = bf16[256,1664]{1,0:T(8,128)(2,1)} async-done(((bf16[2048,1664]{1,0:T(8,128)(2,1)}), bf16[256,1664]{1,0:T(8,128)(2,1)}) %reduce-scatter.5.cloned.1.call-update) | async-done | bytes 851984 | tf_op jit(solution)/shard_map/reduce_scatter | solution.py:1088
  293.9 7.3 %router_back.1 = (f32[256,1536]{1,0:T(8,128)}, f32[256,1536]{1,0:T(8,128)}, bf16[256,1536]{1,0:T(8,128)(2,1)}, bf16[256,128]{1,0:T(8,128)(2,1)}, f32[8,1536]{1,0:T(8,128)}) custom-call(bf16[256,1664]{1,0:T(8,128)(2,1)} %reduce-scatter.5.cloned.1.call-done.total_ref, f32[256,128]{1,0:T(8,128)} %copy-done.20, bf16[1536,128]{1,0:T(8,128)(2,1)} %copy-done.8, ...), custom_call_target="tpu_custom_call" | custom-call | flops 132120576 | bytes 1024 | tf_op jit(solution)/shard_map/router_back/pallas_call | solution.py:421
  301.1 7.9 %collective-permute-done.28 = bf16[768,1024]{1,0:T(8,128)(2,1)} collective-permute-done((bf16[768,1024]{1,0:T(8,128)(2,1)S(1)}, bf16[768,1024]{1,0:T(8,128)(2,1)}, u32[]{:S(2)}, u32[]{:S(2)}) %collective-permute-start.28) | collective-permute-done | bytes 1572896 | tf_op jit(solution)/shard_map/ppermute | solution.py:171
  311.2 2.9 fusion.10
  316.9 30.0 %attend_back.1 = (bf16[256,1536]{1,0:T(8,128)(2,1)S(1)}, bf16[1024,512]{1,0:T(8,128)(2,1)S(1)}, bf16[1024,512]{1,0:T(8,128)(2,1)S(1)}, bf16[1536,2560]{1,0:T(8,128)(2,1)}) custom-call(s32[2]{0:T(128)S(1)} %copy-done.25, bf16[256,1536]{1,0:T(8,128)(2,1)} %copy-done.7, bf16[1024,1024]{1,0:T(8,128)(2,1)} %get-tuple-element.212.k_ref.v_ref, ...), custom_call_target="tpu_custom_call" | custom-call | flops 402653184 | bytes 1024 | tf_op jit(solution)/shard_map/attend_back/pallas_call | solution.py:715
  357.4 5.8 output_grad.1
  363.2 24.8 %collective-permute-done.32 = bf16[768,1024]{1,0:T(8,128)(2,1)} collective-permute-done((bf16[768,1024]{1,0:T(8,128)(2,1)}, bf16[768,1024]{1,0:T(8,128)(2,1)}, u32[]{:S(2)}, u32[]{:S(2)}) %collective-permute-start.32) | collective-permute-done | bytes 1572896 | tf_op jit(solution)/shard_map/ppermute | solution.py:171
  388.0 3.7 add_convert_fusion.3
  391.7 3.7 fusion.12
  396.3 4.3 collective-permute-start.33
  404.1 27.5 %collective-permute-done.33 = bf16[768,1024]{1,0:T(8,128)(2,1)S(1)} collective-permute-done((bf16[768,1024]{1,0:T(8,128)(2,1)}, bf16[768,1024]{1,0:T(8,128)(2,1)S(1)}, u32[]{:S(2)}, u32[]{:S(2)}) %collective-permute-start.33) | collective-permute-done | bytes 1572896 | tf_op jit(solution)/shard_map/ppermute | solution.py:171
  438.9 10.1 %collective-permute-start.36 = (bf16[192,1152]{1,0:T(8,128)(2,1)S(1)}, bf16[192,1152]{1,0:T(8,128)(2,1)S(1)}, u32[]{:S(2)}, u32[]{:S(2)}) collective-permute-start(bf16[192,1152]{1,0:T(8,128)(2,1)S(1)} %pad_maximum_fusion.4), channel_id=1, source_target_pairs={{0,1},{3,2},{4,5},{7,6},{8,9},{11,10},{12,13},{15,14},{16,17},{19,... | collective-permute-start | bytes 1327112 | tf_op jit(solution)/shard_map/ppermute | solution.py:181
  450.3 4.7 collective-permute-start.35
  458.1 4.7 collective-permute-done.35
  465.7 16.7 %collective-permute-done.38 = bf16[768,1024]{1,0:T(8,128)(2,1)S(1)} collective-permute-done((bf16[768,1024]{1,0:T(8,128)(2,1)S(1)}, bf16[768,1024]{1,0:T(8,128)(2,1)S(1)}, u32[]{:S(2)}, u32[]{:S(2)}) %collective-permute-start.38) | collective-permute-done | bytes 1572896 | tf_op jit(solution)/shard_map/ppermute | solution.py:181
  494.1 23.8 %collective-permute-done.42 = bf16[768,1024]{1,0:T(8,128)(2,1)} collective-permute-done((bf16[768,1024]{1,0:T(8,128)(2,1)}, bf16[768,1024]{1,0:T(8,128)(2,1)}, u32[]{:S(2)}, u32[]{:S(2)}) %collective-permute-start.42) | collective-permute-done | bytes 1572896 | tf_op jit(solution)/shard_map/ppermute | solution.py:181
  520.8 2.5 copy-done.44
  525.7 3.3 collective-permute-start.44
  540.3 2.5 convert_dynamic-update-slice_fusion
  543.1 3.5 pad_maximum_fusion
  546.5 5.2 copy-done.27
  566.7 19.9 %collective-permute-done.49 = bf16[192,1664]{1,0:T(8,128)(2,1)S(1)} collective-permute-done((bf16[192,1664]{1,0:T(8,128)(2,1)S(1)}, bf16[192,1664]{1,0:T(8,128)(2,1)S(1)}, u32[]{:S(2)}, u32[]{:S(2)}) %collective-permute-start.49) | collective-permute-done | bytes 639008 | tf_op jit(solution)/shard_map/ppermute | solution.py:181
  (322 shorter events, 123.7 us)
Async XLA Ops:
  7.2 98.3 %all-gather.3.cloned.1.call-start = ((), (), s32[]{:S(2)}) async-start(), calls=%async_computation.4 | async-start | bytes 5308416 | tf_op jit(solution)/shard_map/all_gather | solution.py:1047
  7.9 150.0 %all-gather.5.cloned.1.call-start = ((), (), s32[]{:S(2)}) async-start(), calls=%async_computation.5 | async-start | bytes 7667712 | tf_op jit(solution)/shard_map/all_gather | solution.py:1049
  12.5 34.8 %collective-permute-start = (bf16[192,2688]{1,0:T(8,128)(2,1)S(1)}, bf16[192,2688]{1,0:T(8,128)(2,1)S(1)}, u32[]{:S(2)}, u32[]{:S(2)}) collective-permute-start(bf16[192,2688]{1,0:T(8,128)(2,1)S(1)} %concatenate.31.refs_0_), channel_id=1, source_target_pairs={{0,8},{4,12},{8,0},{12,4},{16,24},{20,28},{24,16},{28,20},{1,9},{5... | collective-permute-start | bytes 3096584 | tf_op jit(solution)/shard_map/ppermute | solution.py:55
  15.5 35.2 %collective-permute-start.1 = (bf16[192,2688]{1,0:T(8,128)(2,1)S(1)}, bf16[192,2688]{1,0:T(8,128)(2,1)}, u32[]{:S(2)}, u32[]{:S(2)}) collective-permute-start(bf16[192,2688]{1,0:T(8,128)(2,1)S(1)} %concatenate.31.refs_0_), channel_id=1, source_target_pairs={{0,16},{4,20},{8,24},{12,28},{16,0},{20,4},{24,8},{28,12},{1,17},{... | collective-permute-start | bytes 3096584 | tf_op jit(solution)/shard_map/ppermute | solution.py:55
  18.3 13.0 %collective-permute-start.2 = (bf16[128,1536]{1,0:T(8,128)(2,1)S(1)}, bf16[128,1536]{1,0:T(8,128)(2,1)}, u32[]{:S(2)}, u32[]{:S(2)}) collective-permute-start(bf16[128,1536]{1,0:T(8,128)(2,1)S(1)} %get-tuple-element.417.refs_10_), channel_id=1, source_target_pairs={{0,1},{1,2},{2,3},{4,5},{5,6},{6,7},{8,9},{9,10},{10,11},{12,13},{... | collective-permute-start | bytes 1179656 | tf_op jit(solution)/shard_map/ppermute | solution.py:114
  22.5 17.2 %collective-permute-start.3 = (bf16[128,1536]{1,0:T(8,128)(2,1)S(1)}, bf16[128,1536]{1,0:T(8,128)(2,1)}, u32[]{:S(2)}, u32[]{:S(2)}) collective-permute-start(bf16[128,1536]{1,0:T(8,128)(2,1)S(1)} %get-tuple-element.416.refs_11_), channel_id=1, source_target_pairs={{0,1},{1,2},{2,3},{4,5},{5,6},{6,7},{8,9},{9,10},{10,11},{12,13},{... | collective-permute-start | bytes 1179656 | tf_op jit(solution)/shard_map/ppermute | solution.py:114
  31.3 15.2 %collective-permute-start.4 = (bf16[128,1536]{1,0:T(8,128)(2,1)}, bf16[128,1536]{1,0:T(8,128)(2,1)}, u32[]{:S(2)}, u32[]{:S(2)}) collective-permute-start(bf16[128,1536]{1,0:T(8,128)(2,1)} %collective-permute-done.2.refs_12_), channel_id=1, source_target_pairs={{0,1},{1,2},{2,3},{4,5},{5,6},{6,7},{8,9},{9,10},{10,11},{12,13},{... | collective-permute-start | bytes 1179656 | tf_op jit(solution)/shard_map/ppermute | solution.py:114
  50.7 243.2 %reduce-scatter.5.cloned.1.call-start = ((), (), s32[]{:S(2)}) async-start(), calls=%async_computation.6 | async-start | bytes 7667712 | tf_op jit(solution)/shard_map/reduce_scatter | solution.py:1088
  50.8 20.1 %collective-permute-start.5 = (bf16[96,2688]{1,0:T(8,128)(2,1)S(1)}, bf16[96,2688]{1,0:T(8,128)(2,1)S(1)}, u32[]{:S(2)}, u32[]{:S(2)}) collective-permute-start(bf16[96,2688]{1,0:T(8,128)(2,1)S(1)} %slice.82), channel_id=1, source_target_pairs={{0,16},{4,20},{8,24},{12,28},{16,0},{20,4},{24,8},{28,12},{1,17},{... | collective-permute-start | bytes 1548296 | tf_op jit(solution)/shard_map/ppermute | solution.py:55
  54.6 16.4 %collective-permute-start.6 = (bf16[96,2688]{1,0:T(8,128)(2,1)S(1)}, bf16[96,2688]{1,0:T(8,128)(2,1)}, u32[]{:S(2)}, u32[]{:S(2)}) collective-permute-start(bf16[96,2688]{1,0:T(8,128)(2,1)S(1)} %slice.83), channel_id=1, source_target_pairs={{0,8},{4,12},{8,0},{12,4},{16,24},{20,28},{24,16},{28,20},{1,9},{5... | collective-permute-start | bytes 1548296 | tf_op jit(solution)/shard_map/ppermute | solution.py:55
  54.6 11.3 %collective-permute-start.7 = (bf16[128,1536]{1,0:T(8,128)(2,1)}, bf16[128,1536]{1,0:T(8,128)(2,1)}, u32[]{:S(2)}, u32[]{:S(2)}) collective-permute-start(bf16[128,1536]{1,0:T(8,128)(2,1)} %collective-permute-done.3.refs_13_), channel_id=1, source_target_pairs={{0,1},{1,2},{2,3},{4,5},{5,6},{6,7},{8,9},{9,10},{10,11},{12,13},{... | collective-permute-start | bytes 1179656 | tf_op jit(solution)/shard_map/ppermute | solution.py:114
  58.7 11.5 %collective-permute-start.8 = (bf16[128,1536]{1,0:T(8,128)(2,1)}, bf16[128,1536]{1,0:T(8,128)(2,1)S(1)}, u32[]{:S(2)}, u32[]{:S(2)}) collective-permute-start(bf16[128,1536]{1,0:T(8,128)(2,1)} %collective-permute-done.4.refs_14_), channel_id=1, source_target_pairs={{0,1},{1,2},{2,3},{4,5},{5,6},{6,7},{8,9},{9,10},{10,11},{12,13},{... | collective-permute-start | bytes 1179656 | tf_op jit(solution)/shard_map/ppermute | solution.py:114
  70.9 12.6 %collective-permute-start.10 = (bf16[192,2688]{1,0:T(8,128)(2,1)S(1)}, bf16[192,2688]{1,0:T(8,128)(2,1)}, u32[]{:S(2)}, u32[]{:S(2)}) collective-permute-start(bf16[192,2688]{1,0:T(8,128)(2,1)S(1)} %collective-permute-done.refs_2_), channel_id=1, source_target_pairs={{0,4},{4,0},{8,12},{12,8},{16,20},{20,16},{24,28},{28,24},{1,5},{5... | collective-permute-start | bytes 3096584 | tf_op jit(solution)/shard_map/ppermute | solution.py:55
  70.9 12.6 %collective-permute-start.11 = (bf16[192,2688]{1,0:T(8,128)(2,1)}, bf16[192,2688]{1,0:T(8,128)(2,1)}, u32[]{:S(2)}, u32[]{:S(2)}) collective-permute-start(bf16[192,2688]{1,0:T(8,128)(2,1)} %collective-permute-done.1.refs_4_), channel_id=1, source_target_pairs={{0,4},{4,0},{8,12},{12,8},{16,20},{20,16},{24,28},{28,24},{1,5},{5... | collective-permute-start | bytes 3096584 | tf_op jit(solution)/shard_map/ppermute | solution.py:55
  71.4 12.1 %collective-permute-start.9 = (bf16[192,2688]{1,0:T(8,128)(2,1)S(1)}, bf16[192,2688]{1,0:T(8,128)(2,1)}, u32[]{:S(2)}, u32[]{:S(2)}) collective-permute-start(bf16[192,2688]{1,0:T(8,128)(2,1)S(1)} %concatenate.31.refs_0_), channel_id=1, source_target_pairs={{0,4},{4,0},{8,12},{12,8},{16,20},{20,16},{24,28},{28,24},{1,5},{5... | collective-permute-start | bytes 3096584 | tf_op jit(solution)/shard_map/ppermute | solution.py:55
  72.7 10.8 %collective-permute-start.13 = (bf16[96,2688]{1,0:T(8,128)(2,1)}, bf16[96,2688]{1,0:T(8,128)(2,1)}, u32[]{:S(2)}, u32[]{:S(2)}) collective-permute-start(bf16[96,2688]{1,0:T(8,128)(2,1)} %collective-permute-done.6.refs_7_), channel_id=1, source_target_pairs={{0,4},{4,0},{8,12},{12,8},{16,20},{20,16},{24,28},{28,24},{1,5},{5... | collective-permute-start | bytes 1548296 | tf_op jit(solution)/shard_map/ppermute | solution.py:55
  77.3 23.1 %collective-permute-start.14 = (bf16[128,1536]{1,0:T(8,128)(2,1)}, bf16[128,1536]{1,0:T(8,128)(2,1)}, u32[]{:S(2)}, u32[]{:S(2)}) collective-permute-start(bf16[128,1536]{1,0:T(8,128)(2,1)} %collective-permute-done.7.refs_15_), channel_id=1, source_target_pairs={{0,1},{1,2},{2,3},{4,5},{5,6},{6,7},{8,9},{9,10},{10,11},{12,13},{... | collective-permute-start | bytes 1179656 | tf_op jit(solution)/shard_map/ppermute | solution.py:114
  122.4 20.8 %collective-permute-start.15 = (bf16[256,1664]{1,0:T(8,128)(2,1)S(1)}, bf16[256,1664]{1,0:T(8,128)(2,1)S(1)}, u32[]{:S(2)}, u32[]{:S(2)}) collective-permute-start(bf16[256,1664]{1,0:T(8,128)(2,1)S(1)} %get-tuple-element.220.refs_0_.hn_ref), channel_id=1, source_target_pairs={{0,8},{4,12},{8,0},{12,4},{16,24},{20,28},{24,16},{28,20},{1,9},{5... | collective-permute-start | bytes 2555912 | tf_op jit(solution)/shard_map/ppermute | solution.py:55
  124.2 20.4 %collective-permute-start.16 = (bf16[256,1664]{1,0:T(8,128)(2,1)S(1)}, bf16[256,1664]{1,0:T(8,128)(2,1)S(1)}, u32[]{:S(2)}, u32[]{:S(2)}) collective-permute-start(bf16[256,1664]{1,0:T(8,128)(2,1)S(1)} %get-tuple-element.220.refs_0_.hn_ref), channel_id=1, source_target_pairs={{0,16},{4,20},{8,24},{12,28},{16,0},{20,4},{24,8},{28,12},{1,17},{... | collective-permute-start | bytes 2555912 | tf_op jit(solution)/shard_map/ppermute | solution.py:55
  144.7 10.4 %collective-permute-start.20 = (bf16[128,1664]{1,0:T(8,128)(2,1)S(1)}, bf16[128,1664]{1,0:T(8,128)(2,1)S(1)}, u32[]{:S(2)}, u32[]{:S(2)}) collective-permute-start(bf16[128,1664]{1,0:T(8,128)(2,1)S(1)} %slice.84), channel_id=1, source_target_pairs={{0,16},{4,20},{8,24},{12,28},{16,0},{20,4},{24,8},{28,12},{1,17},{... | collective-permute-start | bytes 1277960 | tf_op jit(solution)/shard_map/ppermute | solution.py:55
  145.1 10.3 %collective-permute-start.21 = (bf16[128,1664]{1,0:T(8,128)(2,1)S(1)}, bf16[128,1664]{1,0:T(8,128)(2,1)}, u32[]{:S(2)}, u32[]{:S(2)}) collective-permute-start(bf16[128,1664]{1,0:T(8,128)(2,1)S(1)} %slice.85), channel_id=1, source_target_pairs={{0,8},{4,12},{8,0},{12,4},{16,24},{20,28},{24,16},{28,20},{1,9},{5... | collective-permute-start | bytes 1277960 | tf_op jit(solution)/shard_map/ppermute | solution.py:55
  145.5 12.4 %collective-permute-start.17 = (bf16[256,1664]{1,0:T(8,128)(2,1)S(1)}, bf16[256,1664]{1,0:T(8,128)(2,1)}, u32[]{:S(2)}, u32[]{:S(2)}) collective-permute-start(bf16[256,1664]{1,0:T(8,128)(2,1)S(1)} %get-tuple-element.220.refs_0_.hn_ref), channel_id=1, source_target_pairs={{0,4},{4,0},{8,12},{12,8},{16,20},{20,16},{24,28},{28,24},{1,5},{5... | collective-permute-start | bytes 2555912 | tf_op jit(solution)/shard_map/ppermute | solution.py:55
  145.5 12.4 %collective-permute-start.18 = (bf16[256,1664]{1,0:T(8,128)(2,1)S(1)}, bf16[256,1664]{1,0:T(8,128)(2,1)}, u32[]{:S(2)}, u32[]{:S(2)}) collective-permute-start(bf16[256,1664]{1,0:T(8,128)(2,1)S(1)} %collective-permute-done.15.refs_2_), channel_id=1, source_target_pairs={{0,4},{4,0},{8,12},{12,8},{16,20},{20,16},{24,28},{28,24},{1,5},{5... | collective-permute-start | bytes 2555912 | tf_op jit(solution)/shard_map/ppermute | solution.py:55
  146.0 11.8 %collective-permute-start.19 = (bf16[256,1664]{1,0:T(8,128)(2,1)S(1)}, bf16[256,1664]{1,0:T(8,128)(2,1)}, u32[]{:S(2)}, u32[]{:S(2)}) collective-permute-start(bf16[256,1664]{1,0:T(8,128)(2,1)S(1)} %collective-permute-done.16.refs_4_), channel_id=1, source_target_pairs={{0,4},{4,0},{8,12},{12,8},{16,20},{20,16},{24,28},{28,24},{1,5},{5... | collective-permute-start | bytes 2555912 | tf_op jit(solution)/shard_map/ppermute | solution.py:55
  186.4 43.2 %collective-permute-start.24 = (bf16[768,1024]{1,0:T(8,128)(2,1)}, bf16[768,1024]{1,0:T(8,128)(2,1)S(1)}, u32[]{:S(2)}, u32[]{:S(2)}) collective-permute-start(bf16[768,1024]{1,0:T(8,128)(2,1)} %get-tuple-element.237), channel_id=1, source_target_pairs={{0,1},{3,2},{4,5},{7,6},{8,9},{11,10},{12,13},{15,14},{16,17},{19,... | collective-permute-start | bytes 4718600 | tf_op jit(solution)/shard_map/ppermute | solution.py:181
  230.3 204.5 %reduce-scatter.9.cloned.1.call-start = ((), (), s32[]{:S(2)}) async-start(), calls=%async_computation.8 | async-start | bytes 8847360 | tf_op jit(solution)/shard_map/reduce_scatter | solution.py:1101
  230.3 35.5 %collective-permute-start.26 = (bf16[768,1024]{1,0:T(8,128)(2,1)}, bf16[768,1024]{1,0:T(8,128)(2,1)}, u32[]{:S(2)}, u32[]{:S(2)}) collective-permute-start(bf16[768,1024]{1,0:T(8,128)(2,1)} %get-tuple-element.240), channel_id=1, source_target_pairs={{0,1},{3,2},{4,5},{7,6},{8,9},{11,10},{12,13},{15,14},{16,17},{19,... | collective-permute-start | bytes 4718600 | tf_op jit(solution)/shard_map/ppermute | solution.py:181
  232.8 37.1 %collective-permute-start.25 = (bf16[768,1024]{1,0:T(8,128)(2,1)S(1)}, bf16[768,1024]{1,0:T(8,128)(2,1)}, u32[]{:S(2)}, u32[]{:S(2)}) collective-permute-start(bf16[768,1024]{1,0:T(8,128)(2,1)S(1)} %add_convert_fusion.11), channel_id=1, source_target_pairs={{1,2},{2,1},{5,6},{6,5},{9,10},{10,9},{13,14},{14,13},{17,18},{18,... | collective-permute-start | bytes 4718600 | tf_op jit(solution)/shard_map/ppermute | solution.py:181
  272.6 36.5 %collective-permute-start.28 = (bf16[768,1024]{1,0:T(8,128)(2,1)S(1)}, bf16[768,1024]{1,0:T(8,128)(2,1)}, u32[]{:S(2)}, u32[]{:S(2)}) collective-permute-start(bf16[768,1024]{1,0:T(8,128)(2,1)S(1)} %fusion.9), channel_id=1, source_target_pairs={{0,1},{1,0},{2,3},{3,2},{4,5},{5,4},{6,7},{7,6},{8,9},{9,8},{10,11... | collective-permute-start | bytes 4718600 | tf_op jit(solution)/shard_map/ppermute | solution.py:171
  275.1 36.1 %collective-permute-start.27 = (bf16[768,1024]{1,0:T(8,128)(2,1)}, bf16[768,1024]{1,0:T(8,128)(2,1)}, u32[]{:S(2)}, u32[]{:S(2)}) collective-permute-start(bf16[768,1024]{1,0:T(8,128)(2,1)} %add_convert_fusion.9), channel_id=1, source_target_pairs={{1,2},{2,1},{5,6},{6,5},{9,10},{10,9},{13,14},{14,13},{17,18},{18,... | collective-permute-start | bytes 4718600 | tf_op jit(solution)/shard_map/ppermute | solution.py:181
  314.2 35.1 %collective-permute-start.30 = (bf16[768,1024]{1,0:T(8,128)(2,1)S(1)}, bf16[768,1024]{1,0:T(8,128)(2,1)S(1)}, u32[]{:S(2)}, u32[]{:S(2)}) collective-permute-start(bf16[768,1024]{1,0:T(8,128)(2,1)S(1)} %fusion.10), channel_id=1, source_target_pairs={{0,1},{1,0},{2,3},{3,2},{4,5},{5,4},{6,7},{7,6},{8,9},{9,8},{10,11... | collective-permute-start | bytes 4718600 | tf_op jit(solution)/shard_map/ppermute | solution.py:171
  316.0 35.1 %collective-permute-start.29 = (bf16[768,1024]{1,0:T(8,128)(2,1)S(1)}, bf16[768,1024]{1,0:T(8,128)(2,1)S(1)}, u32[]{:S(2)}, u32[]{:S(2)}) collective-permute-start(bf16[768,1024]{1,0:T(8,128)(2,1)S(1)} %add_convert_fusion.7), channel_id=1, source_target_pairs={{1,2},{2,1},{5,6},{6,5},{9,10},{10,9},{13,14},{14,13},{17,18},{18,... | collective-permute-start | bytes 4718600 | tf_op jit(solution)/shard_map/ppermute | solution.py:181
  353.4 140.7 %reduce-scatter.7.cloned.1.call-start = ((), (), s32[]{:S(2)}) async-start(), calls=%async_computation.7 | async-start | bytes 5750784 | tf_op jit(solution)/shard_map/reduce_scatter | solution.py:1104
  353.5 34.5 %collective-permute-start.32 = (bf16[768,1024]{1,0:T(8,128)(2,1)}, bf16[768,1024]{1,0:T(8,128)(2,1)}, u32[]{:S(2)}, u32[]{:S(2)}) collective-permute-start(bf16[768,1024]{1,0:T(8,128)(2,1)} %fusion.11), channel_id=1, source_target_pairs={{0,1},{1,0},{2,3},{3,2},{4,5},{5,4},{6,7},{7,6},{8,9},{9,8},{10,11... | collective-permute-start | bytes 4718600 | tf_op jit(solution)/shard_map/ppermute | solution.py:171
  355.3 36.4 %collective-permute-start.31 = (bf16[768,1024]{1,0:T(8,128)(2,1)}, bf16[768,1024]{1,0:T(8,128)(2,1)}, u32[]{:S(2)}, u32[]{:S(2)}) collective-permute-start(bf16[768,1024]{1,0:T(8,128)(2,1)} %add_convert_fusion.5), channel_id=1, source_target_pairs={{1,2},{2,1},{5,6},{6,5},{9,10},{10,9},{13,14},{14,13},{17,18},{18,... | collective-permute-start | bytes 4718600 | tf_op jit(solution)/shard_map/ppermute | solution.py:181
  395.5 167.7 %reduce-scatter.11.cloned.1.call-start = ((), (), s32[]{:S(2)}) async-start(), calls=%async_computation.9 | async-start | bytes 7077888 | tf_op jit(solution)/shard_map/reduce_scatter | solution.py:1140
  396.3 35.4 %collective-permute-start.33 = (bf16[768,1024]{1,0:T(8,128)(2,1)}, bf16[768,1024]{1,0:T(8,128)(2,1)S(1)}, u32[]{:S(2)}, u32[]{:S(2)}) collective-permute-start(bf16[768,1024]{1,0:T(8,128)(2,1)} %fusion.12), channel_id=1, source_target_pairs={{0,1},{1,0},{2,3},{3,2},{4,5},{5,4},{6,7},{7,6},{8,9},{9,8},{10,11... | collective-permute-start | bytes 4718600 | tf_op jit(solution)/shard_map/ppermute | solution.py:171
  401.8 53.2 %collective-permute-start.39 = (bf16[256,1024]{1,0:T(8,128)(2,1)}, bf16[256,1024]{1,0:T(8,128)(2,1)}, u32[]{:S(2)}, u32[]{:S(2)}) collective-permute-start(bf16[256,1024]{1,0:T(8,128)(2,1)} %slice.106), channel_id=1, source_target_pairs={{3,2},{7,6},{11,10},{15,14},{19,18},{23,22},{27,26},{31,30}} | collective-permute-start | bytes 1572872 | tf_op jit(solution)/shard_map/ppermute | solution.py:1137
  438.1 25.6 %collective-permute-start.37 = (bf16[768,1024]{1,0:T(8,128)(2,1)S(1)}, bf16[768,1024]{1,0:T(8,128)(2,1)S(1)}, u32[]{:S(2)}, u32[]{:S(2)}) collective-permute-start(bf16[768,1024]{1,0:T(8,128)(2,1)S(1)} %copy-done.50), channel_id=1, source_target_pairs={{1,2},{2,1},{5,6},{6,5},{9,10},{10,9},{13,14},{14,13},{17,18},{18,... | collective-permute-start | bytes 4718600 | tf_op jit(solution)/shard_map/ppermute | solution.py:181
  438.9 18.3 %collective-permute-start.36 = (bf16[192,1152]{1,0:T(8,128)(2,1)S(1)}, bf16[192,1152]{1,0:T(8,128)(2,1)S(1)}, u32[]{:S(2)}, u32[]{:S(2)}) collective-permute-start(bf16[192,1152]{1,0:T(8,128)(2,1)S(1)} %pad_maximum_fusion.4), channel_id=1, source_target_pairs={{0,1},{3,2},{4,5},{7,6},{8,9},{11,10},{12,13},{15,14},{16,17},{19,... | collective-permute-start | bytes 1327112 | tf_op jit(solution)/shard_map/ppermute | solution.py:181
  449.0 33.3 %collective-permute-start.38 = (bf16[768,1024]{1,0:T(8,128)(2,1)S(1)}, bf16[768,1024]{1,0:T(8,128)(2,1)S(1)}, u32[]{:S(2)}, u32[]{:S(2)}) collective-permute-start(bf16[768,1024]{1,0:T(8,128)(2,1)S(1)} %add_convert_fusion.1), channel_id=1, source_target_pairs={{1,0},{2,3},{5,4},{6,7},{9,8},{10,11},{13,12},{14,15},{17,16},{18,... | collective-permute-start | bytes 4718600 | tf_op jit(solution)/shard_map/ppermute | solution.py:181
  450.3 12.5 %collective-permute-start.35 = (bf16[192,1536]{1,0:T(8,128)(2,1)S(1)}, bf16[192,1536]{1,0:T(8,128)(2,1)S(1)}, u32[]{:S(2)}, u32[]{:S(2)}) collective-permute-start(bf16[192,1536]{1,0:T(8,128)(2,1)S(1)} %slice.104), channel_id=1, source_target_pairs={{0,1},{3,2},{4,5},{7,6},{8,9},{11,10},{12,13},{15,14},{16,17},{19,... | collective-permute-start | bytes 1769480 | tf_op jit(solution)/shard_map/ppermute | solution.py:181
  483.3 34.6 %collective-permute-start.42 = (bf16[768,1024]{1,0:T(8,128)(2,1)}, bf16[768,1024]{1,0:T(8,128)(2,1)}, u32[]{:S(2)}, u32[]{:S(2)}) collective-permute-start(bf16[768,1024]{1,0:T(8,128)(2,1)} %add_convert_fusion), channel_id=1, source_target_pairs={{1,0},{2,3},{5,4},{6,7},{9,8},{10,11},{13,12},{14,15},{17,16},{18,... | collective-permute-start | bytes 4718600 | tf_op jit(solution)/shard_map/ppermute | solution.py:181
  517.9 33.9 %collective-permute-start.47 = (bf16[256,1024]{1,0:T(8,128)(2,1)}, bf16[256,1024]{1,0:T(8,128)(2,1)}, u32[]{:S(2)}, u32[]{:S(2)}) collective-permute-start(bf16[256,1024]{1,0:T(8,128)(2,1)} %add_convert_fusion.17), channel_id=1, source_target_pairs={{1,0},{2,1},{3,2},{5,4},{6,5},{7,6},{9,8},{10,9},{11,10},{13,12},{... | collective-permute-start | bytes 1572872 | tf_op jit(solution)/shard_map/ppermute | solution.py:1137
  525.7 31.3 %collective-permute-start.44 = (bf16[192,1664]{1,0:T(8,128)(2,1)S(1)}, bf16[192,1664]{1,0:T(8,128)(2,1)S(1)}, u32[]{:S(2)}, u32[]{:S(2)}) collective-permute-start(bf16[192,1664]{1,0:T(8,128)(2,1)S(1)} %copy-done.69), channel_id=1, source_target_pairs={{0,1},{3,2},{4,5},{7,6},{8,9},{11,10},{12,13},{15,14},{16,17},{19,... | collective-permute-start | bytes 1916936 | tf_op jit(solution)/shard_map/ppermute | solution.py:181
  529.0 28.1 %collective-permute-start.46 = (bf16[192,1536]{1,0:T(8,128)(2,1)S(1)}, bf16[192,1536]{1,0:T(8,128)(2,1)}, u32[]{:S(2)}, u32[]{:S(2)}) collective-permute-start(bf16[192,1536]{1,0:T(8,128)(2,1)S(1)} %copy-done.59), channel_id=1, source_target_pairs={{1,0},{2,3},{5,4},{6,7},{9,8},{10,11},{13,12},{14,15},{17,16},{18,... | collective-permute-start | bytes 1769480 | tf_op jit(solution)/shard_map/ppermute | solution.py:181
  530.3 26.8 %collective-permute-start.45 = (bf16[192,1152]{1,0:T(8,128)(2,1)S(1)}, bf16[192,1152]{1,0:T(8,128)(2,1)}, u32[]{:S(2)}, u32[]{:S(2)}) collective-permute-start(bf16[192,1152]{1,0:T(8,128)(2,1)S(1)} %copy-done.61), channel_id=1, source_target_pairs={{1,0},{2,3},{5,4},{6,7},{9,8},{10,11},{13,12},{14,15},{17,16},{18,... | collective-permute-start | bytes 1327112 | tf_op jit(solution)/shard_map/ppermute | solution.py:181
  565.4 21.2 %collective-permute-start.49 = (bf16[192,1664]{1,0:T(8,128)(2,1)S(1)}, bf16[192,1664]{1,0:T(8,128)(2,1)S(1)}, u32[]{:S(2)}, u32[]{:S(2)}) collective-permute-start(bf16[192,1664]{1,0:T(8,128)(2,1)S(1)} %add_convert_fusion.12), channel_id=1, source_target_pairs={{1,0},{2,3},{5,4},{6,7},{9,8},{10,11},{13,12},{14,15},{17,16},{18,... | collective-permute-start | bytes 1916936 | tf_op jit(solution)/shard_map/ppermute | solution.py:181
  (87 other events, 1026.5 us)
Sparse Core Ops, SparseCore 0:
  9.9 57.9 all-gather.2
  70.3 48.3 all-gather.4
  230.4 63.4 reduce-scatter.4
  353.6 68.8 reduce-scatter.8
  426.4 55.7 reduce-scatter.6
  487.8 64.9 reduce-scatter.10

commit v4 on v3

--- a/solution.py
+++ b/solution.py
@@ -181,6 +181,13 @@
                 flight.append((kind, name, v, lax.ppermute(v, "ctx", pairs)))
         self.flights.append(flight)
         return critical
+
+    def launch(self, name, v):
+        if self.plain:
+            self.add(name, v)
+        else:
+            got = lax.ppermute(v, "ctx", [(0, 1), (3, 2)])
+            self.flights[-1].append(("first", name, v, got))
 
     def hold(self, *critical):
         if self.plain:
@@ -1108,9 +1115,9 @@
     )
     gain_grad = jnp.broadcast_to(gain_grad / up(gain_attn)[:, None], (w_query.shape[0], SIDE))
     share_keyval = jnp.concatenate([share_keyval, low(gain_grad)], 1)
-    sums.add("query", share_query)
-    sums.add("keyval", share_keyval)
-    sums.step(take=2)
+    sums.step()
+    sums.launch("query", share_query)
+    sums.launch("keyval", share_keyval)
     gate_up, down = jnp.zeros(w_gate_up.shape, F32), jnp.zeros(w_down.shape, F32)
     placed = set()
 
@@ -1158,12 +1165,12 @@
     while not all(name in sums.done for name in wanted):
         sums.step()
     gate_up, down = place_done(gate_up, down)
-    gate_up, down, grad_inputs = sums.step(gate_up, down, grad_inputs)
     while not ("query" in sums.done and "keyval" in sums.done):
         sums.step()
     total_query, total_keyval = sums.total("query"), sums.total("keyval")
     ready = (total_query, total_keyval[:, : 2 * kv_width], total_keyval[:, 2 * kv_width])
-    total_query, total_keyval, total_gain, outcome = sums.step(*ready, outcome)
+    ready = sums.step(*ready, outcome, gate_up, down, grad_inputs)
+    total_query, total_keyval, total_gain, outcome, gate_up, down, grad_inputs = ready
     while sums.busy():
         sums.step()
     total_output = sums.total("output")

time: 606 us -> 604 us (level)
    ppermute x4, waiting for transfers between devices: 62.6 us -> 35.1 us  [step(): back = lax.ppermute(payload, 'ctx', [(0, 1), (1, 0), (2, 3), (3, 2)])]
    ppermute x0 -> x2, starting transfers between devices: none -> 20.3 us  [launch(): got = lax.ppermute(v, 'ctx', [(0, 1), (3, 2)])]
    reduce_scatter x1, waiting for transfers between devices: 0.01 us -> 18.5 us  [per_device(): lax.psum_scatter(part_first, 'dp', scatter_dimension=0, tiled=True)]
    ppermute x19 -> x17, starting transfers between devices: 41.3 us -> 25.1 us  [step(): flight.append((kind, name, v, lax.ppermute(v, 'ctx', pairs)))]
    unnamed x156 -> x146, local copies, waits for them, and re-layouts: 25.4 us -> 23.7 us
    ppermute x19 -> x17, waiting for transfers between devices: 96.3 us -> 95.4 us  [step(): flight.append((kind, name, v, lax.ppermute(v, 'ctx', pairs)))]
    convert_element_type x19 -> x18, other arithmetic: 31.1 us -> 30.4 us  [low(): return v.astype(BF16)]
  transfers between devices with their start and end apart: 56 -> 56, of which waited for: 24 -> 25; matrix products, arithmetic and copies ran while one was open for 12% -> 12% of each run, Pallas kernels for 20% -> 21%
where the time goes in v4:
time: 604 us; the launch traced here: 593 us
  waiting for transfers between devices  221 us (37%)
  Pallas kernels  150 us (25%)
  starting transfers between devices  96.7 us (16%)
  other arithmetic  67.3 us (11%)
  local copies, waits for them, and re-layouts  36.5 us (6%)
  between operations  16.7 us (3%)
    ppermute x17, waiting for transfers between devices, step(): flight.append((kind, name, v, lax.ppermute(v, 'ctx', pairs)))  95.4 us
    pallas_call x2, Pallas kernels, run_expert(): pl.pallas_call(functools.partial(expert_kernel, counts, cap, tile, e, ear...  68.7 us
    ppermute x18, waiting for transfers between devices, swap(): return lax.ppermute(v, 'dp', [(i, i ^ mask) for i in range(count)])  39.1 us
    ppermute x4, waiting for transfers between devices, step(): back = lax.ppermute(payload, 'ctx', [(0, 1), (1, 0), (2, 3), (3, 2)])  35.1 us
    convert_element_type x18, other arithmetic, low(): return v.astype(BF16)  30.4 us
    pallas_call x1, Pallas kernels, attend_back(): pl.pallas_call(functools.partial(attend_back_kernel, groups), grid_spec=p...  30 us
    ppermute x17, starting transfers between devices, step(): flight.append((kind, name, v, lax.ppermute(v, 'ctx', pairs)))  25.1 us
    ppermute x6, starting transfers between devices, shift(): lax.ppermute(v, 'ctx', [(i, i + step) for i in range(count) if 0 <= i + s...  24.9 us
  transfers between devices with their start and end apart: 56, of which 25 were waited for; matrix products, arithmetic and copies ran while one was open for 12% of the time, Pallas kernels for 21%

profile of v4, /device:TPU:0, one launch (start us, length us, event | category | flops | bytes accessed | tf_op | source)
XLA Modules:
  0.0 592.6 jit_solution(1315912315094983036)
XLA Ops:
  12.5 3.0 collective-permute-start
  18.3 4.3 collective-permute-start.2
  22.5 3.5 collective-permute-start.3
  31.3 5.2 collective-permute-start.4
  39.7 6.8 %collective-permute-done.4.refs_14_ = bf16[128,1536]{1,0:T(8,128)(2,1)} collective-permute-done((bf16[128,1536]{1,0:T(8,128)(2,1)}, bf16[128,1536]{1,0:T(8,128)(2,1)}, u32[]{:S(2)}, u32[]{:S(2)}) %collective-permute-start.4) | collective-permute-done | bytes 393248 | tf_op jit(solution)/shard_map/ppermute | solution.py:114
  47.4 3.3 collective-permute-done.1.refs_4_
  50.8 2.7 collective-permute-start.5
  54.6 4.1 collective-permute-start.7
  58.7 2.8 collective-permute-start.8
  61.6 4.4 collective-permute-done.7.refs_15_
  66.0 4.2 collective-permute-done.8.a_ref
  72.8 3.7 collective-permute-done.12.refs_8_
  77.3 5.0 collective-permute-start.14
  87.7 11.8 %project.1 = (bf16[256,1536]{1,0:T(8,128)(2,1)S(1)}, bf16[1024,1024]{1,0:T(8,128)(2,1)}, bf16[1024,1536]{1,0:T(8,128)(2,1)}, bf16[1536,1536]{1,0:T(8,128)(2,1)},...) custom-call(s32[1]{0:T(128)} %bitcast.index_ref.number_ref, ...), custom_call_target="tpu_custom_call" | custom-call | flops 276824064 | bytes 1024 | tf_op jit(solution)/shard_map/project/pallas_call | solution.py:286
  102.4 3.0 project_last.1
  105.5 16.9 %attend.1 = (f32[256,1536]{1,0:T(8,128)}, f32[4,8,256]{2,1,0:T(8,128)S(1)}, f32[4,8,256]{2,1,0:T(8,128)S(1)}, f32[256,1536]{1,0:T(8,128)}, bf16[256,1664]{1,0:T(...) custom-call(s32[2]{0:T(128)S(1)} %copy-done.25, bf16[256,1536]{1,0:T(8,128)(2,1)} %copy-done.7, ...), custom_call_target="tpu_custom_call" | custom-call | flops 314572800 | bytes 1024 | tf_op jit(solution)/shard_map/attend/pallas_call | solution.py:552
  124.5 18.7 %collective-permute-done.15.refs_2_ = bf16[256,1664]{1,0:T(8,128)(2,1)S(1)} collective-permute-done((bf16[256,1664]{1,0:T(8,128)(2,1)S(1)}, bf16[256,1664]{1,0:T(8,128)(2,1)S(1)}, u32[]{:S(2)}, u32[]{:S(2)}) %collective-permute-start.15) | collective-permute-done | bytes 852000 | tf_op jit(solution)/shard_map/ppermute | solution.py:55
  146.0 9.1 %collective-permute-done.20.refs_6_ = bf16[128,1664]{1,0:T(8,128)(2,1)S(1)} collective-permute-done((bf16[128,1664]{1,0:T(8,128)(2,1)S(1)}, bf16[128,1664]{1,0:T(8,128)(2,1)S(1)}, u32[]{:S(2)}, u32[]{:S(2)}) %collective-permute-start.20) | collective-permute-done | bytes 426016 | tf_op jit(solution)/shard_map/ppermute | solution.py:55
  157.9 28.5 %expert.2 = (bf16[1152,1536]{1,0:T(8,128)(2,1)}, f32[8,256]{1,0:T(8,128)}, bf16[1152,1664]{1,0:T(8,128)(2,1)}, bf16[768,1024]{1,0:T(8,128)(2,1)}, bf16[768,1024]{1,0:T(8,128)(2,1)}, /*index=5*/bf16[768,1024]{1,0:T(8,128)(2,1)}) custom-call(s32[2]{0:T(128)} %get-tuple-element.422.number_ref, bf16[256,1664]{1,0:T(8,128)(2,1)} %copy-done.4, ...), custom_call_target="tpu_custom_call" | custom-call | flops 622854144 | bytes 1024 | tf_op jit(solution)/shard_map/expert/pallas_call | solution.py:939
  186.4 2.9 collective-permute-start.24
  189.3 40.2 %expert.3 = (bf16[1152,1536]{1,0:T(8,128)(2,1)}, f32[8,256]{1,0:T(8,128)}, bf16[2048,1664]{1,0:T(8,128)(2,1)}, bf16[768,1024]{1,0:T(8,128)(2,1)}, bf16[768,1024]{1,0:T(8,128)(2,1)}, /*index=5*/bf16[768,1024]{1,0:T(8,128)(2,1)}) custom-call(s32[2]{0:T(128)} %get-tuple-element.421.number_ref, bf16[256,1664]{1,0:T(8,128)(2,1)} %copy-done.4, ...), custom_call_target="tpu_custom_call" | custom-call | flops 622854144 | bytes 1024 | tf_op jit(solution)/shard_map/expert/pallas_call | solution.py:939
  234.8 31.1 %collective-permute-done.26 = bf16[768,1024]{1,0:T(8,128)(2,1)} collective-permute-done((bf16[768,1024]{1,0:T(8,128)(2,1)}, bf16[768,1024]{1,0:T(8,128)(2,1)}, u32[]{:S(2)}, u32[]{:S(2)}) %collective-permute-start.26) | collective-permute-done | bytes 1572896 | tf_op jit(solution)/shard_map/ppermute | solution.py:181
  265.9 4.0 add_convert_fusion.9
  270.0 2.6 fusion.9
  272.6 2.5 collective-permute-start.28
  276.9 6.7 %combine.1 = bf16[2048,1536]{1,0:T(8,128)(2,1)} custom-call(s32[1]{0:T(128)} %bitcast.index_ref.number_ref, f32[8,256]{1,0:T(8,128)S(1)} %copy-done.23, f32[8,256]{1,0:T(8,128)S(1)} %copy-done.24, bf16[1152,1536]{1,0:T(8,128)(2,1)S(1)} %copy-done.5, bf16[1152,1536]{1,0:T(8,128)(2,1)S(1)} %copy-done.6), custom_call_target="tpu_custom_call" | custom-call | flops 70778880 | bytes 1024 | tf_op jit(solution)/shard_map/combine/pallas_call | solution.py:977
  283.6 10.3 %reduce-scatter.5.cloned.1.call-done.total_ref = bf16[256,1664]{1,0:T(8,128)(2,1)} async-done(((bf16[2048,1664]{1,0:T(8,128)(2,1)}), bf16[256,1664]{1,0:T(8,128)(2,1)}) %reduce-scatter.5.cloned.1.call-update) | async-done | bytes 851984 | tf_op jit(solution)/shard_map/reduce_scatter | solution.py:1095
  293.9 7.3 %router_back.1 = (f32[256,1536]{1,0:T(8,128)}, f32[256,1536]{1,0:T(8,128)}, bf16[256,1536]{1,0:T(8,128)(2,1)}, bf16[256,128]{1,0:T(8,128)(2,1)}, f32[8,1536]{1,0:T(8,128)}) custom-call(bf16[256,1664]{1,0:T(8,128)(2,1)} %reduce-scatter.5.cloned.1.call-done.total_ref, f32[256,128]{1,0:T(8,128)} %copy-done.20, bf16[1536,128]{1,0:T(8,128)(2,1)} %copy-done.8, ...), custom_call_target="tpu_custom_call" | custom-call | flops 132120576 | bytes 1024 | tf_op jit(solution)/shard_map/router_back/pallas_call | solution.py:428
  301.2 7.9 %collective-permute-done.28 = bf16[768,1024]{1,0:T(8,128)(2,1)} collective-permute-done((bf16[768,1024]{1,0:T(8,128)(2,1)S(1)}, bf16[768,1024]{1,0:T(8,128)(2,1)}, u32[]{:S(2)}, u32[]{:S(2)}) %collective-permute-start.28) | collective-permute-done | bytes 1572896 | tf_op jit(solution)/shard_map/ppermute | solution.py:171
  311.2 2.9 fusion.10
  317.0 30.0 %attend_back.1 = (bf16[256,1536]{1,0:T(8,128)(2,1)S(1)}, bf16[1024,512]{1,0:T(8,128)(2,1)S(1)}, bf16[1024,512]{1,0:T(8,128)(2,1)S(1)}, bf16[1536,2560]{1,0:T(8,128)(2,1)}) custom-call(s32[2]{0:T(128)S(1)} %copy-done.25, bf16[256,1536]{1,0:T(8,128)(2,1)} %copy-done.7, bf16[1024,1024]{1,0:T(8,128)(2,1)} %get-tuple-element.210.k_ref.v_ref, ...), custom_call_target="tpu_custom_call" | custom-call | flops 402653184 | bytes 1024 | tf_op jit(solution)/shard_map/attend_back/pallas_call | solution.py:722
  357.4 5.8 output_grad.1
  363.2 24.9 %collective-permute-done.32 = bf16[768,1024]{1,0:T(8,128)(2,1)} collective-permute-done((bf16[768,1024]{1,0:T(8,128)(2,1)}, bf16[768,1024]{1,0:T(8,128)(2,1)}, u32[]{:S(2)}, u32[]{:S(2)}) %collective-permute-start.32) | collective-permute-done | bytes 1572896 | tf_op jit(solution)/shard_map/ppermute | solution.py:171
  388.1 3.7 add_convert_fusion.3
  391.8 3.7 fusion.12
  396.4 4.4 collective-permute-start.35
  400.7 3.2 add_convert_fusion.1
  404.0 18.5 %reduce-scatter.9.cloned.1.call-done = bf16[192,2560]{1,0:T(8,128)(2,1)} async-done(((bf16[1536,2560]{1,0:T(8,128)(2,1)}), bf16[192,2560]{1,0:T(8,128)(2,1)}) %reduce-scatter.9.cloned.1.call-update) | async-done | bytes 983056 | tf_op jit(solution)/shard_map/reduce_scatter | solution.py:1108
  423.5 15.9 %collective-permute-start.33 = (bf16[192,1536]{1,0:T(8,128)(2,1)S(1)}, bf16[192,1536]{1,0:T(8,128)(2,1)S(1)}, u32[]{:S(2)}, u32[]{:S(2)}) collective-permute-start(bf16[192,1536]{1,0:T(8,128)(2,1)S(1)} %slice.104), channel_id=1, source_target_pairs={{0,1},{3,2},{4,5},{7,6},{8,9},{11,10},{12,13},{15,14},{16,17},{19,... | collective-permute-start | bytes 1769480 | tf_op jit(solution)/shard_map/ppermute | solution.py:189
  439.5 2.7 add_convert_fusion.2
  449.0 4.4 collective-permute-start.34
  456.3 2.9 collective-permute-done.34
  459.3 19.8 %collective-permute-done.38 = bf16[768,1024]{1,0:T(8,128)(2,1)S(1)} collective-permute-done((bf16[768,1024]{1,0:T(8,128)(2,1)S(1)}, bf16[768,1024]{1,0:T(8,128)(2,1)S(1)}, u32[]{:S(2)}, u32[]{:S(2)}) %collective-permute-start.38) | collective-permute-done | bytes 1572896 | tf_op jit(solution)/shard_map/ppermute | solution.py:181
  489.9 23.6 %collective-permute-done.42 = bf16[768,1024]{1,0:T(8,128)(2,1)} collective-permute-done((bf16[768,1024]{1,0:T(8,128)(2,1)}, bf16[768,1024]{1,0:T(8,128)(2,1)}, u32[]{:S(2)}, u32[]{:S(2)}) %collective-permute-start.42) | collective-permute-done | bytes 1572896 | tf_op jit(solution)/shard_map/ppermute | solution.py:181
  516.4 2.5 copy-done.43
  538.0 3.5 pad_maximum_fusion
  541.5 5.3 copy-done.27
  561.7 20.8 %collective-permute-done.49 = bf16[192,1664]{1,0:T(8,128)(2,1)S(1)} collective-permute-done((bf16[192,1664]{1,0:T(8,128)(2,1)S(1)}, bf16[192,1664]{1,0:T(8,128)(2,1)S(1)}, u32[]{:S(2)}, u32[]{:S(2)}) %collective-permute-start.49) | collective-permute-done | bytes 639008 | tf_op jit(solution)/shard_map/ppermute | solution.py:181
  (310 shorter events, 121.0 us)
Async XLA Ops:
  7.2 98.2 %all-gather.3.cloned.1.call-start = ((), (), s32[]{:S(2)}) async-start(), calls=%async_computation.4 | async-start | bytes 5308416 | tf_op jit(solution)/shard_map/all_gather | solution.py:1054
  7.9 150.0 %all-gather.5.cloned.1.call-start = ((), (), s32[]{:S(2)}) async-start(), calls=%async_computation.5 | async-start | bytes 7667712 | tf_op jit(solution)/shard_map/all_gather | solution.py:1056
  12.5 34.8 %collective-permute-start = (bf16[192,2688]{1,0:T(8,128)(2,1)S(1)}, bf16[192,2688]{1,0:T(8,128)(2,1)S(1)}, u32[]{:S(2)}, u32[]{:S(2)}) collective-permute-start(bf16[192,2688]{1,0:T(8,128)(2,1)S(1)} %concatenate.31.refs_0_), channel_id=1, source_target_pairs={{0,8},{4,12},{8,0},{12,4},{16,24},{20,28},{24,16},{28,20},{1,9},{5... | collective-permute-start | bytes 3096584 | tf_op jit(solution)/shard_map/ppermute | solution.py:55
  15.5 35.2 %collective-permute-start.1 = (bf16[192,2688]{1,0:T(8,128)(2,1)S(1)}, bf16[192,2688]{1,0:T(8,128)(2,1)}, u32[]{:S(2)}, u32[]{:S(2)}) collective-permute-start(bf16[192,2688]{1,0:T(8,128)(2,1)S(1)} %concatenate.31.refs_0_), channel_id=1, source_target_pairs={{0,16},{4,20},{8,24},{12,28},{16,0},{20,4},{24,8},{28,12},{1,17},{... | collective-permute-start | bytes 3096584 | tf_op jit(solution)/shard_map/ppermute | solution.py:55
  18.3 13.0 %collective-permute-start.2 = (bf16[128,1536]{1,0:T(8,128)(2,1)S(1)}, bf16[128,1536]{1,0:T(8,128)(2,1)}, u32[]{:S(2)}, u32[]{:S(2)}) collective-permute-start(bf16[128,1536]{1,0:T(8,128)(2,1)S(1)} %get-tuple-element.415.refs_10_), channel_id=1, source_target_pairs={{0,1},{1,2},{2,3},{4,5},{5,6},{6,7},{8,9},{9,10},{10,11},{12,13},{... | collective-permute-start | bytes 1179656 | tf_op jit(solution)/shard_map/ppermute | solution.py:114
  22.5 17.2 %collective-permute-start.3 = (bf16[128,1536]{1,0:T(8,128)(2,1)S(1)}, bf16[128,1536]{1,0:T(8,128)(2,1)}, u32[]{:S(2)}, u32[]{:S(2)}) collective-permute-start(bf16[128,1536]{1,0:T(8,128)(2,1)S(1)} %get-tuple-element.414.refs_11_), channel_id=1, source_target_pairs={{0,1},{1,2},{2,3},{4,5},{5,6},{6,7},{8,9},{9,10},{10,11},{12,13},{... | collective-permute-start | bytes 1179656 | tf_op jit(solution)/shard_map/ppermute | solution.py:114
  31.3 15.2 %collective-permute-start.4 = (bf16[128,1536]{1,0:T(8,128)(2,1)}, bf16[128,1536]{1,0:T(8,128)(2,1)}, u32[]{:S(2)}, u32[]{:S(2)}) collective-permute-start(bf16[128,1536]{1,0:T(8,128)(2,1)} %collective-permute-done.2.refs_12_), channel_id=1, source_target_pairs={{0,1},{1,2},{2,3},{4,5},{5,6},{6,7},{8,9},{9,10},{10,11},{12,13},{... | collective-permute-start | bytes 1179656 | tf_op jit(solution)/shard_map/ppermute | solution.py:114
  50.7 243.2 %reduce-scatter.5.cloned.1.call-start = ((), (), s32[]{:S(2)}) async-start(), calls=%async_computation.6 | async-start | bytes 7667712 | tf_op jit(solution)/shard_map/reduce_scatter | solution.py:1095
  50.8 20.1 %collective-permute-start.5 = (bf16[96,2688]{1,0:T(8,128)(2,1)S(1)}, bf16[96,2688]{1,0:T(8,128)(2,1)S(1)}, u32[]{:S(2)}, u32[]{:S(2)}) collective-permute-start(bf16[96,2688]{1,0:T(8,128)(2,1)S(1)} %slice.82), channel_id=1, source_target_pairs={{0,16},{4,20},{8,24},{12,28},{16,0},{20,4},{24,8},{28,12},{1,17},{... | collective-permute-start | bytes 1548296 | tf_op jit(solution)/shard_map/ppermute | solution.py:55
  54.6 16.4 %collective-permute-start.6 = (bf16[96,2688]{1,0:T(8,128)(2,1)S(1)}, bf16[96,2688]{1,0:T(8,128)(2,1)}, u32[]{:S(2)}, u32[]{:S(2)}) collective-permute-start(bf16[96,2688]{1,0:T(8,128)(2,1)S(1)} %slice.83), channel_id=1, source_target_pairs={{0,8},{4,12},{8,0},{12,4},{16,24},{20,28},{24,16},{28,20},{1,9},{5... | collective-permute-start | bytes 1548296 | tf_op jit(solution)/shard_map/ppermute | solution.py:55
  54.6 11.3 %collective-permute-start.7 = (bf16[128,1536]{1,0:T(8,128)(2,1)}, bf16[128,1536]{1,0:T(8,128)(2,1)}, u32[]{:S(2)}, u32[]{:S(2)}) collective-permute-start(bf16[128,1536]{1,0:T(8,128)(2,1)} %collective-permute-done.3.refs_13_), channel_id=1, source_target_pairs={{0,1},{1,2},{2,3},{4,5},{5,6},{6,7},{8,9},{9,10},{10,11},{12,13},{... | collective-permute-start | bytes 1179656 | tf_op jit(solution)/shard_map/ppermute | solution.py:114
  58.7 11.4 %collective-permute-start.8 = (bf16[128,1536]{1,0:T(8,128)(2,1)}, bf16[128,1536]{1,0:T(8,128)(2,1)S(1)}, u32[]{:S(2)}, u32[]{:S(2)}) collective-permute-start(bf16[128,1536]{1,0:T(8,128)(2,1)} %collective-permute-done.4.refs_14_), channel_id=1, source_target_pairs={{0,1},{1,2},{2,3},{4,5},{5,6},{6,7},{8,9},{9,10},{10,11},{12,13},{... | collective-permute-start | bytes 1179656 | tf_op jit(solution)/shard_map/ppermute | solution.py:114
  70.9 12.6 %collective-permute-start.10 = (bf16[192,2688]{1,0:T(8,128)(2,1)S(1)}, bf16[192,2688]{1,0:T(8,128)(2,1)}, u32[]{:S(2)}, u32[]{:S(2)}) collective-permute-start(bf16[192,2688]{1,0:T(8,128)(2,1)S(1)} %collective-permute-done.refs_2_), channel_id=1, source_target_pairs={{0,4},{4,0},{8,12},{12,8},{16,20},{20,16},{24,28},{28,24},{1,5},{5... | collective-permute-start | bytes 3096584 | tf_op jit(solution)/shard_map/ppermute | solution.py:55
  70.9 12.6 %collective-permute-start.11 = (bf16[192,2688]{1,0:T(8,128)(2,1)}, bf16[192,2688]{1,0:T(8,128)(2,1)}, u32[]{:S(2)}, u32[]{:S(2)}) collective-permute-start(bf16[192,2688]{1,0:T(8,128)(2,1)} %collective-permute-done.1.refs_4_), channel_id=1, source_target_pairs={{0,4},{4,0},{8,12},{12,8},{16,20},{20,16},{24,28},{28,24},{1,5},{5... | collective-permute-start | bytes 3096584 | tf_op jit(solution)/shard_map/ppermute | solution.py:55
  71.4 12.1 %collective-permute-start.9 = (bf16[192,2688]{1,0:T(8,128)(2,1)S(1)}, bf16[192,2688]{1,0:T(8,128)(2,1)}, u32[]{:S(2)}, u32[]{:S(2)}) collective-permute-start(bf16[192,2688]{1,0:T(8,128)(2,1)S(1)} %concatenate.31.refs_0_), channel_id=1, source_target_pairs={{0,4},{4,0},{8,12},{12,8},{16,20},{20,16},{24,28},{28,24},{1,5},{5... | collective-permute-start | bytes 3096584 | tf_op jit(solution)/shard_map/ppermute | solution.py:55
  72.7 10.8 %collective-permute-start.13 = (bf16[96,2688]{1,0:T(8,128)(2,1)}, bf16[96,2688]{1,0:T(8,128)(2,1)}, u32[]{:S(2)}, u32[]{:S(2)}) collective-permute-start(bf16[96,2688]{1,0:T(8,128)(2,1)} %collective-permute-done.6.refs_7_), channel_id=1, source_target_pairs={{0,4},{4,0},{8,12},{12,8},{16,20},{20,16},{24,28},{28,24},{1,5},{5... | collective-permute-start | bytes 1548296 | tf_op jit(solution)/shard_map/ppermute | solution.py:55
  77.3 23.0 %collective-permute-start.14 = (bf16[128,1536]{1,0:T(8,128)(2,1)}, bf16[128,1536]{1,0:T(8,128)(2,1)}, u32[]{:S(2)}, u32[]{:S(2)}) collective-permute-start(bf16[128,1536]{1,0:T(8,128)(2,1)} %collective-permute-done.7.refs_15_), channel_id=1, source_target_pairs={{0,1},{1,2},{2,3},{4,5},{5,6},{6,7},{8,9},{9,10},{10,11},{12,13},{... | collective-permute-start | bytes 1179656 | tf_op jit(solution)/shard_map/ppermute | solution.py:114
  122.4 20.8 %collective-permute-start.15 = (bf16[256,1664]{1,0:T(8,128)(2,1)S(1)}, bf16[256,1664]{1,0:T(8,128)(2,1)S(1)}, u32[]{:S(2)}, u32[]{:S(2)}) collective-permute-start(bf16[256,1664]{1,0:T(8,128)(2,1)S(1)} %get-tuple-element.218.refs_0_.hn_ref), channel_id=1, source_target_pairs={{0,8},{4,12},{8,0},{12,4},{16,24},{20,28},{24,16},{28,20},{1,9},{5... | collective-permute-start | bytes 2555912 | tf_op jit(solution)/shard_map/ppermute | solution.py:55
  124.2 20.4 %collective-permute-start.16 = (bf16[256,1664]{1,0:T(8,128)(2,1)S(1)}, bf16[256,1664]{1,0:T(8,128)(2,1)S(1)}, u32[]{:S(2)}, u32[]{:S(2)}) collective-permute-start(bf16[256,1664]{1,0:T(8,128)(2,1)S(1)} %get-tuple-element.218.refs_0_.hn_ref), channel_id=1, source_target_pairs={{0,16},{4,20},{8,24},{12,28},{16,0},{20,4},{24,8},{28,12},{1,17},{... | collective-permute-start | bytes 2555912 | tf_op jit(solution)/shard_map/ppermute | solution.py:55
  144.7 10.4 %collective-permute-start.20 = (bf16[128,1664]{1,0:T(8,128)(2,1)S(1)}, bf16[128,1664]{1,0:T(8,128)(2,1)S(1)}, u32[]{:S(2)}, u32[]{:S(2)}) collective-permute-start(bf16[128,1664]{1,0:T(8,128)(2,1)S(1)} %slice.84), channel_id=1, source_target_pairs={{0,16},{4,20},{8,24},{12,28},{16,0},{20,4},{24,8},{28,12},{1,17},{... | collective-permute-start | bytes 1277960 | tf_op jit(solution)/shard_map/ppermute | solution.py:55
  145.1 10.3 %collective-permute-start.21 = (bf16[128,1664]{1,0:T(8,128)(2,1)S(1)}, bf16[128,1664]{1,0:T(8,128)(2,1)}, u32[]{:S(2)}, u32[]{:S(2)}) collective-permute-start(bf16[128,1664]{1,0:T(8,128)(2,1)S(1)} %slice.85), channel_id=1, source_target_pairs={{0,8},{4,12},{8,0},{12,4},{16,24},{20,28},{24,16},{28,20},{1,9},{5... | collective-permute-start | bytes 1277960 | tf_op jit(solution)/shard_map/ppermute | solution.py:55
  145.5 12.4 %collective-permute-start.17 = (bf16[256,1664]{1,0:T(8,128)(2,1)S(1)}, bf16[256,1664]{1,0:T(8,128)(2,1)}, u32[]{:S(2)}, u32[]{:S(2)}) collective-permute-start(bf16[256,1664]{1,0:T(8,128)(2,1)S(1)} %get-tuple-element.218.refs_0_.hn_ref), channel_id=1, source_target_pairs={{0,4},{4,0},{8,12},{12,8},{16,20},{20,16},{24,28},{28,24},{1,5},{5... | collective-permute-start | bytes 2555912 | tf_op jit(solution)/shard_map/ppermute | solution.py:55
  145.5 12.4 %collective-permute-start.18 = (bf16[256,1664]{1,0:T(8,128)(2,1)S(1)}, bf16[256,1664]{1,0:T(8,128)(2,1)}, u32[]{:S(2)}, u32[]{:S(2)}) collective-permute-start(bf16[256,1664]{1,0:T(8,128)(2,1)S(1)} %collective-permute-done.15.refs_2_), channel_id=1, source_target_pairs={{0,4},{4,0},{8,12},{12,8},{16,20},{20,16},{24,28},{28,24},{1,5},{5... | collective-permute-start | bytes 2555912 | tf_op jit(solution)/shard_map/ppermute | solution.py:55
  146.0 11.9 %collective-permute-start.19 = (bf16[256,1664]{1,0:T(8,128)(2,1)S(1)}, bf16[256,1664]{1,0:T(8,128)(2,1)}, u32[]{:S(2)}, u32[]{:S(2)}) collective-permute-start(bf16[256,1664]{1,0:T(8,128)(2,1)S(1)} %collective-permute-done.16.refs_4_), channel_id=1, source_target_pairs={{0,4},{4,0},{8,12},{12,8},{16,20},{20,16},{24,28},{28,24},{1,5},{5... | collective-permute-start | bytes 2555912 | tf_op jit(solution)/shard_map/ppermute | solution.py:55
  186.4 43.1 %collective-permute-start.24 = (bf16[768,1024]{1,0:T(8,128)(2,1)}, bf16[768,1024]{1,0:T(8,128)(2,1)S(1)}, u32[]{:S(2)}, u32[]{:S(2)}) collective-permute-start(bf16[768,1024]{1,0:T(8,128)(2,1)} %get-tuple-element.235), channel_id=1, source_target_pairs={{0,1},{3,2},{4,5},{7,6},{8,9},{11,10},{12,13},{15,14},{16,17},{19,... | collective-permute-start | bytes 4718600 | tf_op jit(solution)/shard_map/ppermute | solution.py:181
  230.3 192.2 %reduce-scatter.9.cloned.1.call-start = ((), (), s32[]{:S(2)}) async-start(), calls=%async_computation.8 | async-start | bytes 8847360 | tf_op jit(solution)/shard_map/reduce_scatter | solution.py:1108
  230.3 35.6 %collective-permute-start.26 = (bf16[768,1024]{1,0:T(8,128)(2,1)}, bf16[768,1024]{1,0:T(8,128)(2,1)}, u32[]{:S(2)}, u32[]{:S(2)}) collective-permute-start(bf16[768,1024]{1,0:T(8,128)(2,1)} %get-tuple-element.238), channel_id=1, source_target_pairs={{0,1},{3,2},{4,5},{7,6},{8,9},{11,10},{12,13},{15,14},{16,17},{19,... | collective-permute-start | bytes 4718600 | tf_op jit(solution)/shard_map/ppermute | solution.py:181
  232.8 37.1 %collective-permute-start.25 = (bf16[768,1024]{1,0:T(8,128)(2,1)S(1)}, bf16[768,1024]{1,0:T(8,128)(2,1)}, u32[]{:S(2)}, u32[]{:S(2)}) collective-permute-start(bf16[768,1024]{1,0:T(8,128)(2,1)S(1)} %add_convert_fusion.11), channel_id=1, source_target_pairs={{1,2},{2,1},{5,6},{6,5},{9,10},{10,9},{13,14},{14,13},{17,18},{18,... | collective-permute-start | bytes 4718600 | tf_op jit(solution)/shard_map/ppermute | solution.py:181
  272.6 36.5 %collective-permute-start.28 = (bf16[768,1024]{1,0:T(8,128)(2,1)S(1)}, bf16[768,1024]{1,0:T(8,128)(2,1)}, u32[]{:S(2)}, u32[]{:S(2)}) collective-permute-start(bf16[768,1024]{1,0:T(8,128)(2,1)S(1)} %fusion.9), channel_id=1, source_target_pairs={{0,1},{1,0},{2,3},{3,2},{4,5},{5,4},{6,7},{7,6},{8,9},{9,8},{10,11... | collective-permute-start | bytes 4718600 | tf_op jit(solution)/shard_map/ppermute | solution.py:171
  275.1 36.1 %collective-permute-start.27 = (bf16[768,1024]{1,0:T(8,128)(2,1)}, bf16[768,1024]{1,0:T(8,128)(2,1)}, u32[]{:S(2)}, u32[]{:S(2)}) collective-permute-start(bf16[768,1024]{1,0:T(8,128)(2,1)} %add_convert_fusion.9), channel_id=1, source_target_pairs={{1,2},{2,1},{5,6},{6,5},{9,10},{10,9},{13,14},{14,13},{17,18},{18,... | collective-permute-start | bytes 4718600 | tf_op jit(solution)/shard_map/ppermute | solution.py:181
  314.2 35.1 %collective-permute-start.30 = (bf16[768,1024]{1,0:T(8,128)(2,1)S(1)}, bf16[768,1024]{1,0:T(8,128)(2,1)S(1)}, u32[]{:S(2)}, u32[]{:S(2)}) collective-permute-start(bf16[768,1024]{1,0:T(8,128)(2,1)S(1)} %fusion.10), channel_id=1, source_target_pairs={{0,1},{1,0},{2,3},{3,2},{4,5},{5,4},{6,7},{7,6},{8,9},{9,8},{10,11... | collective-permute-start | bytes 4718600 | tf_op jit(solution)/shard_map/ppermute | solution.py:171
  316.0 35.1 %collective-permute-start.29 = (bf16[768,1024]{1,0:T(8,128)(2,1)S(1)}, bf16[768,1024]{1,0:T(8,128)(2,1)S(1)}, u32[]{:S(2)}, u32[]{:S(2)}) collective-permute-start(bf16[768,1024]{1,0:T(8,128)(2,1)S(1)} %add_convert_fusion.7), channel_id=1, source_target_pairs={{1,2},{2,1},{5,6},{6,5},{9,10},{10,9},{13,14},{14,13},{17,18},{18,... | collective-permute-start | bytes 4718600 | tf_op jit(solution)/shard_map/ppermute | solution.py:181
  353.4 136.5 %reduce-scatter.7.cloned.1.call-start = ((), (), s32[]{:S(2)}) async-start(), calls=%async_computation.7 | async-start | bytes 5750784 | tf_op jit(solution)/shard_map/reduce_scatter | solution.py:1111
  353.5 34.6 %collective-permute-start.32 = (bf16[768,1024]{1,0:T(8,128)(2,1)}, bf16[768,1024]{1,0:T(8,128)(2,1)}, u32[]{:S(2)}, u32[]{:S(2)}) collective-permute-start(bf16[768,1024]{1,0:T(8,128)(2,1)} %fusion.11), channel_id=1, source_target_pairs={{0,1},{1,0},{2,3},{3,2},{4,5},{5,4},{6,7},{7,6},{8,9},{9,8},{10,11... | collective-permute-start | bytes 4718600 | tf_op jit(solution)/shard_map/ppermute | solution.py:171
  355.3 36.4 %collective-permute-start.31 = (bf16[768,1024]{1,0:T(8,128)(2,1)}, bf16[768,1024]{1,0:T(8,128)(2,1)}, u32[]{:S(2)}, u32[]{:S(2)}) collective-permute-start(bf16[768,1024]{1,0:T(8,128)(2,1)} %add_convert_fusion.5), channel_id=1, source_target_pairs={{1,2},{2,1},{5,6},{6,5},{9,10},{10,9},{13,14},{14,13},{17,18},{18,... | collective-permute-start | bytes 4718600 | tf_op jit(solution)/shard_map/ppermute | solution.py:181
  395.6 162.7 %reduce-scatter.11.cloned.1.call-start = ((), (), s32[]{:S(2)}) async-start(), calls=%async_computation.9 | async-start | bytes 7077888 | tf_op jit(solution)/shard_map/reduce_scatter | solution.py:1147
  396.4 43.1 %collective-permute-start.35 = (bf16[768,1024]{1,0:T(8,128)(2,1)}, bf16[768,1024]{1,0:T(8,128)(2,1)}, u32[]{:S(2)}, u32[]{:S(2)}) collective-permute-start(bf16[768,1024]{1,0:T(8,128)(2,1)} %fusion.12), channel_id=1, source_target_pairs={{0,1},{1,0},{2,3},{3,2},{4,5},{5,4},{6,7},{7,6},{8,9},{9,8},{10,11... | collective-permute-start | bytes 4718600 | tf_op jit(solution)/shard_map/ppermute | solution.py:171
  423.5 24.2 %collective-permute-start.33 = (bf16[192,1536]{1,0:T(8,128)(2,1)S(1)}, bf16[192,1536]{1,0:T(8,128)(2,1)S(1)}, u32[]{:S(2)}, u32[]{:S(2)}) collective-permute-start(bf16[192,1536]{1,0:T(8,128)(2,1)S(1)} %slice.104), channel_id=1, source_target_pairs={{0,1},{3,2},{4,5},{7,6},{8,9},{11,10},{12,13},{15,14},{16,17},{19,... | collective-permute-start | bytes 1769480 | tf_op jit(solution)/shard_map/ppermute | solution.py:189
  442.1 12.3 %collective-permute-start.37 = (bf16[768,1024]{1,0:T(8,128)(2,1)S(1)}, bf16[768,1024]{1,0:T(8,128)(2,1)S(1)}, u32[]{:S(2)}, u32[]{:S(2)}) collective-permute-start(bf16[768,1024]{1,0:T(8,128)(2,1)S(1)} %add_convert_fusion.2), channel_id=1, source_target_pairs={{1,2},{2,1},{5,6},{6,5},{9,10},{10,9},{13,14},{14,13},{17,18},{18,... | collective-permute-start | bytes 4718600 | tf_op jit(solution)/shard_map/ppermute | solution.py:181
  443.3 10.2 %collective-permute-start.39 = (bf16[256,1024]{1,0:T(8,128)(2,1)S(1)}, bf16[256,1024]{1,0:T(8,128)(2,1)S(1)}, u32[]{:S(2)}, u32[]{:S(2)}) collective-permute-start(bf16[256,1024]{1,0:T(8,128)(2,1)S(1)} %slice.106), channel_id=1, source_target_pairs={{3,2},{7,6},{11,10},{15,14},{19,18},{23,22},{27,26},{31,30}} | collective-permute-start | bytes 1572872 | tf_op jit(solution)/shard_map/ppermute | solution.py:1144
  445.2 34.0 %collective-permute-start.38 = (bf16[768,1024]{1,0:T(8,128)(2,1)S(1)}, bf16[768,1024]{1,0:T(8,128)(2,1)S(1)}, u32[]{:S(2)}, u32[]{:S(2)}) collective-permute-start(bf16[768,1024]{1,0:T(8,128)(2,1)S(1)} %copy-done.40), channel_id=1, source_target_pairs={{1,0},{2,3},{5,4},{6,7},{9,8},{10,11},{13,12},{14,15},{17,16},{18,... | collective-permute-start | bytes 4718600 | tf_op jit(solution)/shard_map/ppermute | solution.py:181
  449.0 10.2 %collective-permute-start.34 = (bf16[192,1152]{1,0:T(8,128)(2,1)S(1)}, bf16[192,1152]{1,0:T(8,128)(2,1)S(1)}, u32[]{:S(2)}, u32[]{:S(2)}) collective-permute-start(bf16[192,1152]{1,0:T(8,128)(2,1)S(1)} %pad_maximum_fusion.4), channel_id=1, source_target_pairs={{0,1},{3,2},{4,5},{7,6},{8,9},{11,10},{12,13},{15,14},{16,17},{19,... | collective-permute-start | bytes 1327112 | tf_op jit(solution)/shard_map/ppermute | solution.py:189
  480.1 33.4 %collective-permute-start.42 = (bf16[768,1024]{1,0:T(8,128)(2,1)}, bf16[768,1024]{1,0:T(8,128)(2,1)}, u32[]{:S(2)}, u32[]{:S(2)}) collective-permute-start(bf16[768,1024]{1,0:T(8,128)(2,1)} %add_convert_fusion), channel_id=1, source_target_pairs={{1,0},{2,3},{5,4},{6,7},{9,8},{10,11},{13,12},{14,15},{17,16},{18,... | collective-permute-start | bytes 4718600 | tf_op jit(solution)/shard_map/ppermute | solution.py:181
  513.4 33.4 %collective-permute-start.48 = (bf16[256,1024]{1,0:T(8,128)(2,1)}, bf16[256,1024]{1,0:T(8,128)(2,1)}, u32[]{:S(2)}, u32[]{:S(2)}) collective-permute-start(bf16[256,1024]{1,0:T(8,128)(2,1)} %add_convert_fusion.16), channel_id=1, source_target_pairs={{1,0},{2,1},{3,2},{5,4},{6,5},{7,6},{9,8},{10,9},{11,10},{13,12},{... | collective-permute-start | bytes 1572872 | tf_op jit(solution)/shard_map/ppermute | solution.py:1144
  522.1 29.9 %collective-permute-start.44 = (bf16[192,1664]{1,0:T(8,128)(2,1)S(1)}, bf16[192,1664]{1,0:T(8,128)(2,1)S(1)}, u32[]{:S(2)}, u32[]{:S(2)}) collective-permute-start(bf16[192,1664]{1,0:T(8,128)(2,1)S(1)} %copy-done.64), channel_id=1, source_target_pairs={{0,1},{3,2},{4,5},{7,6},{8,9},{11,10},{12,13},{15,14},{16,17},{19,... | collective-permute-start | bytes 1916936 | tf_op jit(solution)/shard_map/ppermute | solution.py:181
  524.0 28.2 %collective-permute-start.46 = (bf16[192,1536]{1,0:T(8,128)(2,1)S(1)}, bf16[192,1536]{1,0:T(8,128)(2,1)}, u32[]{:S(2)}, u32[]{:S(2)}) collective-permute-start(bf16[192,1536]{1,0:T(8,128)(2,1)S(1)} %copy-done.54), channel_id=1, source_target_pairs={{1,0},{2,3},{5,4},{6,7},{9,8},{10,11},{13,12},{14,15},{17,16},{18,... | collective-permute-start | bytes 1769480 | tf_op jit(solution)/shard_map/ppermute | solution.py:181
  525.3 26.9 %collective-permute-start.45 = (bf16[192,1152]{1,0:T(8,128)(2,1)S(1)}, bf16[192,1152]{1,0:T(8,128)(2,1)}, u32[]{:S(2)}, u32[]{:S(2)}) collective-permute-start(bf16[192,1152]{1,0:T(8,128)(2,1)S(1)} %copy-done.56), channel_id=1, source_target_pairs={{1,0},{2,3},{5,4},{6,7},{9,8},{10,11},{13,12},{14,15},{17,16},{18,... | collective-permute-start | bytes 1327112 | tf_op jit(solution)/shard_map/ppermute | solution.py:181
  560.5 22.1 %collective-permute-start.49 = (bf16[192,1664]{1,0:T(8,128)(2,1)S(1)}, bf16[192,1664]{1,0:T(8,128)(2,1)S(1)}, u32[]{:S(2)}, u32[]{:S(2)}) collective-permute-start(bf16[192,1664]{1,0:T(8,128)(2,1)S(1)} %add_convert_fusion.12), channel_id=1, source_target_pairs={{1,0},{2,3},{5,4},{6,7},{9,8},{10,11},{13,12},{14,15},{17,16},{18,... | collective-permute-start | bytes 1916936 | tf_op jit(solution)/shard_map/ppermute | solution.py:181
  (81 other events, 951.6 us)
Sparse Core Ops, SparseCore 0:
  9.9 57.9 all-gather.2
  70.3 48.3 all-gather.4
  230.4 63.4 reduce-scatter.4
  353.5 68.8 reduce-scatter.8
  426.4 55.8 reduce-scatter.6
  485.5 65.5 reduce-scatter.10

commit v5 on v4

--- a/solution.py
+++ b/solution.py
@@ -785,26 +785,31 @@
 
 def expert_kernel(counts, cap, tile, e, earlier, last, number_ref, *refs):
     parts, refs = refs[: sum(counts)], refs[sum(counts) :]
-    cot_ref, wgu_all_ref, wd_all_ref = refs[:3]
+    cot_all_ref, wgu_all_ref, wd_all_ref = refs[:3]
     gin_before, refs = refs[3 : 3 + earlier], refs[3 + earlier :]
     out_ref, slots_ref, result_ref = refs[:3]
     grads = refs[3:6]
-    x_ref, c_ref, ggu_ref, act_ref, sg_ref, wgu_ref, wd_ref, sems = refs[6:14]
+    x_ref, c_ref, ggu_ref, act_ref, sg_ref, wgu_ref, wd_ref, cot_ref, cot_sems, sems = refs[6:16]
     if last:
-        gin_ref, load_ref, store_ref = refs[14:]
+        gin_ref, load_ref, store_ref = refs[16:]
     else:
         gin_ref = result_ref
-    loads = [
-        pltpu.make_async_copy(wgu_all_ref.at[e], wgu_ref, sems.at[0]),
-        pltpu.make_async_copy(wd_all_ref.at[e], wd_ref, sems.at[1]),
-    ]
-    for load in loads:
-        load.start()
     blocks = len(counts)
     hidden, width = wd_ref.shape
     rows = cot_ref.shape[0] // blocks
     total = blocks * cap
     index, expert = number_ref[0], number_ref[1]
+    cot_loads = []
+    for b in range(blocks):
+        src = pl.ds(pl.multiple_of((index ^ b) * rows, rows), rows)
+        dst = cot_ref.at[b * rows : (b + 1) * rows]
+        cot_loads.append(pltpu.make_async_copy(cot_all_ref.at[src], dst, cot_sems.at[b]))
+    loads = [
+        pltpu.make_async_copy(wgu_all_ref.at[e], wgu_ref, sems.at[0]),
+        pltpu.make_async_copy(wd_all_ref.at[e], wd_ref, sems.at[1]),
+    ]
+    for load in cot_loads + loads:
+        load.start()
     lane = lax.broadcasted_iota(jnp.int32, (8, SIDE), 1)
     pick_slot = low(jnp.where(lane == expert, 1.0, 0.0))
     pick_gate = low(jnp.where((lane == expert) | (lane == expert + SIDE // 2), 1.0, 0.0))
@@ -812,7 +817,8 @@
     for b in range(blocks):
         hn = parts[n : n + counts[b]]
         n += counts[b]
-        src = pl.ds(pl.multiple_of((index ^ b) * rows, rows), rows)
+        src = slice(b * rows, (b + 1) * rows)
+        cot_loads[b].wait()
         slot = dot_nt(pick_slot, cot_ref[src, width:])[:1] - 1.0
         gate = [dot_nt(pick_gate, part[:, width:]) for part in hn]
         gate = (jnp.concatenate(gate, 1) if len(gate) > 1 else gate[0])[:1]
@@ -881,7 +887,7 @@
         if b + 1 < blocks:
             for load in load_before(b + 1):
                 load.start()
-        src = pl.ds(pl.multiple_of((index ^ b) * rows, rows), rows)
+        src = slice(b * rows, (b + 1) * rows)
         order = up(cot_ref[src, width:])
         lane = lax.broadcasted_iota(jnp.int32, order.shape, 1)
         place = lax.broadcasted_iota(jnp.int32, (rows, cap), 1).astype(F32)
@@ -927,6 +933,8 @@
         pltpu.VMEM((total, 128), F32),
         pltpu.VMEM((width, 2 * hidden), BF16),
         pltpu.VMEM((hidden, width), BF16),
+        pltpu.VMEM(cot.shape, BF16),
+        pltpu.SemaphoreType.DMA((blocks,)),
         pltpu.SemaphoreType.DMA((4 + 2 * earlier,)),
     ]
     if last:
@@ -939,8 +947,8 @@
     got = pl.pallas_call(
         functools.partial(expert_kernel, counts, cap, tile, e, earlier, last),
         in_specs=[pl.BlockSpec(memory_space=pltpu.SMEM)]
-        + [WHOLE] * (len(flat) + 1)
-        + [anywhere] * (2 + earlier),
+        + [WHOLE] * len(flat)
+        + [anywhere] * (3 + earlier),
         out_specs=[WHOLE, WHOLE, anywhere if last else WHOLE] + [WHOLE] * 3,
         out_shape=[
             pltpu.HBM((total, width), BF16),
@@ -952,7 +960,7 @@
         compiler_params=params(56),
         cost_estimate=cost(44 * total * width * hidden),
         name="expert",
-    )(number, *flat, cot, w_gate_up, w_down, *gins[:earlier])
+    )(number, *flat, *hbm(cot), w_gate_up, w_down, *gins[:earlier])
     return got[0], got[1], got[2], got[3:]
 
 

time: 604 us -> 604 us (level)
  transfers between devices with their start and end apart: 56 -> 56, of which waited for: 25 -> 25; matrix products, arithmetic and copies ran while one was open for 12% -> 12% of each run, Pallas kernels for 21% -> 20%
where the time goes in v5:
time: 604 us; the launch traced here: 593 us
  waiting for transfers between devices  223 us (37%)
  Pallas kernels  150 us (25%)
  starting transfers between devices  95.9 us (16%)
  other arithmetic  67.4 us (11%)
  local copies, waits for them, and re-layouts  36.3 us (6%)
  between operations  16.7 us (3%)
    ppermute x17, waiting for transfers between devices, step(): flight.append((kind, name, v, lax.ppermute(v, 'ctx', pairs)))  96.6 us
    pallas_call x2, Pallas kernels, run_expert(): pl.pallas_call(functools.partial(expert_kernel, counts, cap, tile, e, ear...  68.2 us
    ppermute x18, waiting for transfers between devices, swap(): return lax.ppermute(v, 'dp', [(i, i ^ mask) for i in range(count)])  39.1 us
    ppermute x4, waiting for transfers between devices, step(): back = lax.ppermute(payload, 'ctx', [(0, 1), (1, 0), (2, 3), (3, 2)])  35 us
    convert_element_type x18, other arithmetic, low(): return v.astype(BF16)  30.5 us
    pallas_call x1, Pallas kernels, attend_back(): pl.pallas_call(functools.partial(attend_back_kernel, groups), grid_spec=p...  30 us
    ppermute x17, starting transfers between devices, step(): flight.append((kind, name, v, lax.ppermute(v, 'ctx', pairs)))  25.1 us
    ppermute x6, starting transfers between devices, shift(): lax.ppermute(v, 'ctx', [(i, i + step) for i in range(count) if 0 <= i + s...  24.9 us
  transfers between devices with their start and end apart: 56, of which 25 were waited for; matrix products, arithmetic and copies ran while one was open for 12% of the time, Pallas kernels for 20%

profile of v5, /device:TPU:0, one launch (start us, length us, event | category | flops | bytes accessed | tf_op | source)
XLA Modules:
  0.0 592.5 jit_solution(18344682691470121513)
XLA Ops:
  12.5 3.0 collective-permute-start
  18.3 4.3 collective-permute-start.2
  22.5 3.5 collective-permute-start.3
  31.3 5.2 collective-permute-start.4
  39.7 6.8 %collective-permute-done.4.refs_14_ = bf16[128,1536]{1,0:T(8,128)(2,1)} collective-permute-done((bf16[128,1536]{1,0:T(8,128)(2,1)}, bf16[128,1536]{1,0:T(8,128)(2,1)}, u32[]{:S(2)}, u32[]{:S(2)}) %collective-permute-start.4) | collective-permute-done | bytes 393248 | tf_op jit(solution)/shard_map/ppermute | solution.py:114
  47.4 3.3 collective-permute-done.1.refs_4_
  50.8 2.7 collective-permute-start.5
  54.6 4.1 collective-permute-start.7
  58.7 2.8 collective-permute-start.8
  61.6 4.4 collective-permute-done.7.refs_15_
  66.0 4.2 collective-permute-done.8.a_ref
  72.8 3.7 collective-permute-done.12.refs_8_
  77.3 5.0 collective-permute-start.14
  87.7 11.8 %project.1 = (bf16[256,1536]{1,0:T(8,128)(2,1)S(1)}, bf16[1024,1024]{1,0:T(8,128)(2,1)}, bf16[1024,1536]{1,0:T(8,128)(2,1)}, bf16[1536,1536]{1,0:T(8,128)(2,1)},...) custom-call(s32[1]{0:T(128)} %bitcast.index_ref.number_ref, ...), custom_call_target="tpu_custom_call" | custom-call | flops 276824064 | bytes 1024 | tf_op jit(solution)/shard_map/project/pallas_call | solution.py:286
  102.4 3.0 project_last.1
  105.5 16.9 %attend.1 = (f32[256,1536]{1,0:T(8,128)}, f32[4,8,256]{2,1,0:T(8,128)S(1)}, f32[4,8,256]{2,1,0:T(8,128)S(1)}, f32[256,1536]{1,0:T(8,128)}, bf16[256,1664]{1,0:T(...) custom-call(s32[2]{0:T(128)S(1)} %copy-done.25, bf16[256,1536]{1,0:T(8,128)(2,1)} %copy-done.7, ...), custom_call_target="tpu_custom_call" | custom-call | flops 314572800 | bytes 1024 | tf_op jit(solution)/shard_map/attend/pallas_call | solution.py:552
  124.5 18.7 %collective-permute-done.15.refs_2_ = bf16[256,1664]{1,0:T(8,128)(2,1)S(1)} collective-permute-done((bf16[256,1664]{1,0:T(8,128)(2,1)S(1)}, bf16[256,1664]{1,0:T(8,128)(2,1)S(1)}, u32[]{:S(2)}, u32[]{:S(2)}) %collective-permute-start.15) | collective-permute-done | bytes 852000 | tf_op jit(solution)/shard_map/ppermute | solution.py:55
  146.0 9.1 %collective-permute-done.20.refs_6_ = bf16[128,1664]{1,0:T(8,128)(2,1)S(1)} collective-permute-done((bf16[128,1664]{1,0:T(8,128)(2,1)S(1)}, bf16[128,1664]{1,0:T(8,128)(2,1)S(1)}, u32[]{:S(2)}, u32[]{:S(2)}) %collective-permute-start.20) | collective-permute-done | bytes 426016 | tf_op jit(solution)/shard_map/ppermute | solution.py:55
  157.9 28.2 %expert.2 = (bf16[1152,1536]{1,0:T(8,128)(2,1)}, f32[8,256]{1,0:T(8,128)}, bf16[1152,1664]{1,0:T(8,128)(2,1)}, bf16[768,1024]{1,0:T(8,128)(2,1)}, bf16[768,1024]{1,0:T(8,128)(2,1)}, /*index=5*/bf16[768,1024]{1,0:T(8,128)(2,1)}) custom-call(s32[2]{0:T(128)} %get-tuple-element.422.number_ref, bf16[256,1664]{1,0:T(8,128)(2,1)} %copy-done.4, ...), custom_call_target="tpu_custom_call" | custom-call | flops 622854144 | bytes 1024 | tf_op jit(solution)/shard_map/expert/pallas_call | solution.py:947
  186.2 2.9 collective-permute-start.24
  189.1 39.9 %expert.3 = (bf16[1152,1536]{1,0:T(8,128)(2,1)}, f32[8,256]{1,0:T(8,128)}, bf16[2048,1664]{1,0:T(8,128)(2,1)}, bf16[768,1024]{1,0:T(8,128)(2,1)}, bf16[768,1024]{1,0:T(8,128)(2,1)}, /*index=5*/bf16[768,1024]{1,0:T(8,128)(2,1)}) custom-call(s32[2]{0:T(128)} %get-tuple-element.421.number_ref, bf16[256,1664]{1,0:T(8,128)(2,1)} %copy-done.4, ...), custom_call_target="tpu_custom_call" | custom-call | flops 622854144 | bytes 1024 | tf_op jit(solution)/shard_map/expert/pallas_call | solution.py:947
  234.3 31.1 %collective-permute-done.26 = bf16[768,1024]{1,0:T(8,128)(2,1)} collective-permute-done((bf16[768,1024]{1,0:T(8,128)(2,1)}, bf16[768,1024]{1,0:T(8,128)(2,1)}, u32[]{:S(2)}, u32[]{:S(2)}) %collective-permute-start.26) | collective-permute-done | bytes 1572896 | tf_op jit(solution)/shard_map/ppermute | solution.py:181
  265.4 4.0 add_convert_fusion.9
  269.4 2.6 fusion.9
  272.1 2.5 collective-permute-start.28
  276.4 6.7 %combine.1 = bf16[2048,1536]{1,0:T(8,128)(2,1)} custom-call(s32[1]{0:T(128)} %bitcast.index_ref.number_ref, f32[8,256]{1,0:T(8,128)S(1)} %copy-done.23, f32[8,256]{1,0:T(8,128)S(1)} %copy-done.24, bf16[1152,1536]{1,0:T(8,128)(2,1)S(1)} %copy-done.5, bf16[1152,1536]{1,0:T(8,128)(2,1)S(1)} %copy-done.6), custom_call_target="tpu_custom_call" | custom-call | flops 70778880 | bytes 1024 | tf_op jit(solution)/shard_map/combine/pallas_call | solution.py:985
  283.1 10.3 %reduce-scatter.5.cloned.1.call-done.total_ref = bf16[256,1664]{1,0:T(8,128)(2,1)} async-done(((bf16[2048,1664]{1,0:T(8,128)(2,1)}), bf16[256,1664]{1,0:T(8,128)(2,1)}) %reduce-scatter.5.cloned.1.call-update) | async-done | bytes 851984 | tf_op jit(solution)/shard_map/reduce_scatter | solution.py:1103
  293.4 7.3 %router_back.1 = (f32[256,1536]{1,0:T(8,128)}, f32[256,1536]{1,0:T(8,128)}, bf16[256,1536]{1,0:T(8,128)(2,1)}, bf16[256,128]{1,0:T(8,128)(2,1)}, f32[8,1536]{1,0:T(8,128)}) custom-call(bf16[256,1664]{1,0:T(8,128)(2,1)} %reduce-scatter.5.cloned.1.call-done.total_ref, f32[256,128]{1,0:T(8,128)} %copy-done.20, bf16[1536,128]{1,0:T(8,128)(2,1)} %copy-done.8, ...), custom_call_target="tpu_custom_call" | custom-call | flops 132120576 | bytes 1024 | tf_op jit(solution)/shard_map/router_back/pallas_call | solution.py:428
  300.7 7.9 %collective-permute-done.28 = bf16[768,1024]{1,0:T(8,128)(2,1)} collective-permute-done((bf16[768,1024]{1,0:T(8,128)(2,1)S(1)}, bf16[768,1024]{1,0:T(8,128)(2,1)}, u32[]{:S(2)}, u32[]{:S(2)}) %collective-permute-start.28) | collective-permute-done | bytes 1572896 | tf_op jit(solution)/shard_map/ppermute | solution.py:171
  310.7 2.9 fusion.10
  316.4 30.0 %attend_back.1 = (bf16[256,1536]{1,0:T(8,128)(2,1)S(1)}, bf16[1024,512]{1,0:T(8,128)(2,1)S(1)}, bf16[1024,512]{1,0:T(8,128)(2,1)S(1)}, bf16[1536,2560]{1,0:T(8,128)(2,1)}) custom-call(s32[2]{0:T(128)S(1)} %copy-done.25, bf16[256,1536]{1,0:T(8,128)(2,1)} %copy-done.7, bf16[1024,1024]{1,0:T(8,128)(2,1)} %get-tuple-element.210.k_ref.v_ref, ...), custom_call_target="tpu_custom_call" | custom-call | flops 402653184 | bytes 1024 | tf_op jit(solution)/shard_map/attend_back/pallas_call | solution.py:722
  356.9 5.8 output_grad.1
  362.7 24.8 %collective-permute-done.32 = bf16[768,1024]{1,0:T(8,128)(2,1)} collective-permute-done((bf16[768,1024]{1,0:T(8,128)(2,1)}, bf16[768,1024]{1,0:T(8,128)(2,1)}, u32[]{:S(2)}, u32[]{:S(2)}) %collective-permute-start.32) | collective-permute-done | bytes 1572896 | tf_op jit(solution)/shard_map/ppermute | solution.py:171
  387.4 3.7 add_convert_fusion.3
  391.1 3.7 fusion.12
  395.7 4.3 collective-permute-start.35
  400.1 3.2 add_convert_fusion.1
  403.3 18.6 %reduce-scatter.9.cloned.1.call-done = bf16[192,2560]{1,0:T(8,128)(2,1)} async-done(((bf16[1536,2560]{1,0:T(8,128)(2,1)}), bf16[192,2560]{1,0:T(8,128)(2,1)}) %reduce-scatter.9.cloned.1.call-update) | async-done | bytes 983056 | tf_op jit(solution)/shard_map/reduce_scatter | solution.py:1116
  423.0 15.1 %collective-permute-start.33 = (bf16[192,1536]{1,0:T(8,128)(2,1)S(1)}, bf16[192,1536]{1,0:T(8,128)(2,1)S(1)}, u32[]{:S(2)}, u32[]{:S(2)}) collective-permute-start(bf16[192,1536]{1,0:T(8,128)(2,1)S(1)} %slice.104), channel_id=1, source_target_pairs={{0,1},{3,2},{4,5},{7,6},{8,9},{11,10},{12,13},{15,14},{16,17},{19,... | collective-permute-start | bytes 1769480 | tf_op jit(solution)/shard_map/ppermute | solution.py:189
  438.1 2.8 add_convert_fusion.2
  447.9 4.4 collective-permute-start.34
  455.2 2.9 collective-permute-done.34
  458.2 19.9 %collective-permute-done.38 = bf16[768,1024]{1,0:T(8,128)(2,1)S(1)} collective-permute-done((bf16[768,1024]{1,0:T(8,128)(2,1)S(1)}, bf16[768,1024]{1,0:T(8,128)(2,1)S(1)}, u32[]{:S(2)}, u32[]{:S(2)}) %collective-permute-start.38) | collective-permute-done | bytes 1572896 | tf_op jit(solution)/shard_map/ppermute | solution.py:181
  488.8 23.6 %collective-permute-done.42 = bf16[768,1024]{1,0:T(8,128)(2,1)} collective-permute-done((bf16[768,1024]{1,0:T(8,128)(2,1)}, bf16[768,1024]{1,0:T(8,128)(2,1)}, u32[]{:S(2)}, u32[]{:S(2)}) %collective-permute-start.42) | collective-permute-done | bytes 1572896 | tf_op jit(solution)/shard_map/ppermute | solution.py:181
  515.4 2.5 copy-done.43
  536.8 3.5 pad_maximum_fusion
  540.3 5.2 copy-done.27
  560.5 22.0 %collective-permute-done.49 = bf16[192,1664]{1,0:T(8,128)(2,1)S(1)} collective-permute-done((bf16[192,1664]{1,0:T(8,128)(2,1)S(1)}, bf16[192,1664]{1,0:T(8,128)(2,1)S(1)}, u32[]{:S(2)}, u32[]{:S(2)}) %collective-permute-start.49) | collective-permute-done | bytes 639008 | tf_op jit(solution)/shard_map/ppermute | solution.py:181
  (310 shorter events, 120.8 us)
Async XLA Ops:
  7.2 98.2 %all-gather.3.cloned.1.call-start = ((), (), s32[]{:S(2)}) async-start(), calls=%async_computation.4 | async-start | bytes 5308416 | tf_op jit(solution)/shard_map/all_gather | solution.py:1062
  7.9 150.0 %all-gather.5.cloned.1.call-start = ((), (), s32[]{:S(2)}) async-start(), calls=%async_computation.5 | async-start | bytes 7667712 | tf_op jit(solution)/shard_map/all_gather | solution.py:1064
  12.5 34.8 %collective-permute-start = (bf16[192,2688]{1,0:T(8,128)(2,1)S(1)}, bf16[192,2688]{1,0:T(8,128)(2,1)S(1)}, u32[]{:S(2)}, u32[]{:S(2)}) collective-permute-start(bf16[192,2688]{1,0:T(8,128)(2,1)S(1)} %concatenate.31.refs_0_), channel_id=1, source_target_pairs={{0,8},{4,12},{8,0},{12,4},{16,24},{20,28},{24,16},{28,20},{1,9},{5... | collective-permute-start | bytes 3096584 | tf_op jit(solution)/shard_map/ppermute | solution.py:55
  15.5 35.2 %collective-permute-start.1 = (bf16[192,2688]{1,0:T(8,128)(2,1)S(1)}, bf16[192,2688]{1,0:T(8,128)(2,1)}, u32[]{:S(2)}, u32[]{:S(2)}) collective-permute-start(bf16[192,2688]{1,0:T(8,128)(2,1)S(1)} %concatenate.31.refs_0_), channel_id=1, source_target_pairs={{0,16},{4,20},{8,24},{12,28},{16,0},{20,4},{24,8},{28,12},{1,17},{... | collective-permute-start | bytes 3096584 | tf_op jit(solution)/shard_map/ppermute | solution.py:55
  18.3 13.0 %collective-permute-start.2 = (bf16[128,1536]{1,0:T(8,128)(2,1)S(1)}, bf16[128,1536]{1,0:T(8,128)(2,1)}, u32[]{:S(2)}, u32[]{:S(2)}) collective-permute-start(bf16[128,1536]{1,0:T(8,128)(2,1)S(1)} %get-tuple-element.415.refs_10_), channel_id=1, source_target_pairs={{0,1},{1,2},{2,3},{4,5},{5,6},{6,7},{8,9},{9,10},{10,11},{12,13},{... | collective-permute-start | bytes 1179656 | tf_op jit(solution)/shard_map/ppermute | solution.py:114
  22.5 17.2 %collective-permute-start.3 = (bf16[128,1536]{1,0:T(8,128)(2,1)S(1)}, bf16[128,1536]{1,0:T(8,128)(2,1)}, u32[]{:S(2)}, u32[]{:S(2)}) collective-permute-start(bf16[128,1536]{1,0:T(8,128)(2,1)S(1)} %get-tuple-element.414.refs_11_), channel_id=1, source_target_pairs={{0,1},{1,2},{2,3},{4,5},{5,6},{6,7},{8,9},{9,10},{10,11},{12,13},{... | collective-permute-start | bytes 1179656 | tf_op jit(solution)/shard_map/ppermute | solution.py:114
  31.3 15.2 %collective-permute-start.4 = (bf16[128,1536]{1,0:T(8,128)(2,1)}, bf16[128,1536]{1,0:T(8,128)(2,1)}, u32[]{:S(2)}, u32[]{:S(2)}) collective-permute-start(bf16[128,1536]{1,0:T(8,128)(2,1)} %collective-permute-done.2.refs_12_), channel_id=1, source_target_pairs={{0,1},{1,2},{2,3},{4,5},{5,6},{6,7},{8,9},{9,10},{10,11},{12,13},{... | collective-permute-start | bytes 1179656 | tf_op jit(solution)/shard_map/ppermute | solution.py:114
  50.7 242.7 %reduce-scatter.5.cloned.1.call-start = ((), (), s32[]{:S(2)}) async-start(), calls=%async_computation.6 | async-start | bytes 7667712 | tf_op jit(solution)/shard_map/reduce_scatter | solution.py:1103
  50.8 20.1 %collective-permute-start.5 = (bf16[96,2688]{1,0:T(8,128)(2,1)S(1)}, bf16[96,2688]{1,0:T(8,128)(2,1)S(1)}, u32[]{:S(2)}, u32[]{:S(2)}) collective-permute-start(bf16[96,2688]{1,0:T(8,128)(2,1)S(1)} %slice.82), channel_id=1, source_target_pairs={{0,16},{4,20},{8,24},{12,28},{16,0},{20,4},{24,8},{28,12},{1,17},{... | collective-permute-start | bytes 1548296 | tf_op jit(solution)/shard_map/ppermute | solution.py:55
  54.6 16.4 %collective-permute-start.6 = (bf16[96,2688]{1,0:T(8,128)(2,1)S(1)}, bf16[96,2688]{1,0:T(8,128)(2,1)}, u32[]{:S(2)}, u32[]{:S(2)}) collective-permute-start(bf16[96,2688]{1,0:T(8,128)(2,1)S(1)} %slice.83), channel_id=1, source_target_pairs={{0,8},{4,12},{8,0},{12,4},{16,24},{20,28},{24,16},{28,20},{1,9},{5... | collective-permute-start | bytes 1548296 | tf_op jit(solution)/shard_map/ppermute | solution.py:55
  54.6 11.3 %collective-permute-start.7 = (bf16[128,1536]{1,0:T(8,128)(2,1)}, bf16[128,1536]{1,0:T(8,128)(2,1)}, u32[]{:S(2)}, u32[]{:S(2)}) collective-permute-start(bf16[128,1536]{1,0:T(8,128)(2,1)} %collective-permute-done.3.refs_13_), channel_id=1, source_target_pairs={{0,1},{1,2},{2,3},{4,5},{5,6},{6,7},{8,9},{9,10},{10,11},{12,13},{... | collective-permute-start | bytes 1179656 | tf_op jit(solution)/shard_map/ppermute | solution.py:114
  58.7 11.4 %collective-permute-start.8 = (bf16[128,1536]{1,0:T(8,128)(2,1)}, bf16[128,1536]{1,0:T(8,128)(2,1)S(1)}, u32[]{:S(2)}, u32[]{:S(2)}) collective-permute-start(bf16[128,1536]{1,0:T(8,128)(2,1)} %collective-permute-done.4.refs_14_), channel_id=1, source_target_pairs={{0,1},{1,2},{2,3},{4,5},{5,6},{6,7},{8,9},{9,10},{10,11},{12,13},{... | collective-permute-start | bytes 1179656 | tf_op jit(solution)/shard_map/ppermute | solution.py:114
  70.9 12.6 %collective-permute-start.10 = (bf16[192,2688]{1,0:T(8,128)(2,1)S(1)}, bf16[192,2688]{1,0:T(8,128)(2,1)}, u32[]{:S(2)}, u32[]{:S(2)}) collective-permute-start(bf16[192,2688]{1,0:T(8,128)(2,1)S(1)} %collective-permute-done.refs_2_), channel_id=1, source_target_pairs={{0,4},{4,0},{8,12},{12,8},{16,20},{20,16},{24,28},{28,24},{1,5},{5... | collective-permute-start | bytes 3096584 | tf_op jit(solution)/shard_map/ppermute | solution.py:55
  70.9 12.6 %collective-permute-start.11 = (bf16[192,2688]{1,0:T(8,128)(2,1)}, bf16[192,2688]{1,0:T(8,128)(2,1)}, u32[]{:S(2)}, u32[]{:S(2)}) collective-permute-start(bf16[192,2688]{1,0:T(8,128)(2,1)} %collective-permute-done.1.refs_4_), channel_id=1, source_target_pairs={{0,4},{4,0},{8,12},{12,8},{16,20},{20,16},{24,28},{28,24},{1,5},{5... | collective-permute-start | bytes 3096584 | tf_op jit(solution)/shard_map/ppermute | solution.py:55
  71.4 12.1 %collective-permute-start.9 = (bf16[192,2688]{1,0:T(8,128)(2,1)S(1)}, bf16[192,2688]{1,0:T(8,128)(2,1)}, u32[]{:S(2)}, u32[]{:S(2)}) collective-permute-start(bf16[192,2688]{1,0:T(8,128)(2,1)S(1)} %concatenate.31.refs_0_), channel_id=1, source_target_pairs={{0,4},{4,0},{8,12},{12,8},{16,20},{20,16},{24,28},{28,24},{1,5},{5... | collective-permute-start | bytes 3096584 | tf_op jit(solution)/shard_map/ppermute | solution.py:55
  72.7 10.8 %collective-permute-start.13 = (bf16[96,2688]{1,0:T(8,128)(2,1)}, bf16[96,2688]{1,0:T(8,128)(2,1)}, u32[]{:S(2)}, u32[]{:S(2)}) collective-permute-start(bf16[96,2688]{1,0:T(8,128)(2,1)} %collective-permute-done.6.refs_7_), channel_id=1, source_target_pairs={{0,4},{4,0},{8,12},{12,8},{16,20},{20,16},{24,28},{28,24},{1,5},{5... | collective-permute-start | bytes 1548296 | tf_op jit(solution)/shard_map/ppermute | solution.py:55
  77.3 23.0 %collective-permute-start.14 = (bf16[128,1536]{1,0:T(8,128)(2,1)}, bf16[128,1536]{1,0:T(8,128)(2,1)}, u32[]{:S(2)}, u32[]{:S(2)}) collective-permute-start(bf16[128,1536]{1,0:T(8,128)(2,1)} %collective-permute-done.7.refs_15_), channel_id=1, source_target_pairs={{0,1},{1,2},{2,3},{4,5},{5,6},{6,7},{8,9},{9,10},{10,11},{12,13},{... | collective-permute-start | bytes 1179656 | tf_op jit(solution)/shard_map/ppermute | solution.py:114
  122.4 20.8 %collective-permute-start.15 = (bf16[256,1664]{1,0:T(8,128)(2,1)S(1)}, bf16[256,1664]{1,0:T(8,128)(2,1)S(1)}, u32[]{:S(2)}, u32[]{:S(2)}) collective-permute-start(bf16[256,1664]{1,0:T(8,128)(2,1)S(1)} %get-tuple-element.218.refs_0_.hn_ref), channel_id=1, source_target_pairs={{0,8},{4,12},{8,0},{12,4},{16,24},{20,28},{24,16},{28,20},{1,9},{5... | collective-permute-start | bytes 2555912 | tf_op jit(solution)/shard_map/ppermute | solution.py:55
  124.2 20.4 %collective-permute-start.16 = (bf16[256,1664]{1,0:T(8,128)(2,1)S(1)}, bf16[256,1664]{1,0:T(8,128)(2,1)S(1)}, u32[]{:S(2)}, u32[]{:S(2)}) collective-permute-start(bf16[256,1664]{1,0:T(8,128)(2,1)S(1)} %get-tuple-element.218.refs_0_.hn_ref), channel_id=1, source_target_pairs={{0,16},{4,20},{8,24},{12,28},{16,0},{20,4},{24,8},{28,12},{1,17},{... | collective-permute-start | bytes 2555912 | tf_op jit(solution)/shard_map/ppermute | solution.py:55
  144.7 10.4 %collective-permute-start.20 = (bf16[128,1664]{1,0:T(8,128)(2,1)S(1)}, bf16[128,1664]{1,0:T(8,128)(2,1)S(1)}, u32[]{:S(2)}, u32[]{:S(2)}) collective-permute-start(bf16[128,1664]{1,0:T(8,128)(2,1)S(1)} %slice.84), channel_id=1, source_target_pairs={{0,16},{4,20},{8,24},{12,28},{16,0},{20,4},{24,8},{28,12},{1,17},{... | collective-permute-start | bytes 1277960 | tf_op jit(solution)/shard_map/ppermute | solution.py:55
  145.1 10.3 %collective-permute-start.21 = (bf16[128,1664]{1,0:T(8,128)(2,1)S(1)}, bf16[128,1664]{1,0:T(8,128)(2,1)}, u32[]{:S(2)}, u32[]{:S(2)}) collective-permute-start(bf16[128,1664]{1,0:T(8,128)(2,1)S(1)} %slice.85), channel_id=1, source_target_pairs={{0,8},{4,12},{8,0},{12,4},{16,24},{20,28},{24,16},{28,20},{1,9},{5... | collective-permute-start | bytes 1277960 | tf_op jit(solution)/shard_map/ppermute | solution.py:55
  145.5 12.4 %collective-permute-start.17 = (bf16[256,1664]{1,0:T(8,128)(2,1)S(1)}, bf16[256,1664]{1,0:T(8,128)(2,1)}, u32[]{:S(2)}, u32[]{:S(2)}) collective-permute-start(bf16[256,1664]{1,0:T(8,128)(2,1)S(1)} %get-tuple-element.218.refs_0_.hn_ref), channel_id=1, source_target_pairs={{0,4},{4,0},{8,12},{12,8},{16,20},{20,16},{24,28},{28,24},{1,5},{5... | collective-permute-start | bytes 2555912 | tf_op jit(solution)/shard_map/ppermute | solution.py:55
  145.5 12.4 %collective-permute-start.18 = (bf16[256,1664]{1,0:T(8,128)(2,1)S(1)}, bf16[256,1664]{1,0:T(8,128)(2,1)}, u32[]{:S(2)}, u32[]{:S(2)}) collective-permute-start(bf16[256,1664]{1,0:T(8,128)(2,1)S(1)} %collective-permute-done.15.refs_2_), channel_id=1, source_target_pairs={{0,4},{4,0},{8,12},{12,8},{16,20},{20,16},{24,28},{28,24},{1,5},{5... | collective-permute-start | bytes 2555912 | tf_op jit(solution)/shard_map/ppermute | solution.py:55
  146.0 11.9 %collective-permute-start.19 = (bf16[256,1664]{1,0:T(8,128)(2,1)S(1)}, bf16[256,1664]{1,0:T(8,128)(2,1)}, u32[]{:S(2)}, u32[]{:S(2)}) collective-permute-start(bf16[256,1664]{1,0:T(8,128)(2,1)S(1)} %collective-permute-done.16.refs_4_), channel_id=1, source_target_pairs={{0,4},{4,0},{8,12},{12,8},{16,20},{20,16},{24,28},{28,24},{1,5},{5... | collective-permute-start | bytes 2555912 | tf_op jit(solution)/shard_map/ppermute | solution.py:55
  186.2 42.8 %collective-permute-start.24 = (bf16[768,1024]{1,0:T(8,128)(2,1)}, bf16[768,1024]{1,0:T(8,128)(2,1)S(1)}, u32[]{:S(2)}, u32[]{:S(2)}) collective-permute-start(bf16[768,1024]{1,0:T(8,128)(2,1)} %get-tuple-element.235), channel_id=1, source_target_pairs={{0,1},{3,2},{4,5},{7,6},{8,9},{11,10},{12,13},{15,14},{16,17},{19,... | collective-permute-start | bytes 4718600 | tf_op jit(solution)/shard_map/ppermute | solution.py:181
  229.8 192.1 %reduce-scatter.9.cloned.1.call-start = ((), (), s32[]{:S(2)}) async-start(), calls=%async_computation.8 | async-start | bytes 8847360 | tf_op jit(solution)/shard_map/reduce_scatter | solution.py:1116
  229.8 35.6 %collective-permute-start.26 = (bf16[768,1024]{1,0:T(8,128)(2,1)}, bf16[768,1024]{1,0:T(8,128)(2,1)}, u32[]{:S(2)}, u32[]{:S(2)}) collective-permute-start(bf16[768,1024]{1,0:T(8,128)(2,1)} %get-tuple-element.238), channel_id=1, source_target_pairs={{0,1},{3,2},{4,5},{7,6},{8,9},{11,10},{12,13},{15,14},{16,17},{19,... | collective-permute-start | bytes 4718600 | tf_op jit(solution)/shard_map/ppermute | solution.py:181
  232.3 37.1 %collective-permute-start.25 = (bf16[768,1024]{1,0:T(8,128)(2,1)S(1)}, bf16[768,1024]{1,0:T(8,128)(2,1)}, u32[]{:S(2)}, u32[]{:S(2)}) collective-permute-start(bf16[768,1024]{1,0:T(8,128)(2,1)S(1)} %add_convert_fusion.11), channel_id=1, source_target_pairs={{1,2},{2,1},{5,6},{6,5},{9,10},{10,9},{13,14},{14,13},{17,18},{18,... | collective-permute-start | bytes 4718600 | tf_op jit(solution)/shard_map/ppermute | solution.py:181
  272.1 36.5 %collective-permute-start.28 = (bf16[768,1024]{1,0:T(8,128)(2,1)S(1)}, bf16[768,1024]{1,0:T(8,128)(2,1)}, u32[]{:S(2)}, u32[]{:S(2)}) collective-permute-start(bf16[768,1024]{1,0:T(8,128)(2,1)S(1)} %fusion.9), channel_id=1, source_target_pairs={{0,1},{1,0},{2,3},{3,2},{4,5},{5,4},{6,7},{7,6},{8,9},{9,8},{10,11... | collective-permute-start | bytes 4718600 | tf_op jit(solution)/shard_map/ppermute | solution.py:171
  274.6 36.1 %collective-permute-start.27 = (bf16[768,1024]{1,0:T(8,128)(2,1)}, bf16[768,1024]{1,0:T(8,128)(2,1)}, u32[]{:S(2)}, u32[]{:S(2)}) collective-permute-start(bf16[768,1024]{1,0:T(8,128)(2,1)} %add_convert_fusion.9), channel_id=1, source_target_pairs={{1,2},{2,1},{5,6},{6,5},{9,10},{10,9},{13,14},{14,13},{17,18},{18,... | collective-permute-start | bytes 4718600 | tf_op jit(solution)/shard_map/ppermute | solution.py:181
  313.7 35.1 %collective-permute-start.30 = (bf16[768,1024]{1,0:T(8,128)(2,1)S(1)}, bf16[768,1024]{1,0:T(8,128)(2,1)S(1)}, u32[]{:S(2)}, u32[]{:S(2)}) collective-permute-start(bf16[768,1024]{1,0:T(8,128)(2,1)S(1)} %fusion.10), channel_id=1, source_target_pairs={{0,1},{1,0},{2,3},{3,2},{4,5},{5,4},{6,7},{7,6},{8,9},{9,8},{10,11... | collective-permute-start | bytes 4718600 | tf_op jit(solution)/shard_map/ppermute | solution.py:171
  315.5 35.1 %collective-permute-start.29 = (bf16[768,1024]{1,0:T(8,128)(2,1)S(1)}, bf16[768,1024]{1,0:T(8,128)(2,1)S(1)}, u32[]{:S(2)}, u32[]{:S(2)}) collective-permute-start(bf16[768,1024]{1,0:T(8,128)(2,1)S(1)} %add_convert_fusion.7), channel_id=1, source_target_pairs={{1,2},{2,1},{5,6},{6,5},{9,10},{10,9},{13,14},{14,13},{17,18},{18,... | collective-permute-start | bytes 4718600 | tf_op jit(solution)/shard_map/ppermute | solution.py:181
  352.9 135.9 %reduce-scatter.7.cloned.1.call-start = ((), (), s32[]{:S(2)}) async-start(), calls=%async_computation.7 | async-start | bytes 5750784 | tf_op jit(solution)/shard_map/reduce_scatter | solution.py:1119
  352.9 34.5 %collective-permute-start.32 = (bf16[768,1024]{1,0:T(8,128)(2,1)}, bf16[768,1024]{1,0:T(8,128)(2,1)}, u32[]{:S(2)}, u32[]{:S(2)}) collective-permute-start(bf16[768,1024]{1,0:T(8,128)(2,1)} %fusion.11), channel_id=1, source_target_pairs={{0,1},{1,0},{2,3},{3,2},{4,5},{5,4},{6,7},{7,6},{8,9},{9,8},{10,11... | collective-permute-start | bytes 4718600 | tf_op jit(solution)/shard_map/ppermute | solution.py:171
  354.8 36.3 %collective-permute-start.31 = (bf16[768,1024]{1,0:T(8,128)(2,1)}, bf16[768,1024]{1,0:T(8,128)(2,1)}, u32[]{:S(2)}, u32[]{:S(2)}) collective-permute-start(bf16[768,1024]{1,0:T(8,128)(2,1)} %add_convert_fusion.5), channel_id=1, source_target_pairs={{1,2},{2,1},{5,6},{6,5},{9,10},{10,9},{13,14},{14,13},{17,18},{18,... | collective-permute-start | bytes 4718600 | tf_op jit(solution)/shard_map/ppermute | solution.py:181
  394.9 162.1 %reduce-scatter.11.cloned.1.call-start = ((), (), s32[]{:S(2)}) async-start(), calls=%async_computation.9 | async-start | bytes 7077888 | tf_op jit(solution)/shard_map/reduce_scatter | solution.py:1155
  395.7 42.4 %collective-permute-start.35 = (bf16[768,1024]{1,0:T(8,128)(2,1)}, bf16[768,1024]{1,0:T(8,128)(2,1)}, u32[]{:S(2)}, u32[]{:S(2)}) collective-permute-start(bf16[768,1024]{1,0:T(8,128)(2,1)} %fusion.12), channel_id=1, source_target_pairs={{0,1},{1,0},{2,3},{3,2},{4,5},{5,4},{6,7},{7,6},{8,9},{9,8},{10,11... | collective-permute-start | bytes 4718600 | tf_op jit(solution)/shard_map/ppermute | solution.py:171
  423.0 23.6 %collective-permute-start.33 = (bf16[192,1536]{1,0:T(8,128)(2,1)S(1)}, bf16[192,1536]{1,0:T(8,128)(2,1)S(1)}, u32[]{:S(2)}, u32[]{:S(2)}) collective-permute-start(bf16[192,1536]{1,0:T(8,128)(2,1)S(1)} %slice.104), channel_id=1, source_target_pairs={{0,1},{3,2},{4,5},{7,6},{8,9},{11,10},{12,13},{15,14},{16,17},{19,... | collective-permute-start | bytes 1769480 | tf_op jit(solution)/shard_map/ppermute | solution.py:189
  441.0 12.3 %collective-permute-start.37 = (bf16[768,1024]{1,0:T(8,128)(2,1)S(1)}, bf16[768,1024]{1,0:T(8,128)(2,1)S(1)}, u32[]{:S(2)}, u32[]{:S(2)}) collective-permute-start(bf16[768,1024]{1,0:T(8,128)(2,1)S(1)} %add_convert_fusion.2), channel_id=1, source_target_pairs={{1,2},{2,1},{5,6},{6,5},{9,10},{10,9},{13,14},{14,13},{17,18},{18,... | collective-permute-start | bytes 4718600 | tf_op jit(solution)/shard_map/ppermute | solution.py:181
  442.1 10.2 %collective-permute-start.39 = (bf16[256,1024]{1,0:T(8,128)(2,1)S(1)}, bf16[256,1024]{1,0:T(8,128)(2,1)S(1)}, u32[]{:S(2)}, u32[]{:S(2)}) collective-permute-start(bf16[256,1024]{1,0:T(8,128)(2,1)S(1)} %slice.106), channel_id=1, source_target_pairs={{3,2},{7,6},{11,10},{15,14},{19,18},{23,22},{27,26},{31,30}} | collective-permute-start | bytes 1572872 | tf_op jit(solution)/shard_map/ppermute | solution.py:1152
  444.0 34.0 %collective-permute-start.38 = (bf16[768,1024]{1,0:T(8,128)(2,1)S(1)}, bf16[768,1024]{1,0:T(8,128)(2,1)S(1)}, u32[]{:S(2)}, u32[]{:S(2)}) collective-permute-start(bf16[768,1024]{1,0:T(8,128)(2,1)S(1)} %copy-done.40), channel_id=1, source_target_pairs={{1,0},{2,3},{5,4},{6,7},{9,8},{10,11},{13,12},{14,15},{17,16},{18,... | collective-permute-start | bytes 4718600 | tf_op jit(solution)/shard_map/ppermute | solution.py:181
  447.9 10.2 %collective-permute-start.34 = (bf16[192,1152]{1,0:T(8,128)(2,1)S(1)}, bf16[192,1152]{1,0:T(8,128)(2,1)S(1)}, u32[]{:S(2)}, u32[]{:S(2)}) collective-permute-start(bf16[192,1152]{1,0:T(8,128)(2,1)S(1)} %pad_maximum_fusion.4), channel_id=1, source_target_pairs={{0,1},{3,2},{4,5},{7,6},{8,9},{11,10},{12,13},{15,14},{16,17},{19,... | collective-permute-start | bytes 1327112 | tf_op jit(solution)/shard_map/ppermute | solution.py:189
  479.0 33.4 %collective-permute-start.42 = (bf16[768,1024]{1,0:T(8,128)(2,1)}, bf16[768,1024]{1,0:T(8,128)(2,1)}, u32[]{:S(2)}, u32[]{:S(2)}) collective-permute-start(bf16[768,1024]{1,0:T(8,128)(2,1)} %add_convert_fusion), channel_id=1, source_target_pairs={{1,0},{2,3},{5,4},{6,7},{9,8},{10,11},{13,12},{14,15},{17,16},{18,... | collective-permute-start | bytes 4718600 | tf_op jit(solution)/shard_map/ppermute | solution.py:181
  512.4 33.2 %collective-permute-start.48 = (bf16[256,1024]{1,0:T(8,128)(2,1)}, bf16[256,1024]{1,0:T(8,128)(2,1)}, u32[]{:S(2)}, u32[]{:S(2)}) collective-permute-start(bf16[256,1024]{1,0:T(8,128)(2,1)} %add_convert_fusion.16), channel_id=1, source_target_pairs={{1,0},{2,1},{3,2},{5,4},{6,5},{7,6},{9,8},{10,9},{11,10},{13,12},{... | collective-permute-start | bytes 1572872 | tf_op jit(solution)/shard_map/ppermute | solution.py:1152
  521.1 29.7 %collective-permute-start.44 = (bf16[192,1664]{1,0:T(8,128)(2,1)S(1)}, bf16[192,1664]{1,0:T(8,128)(2,1)S(1)}, u32[]{:S(2)}, u32[]{:S(2)}) collective-permute-start(bf16[192,1664]{1,0:T(8,128)(2,1)S(1)} %copy-done.64), channel_id=1, source_target_pairs={{0,1},{3,2},{4,5},{7,6},{8,9},{11,10},{12,13},{15,14},{16,17},{19,... | collective-permute-start | bytes 1916936 | tf_op jit(solution)/shard_map/ppermute | solution.py:181
  523.0 28.0 %collective-permute-start.46 = (bf16[192,1536]{1,0:T(8,128)(2,1)S(1)}, bf16[192,1536]{1,0:T(8,128)(2,1)}, u32[]{:S(2)}, u32[]{:S(2)}) collective-permute-start(bf16[192,1536]{1,0:T(8,128)(2,1)S(1)} %copy-done.54), channel_id=1, source_target_pairs={{1,0},{2,3},{5,4},{6,7},{9,8},{10,11},{13,12},{14,15},{17,16},{18,... | collective-permute-start | bytes 1769480 | tf_op jit(solution)/shard_map/ppermute | solution.py:181
  524.3 26.7 %collective-permute-start.45 = (bf16[192,1152]{1,0:T(8,128)(2,1)S(1)}, bf16[192,1152]{1,0:T(8,128)(2,1)}, u32[]{:S(2)}, u32[]{:S(2)}) collective-permute-start(bf16[192,1152]{1,0:T(8,128)(2,1)S(1)} %copy-done.56), channel_id=1, source_target_pairs={{1,0},{2,3},{5,4},{6,7},{9,8},{10,11},{13,12},{14,15},{17,16},{18,... | collective-permute-start | bytes 1327112 | tf_op jit(solution)/shard_map/ppermute | solution.py:181
  559.2 23.3 %collective-permute-start.49 = (bf16[192,1664]{1,0:T(8,128)(2,1)S(1)}, bf16[192,1664]{1,0:T(8,128)(2,1)S(1)}, u32[]{:S(2)}, u32[]{:S(2)}) collective-permute-start(bf16[192,1664]{1,0:T(8,128)(2,1)S(1)} %add_convert_fusion.12), channel_id=1, source_target_pairs={{1,0},{2,3},{5,4},{6,7},{9,8},{10,11},{13,12},{14,15},{17,16},{18,... | collective-permute-start | bytes 1916936 | tf_op jit(solution)/shard_map/ppermute | solution.py:181
  (81 other events, 950.0 us)
Sparse Core Ops, SparseCore 0:
  9.9 57.9 all-gather.2
  70.3 48.3 all-gather.4
  229.9 63.4 reduce-scatter.4
  353.0 68.8 reduce-scatter.8
  425.9 55.7 reduce-scatter.6
  484.9 65.6 reduce-scatter.10
